TPU v7x, 32 devices: a whole 2x2x4 slice. The times are simulated.
32 devices in a mesh: blk: 8 (over z, x), rep: 4 (over y, core).
Axes of the slice: x: 2, y: 2, z: 4, core: 2. Of those that a mesh axis runs over, the one named last changes fastest.
Arguments:
- features: bfloat16 [8192, 128], P('blk'), may hold values from -6 to 6
- weight: bfloat16 [128, 128], replicated, may hold values from -0.5 to 0.5
- bias: float32 [128], replicated, may hold values from -3 to 3
- tiles: bfloat16 [8, 4, 8, 4, 128, 128], P('blk', 'rep'), may hold values from -0.1875 to 0.1875
- tile_row: int32 [8, 4, 8, 4], P('blk', 'rep'), may hold values from 0 to 7
- tile_col: int32 [8, 4, 8, 4], P('blk', 'rep'), may hold values from 0 to 7
- tile_live: int32 [8, 4, 8], P('blk', 'rep'), may hold values from 1 to 4, as said below
- label_mask: int32 [8192], P(('blk', 'rep')), may hold values 0 or 1
- cotangent: bfloat16 [8192, 128], P(('blk', 'rep')), may hold values from -6 to 6
Outputs:
- output: bfloat16 [8192, 128], P(('blk', 'rep'))
- grad_weight: float32 [128, 128], replicated
- grad_bias: float32 [128], replicated
Inputs may be any that keep to these rules, and one draw needn't show every extreme that they name: `tile_live`: some entry equals 4 and some equals 1.
All inputs are finite; a program needn't handle non-finite values. No bound on the sum of `label_mask` on one device may be relied on, other than what follows from the above.
Results may differ from a plain program's by a relative error of at most 0.0056.
Values may be sent and summed in bfloat16 or wider, within the bound.
No kernel may reach another device: no remote copies, remote signals or barrier semaphores. Data moves between devices by JAX's collectives and lax.ppermute only.
A program may use at most 64 MiB of HBM per device.

v0:
```python
import jax
import jax.numpy as jnp
from jax import lax
from jax.sharding import PartitionSpec as P


def passed_along(array, axis, by):
    length = lax.axis_size(axis)
    return lax.ppermute(array, axis, [(i, (i + by) % length) for i in range(length)])


def shard_term(block_feat, values, rows_idx, cols_idx, count):
    tile = values.shape[-1]
    slots = values.shape[0]
    blocks = block_feat.shape[0] // tile
    stacked = block_feat.reshape(blocks, tile, block_feat.shape[1])
    picked = jnp.take(stacked, cols_idx, axis=0)
    prod = jnp.einsum("kij,kjf->kif", values, picked, preferred_element_type=jnp.float32)
    alive = jnp.arange(slots, dtype=jnp.int32) < count
    chosen = (rows_idx[None, :] == jnp.arange(blocks, dtype=jnp.int32)[:, None]) & alive[None, :]
    onehot = jnp.where(chosen, 1.0, 0.0).astype(jnp.float32)
    summed = jnp.einsum("rk,kif->rif", onehot, prod, precision=lax.Precision.HIGHEST)
    return summed.reshape(blocks * tile, block_feat.shape[1])


def shards(features, weight, bias, tiles, tile_row, tile_col, tile_live, label_mask, cotangent):
    local_tiles = tiles[0, 0]
    local_rows = tile_row[0, 0]
    local_cols = tile_col[0, 0]
    local_live = tile_live[0, 0]
    nblk = lax.axis_size("blk")
    me_blk = lax.axis_index("blk")

    def term(block, shard):
        return shard_term(
            block,
            lax.dynamic_index_in_dim(local_tiles, shard, 0, False),
            lax.dynamic_index_in_dim(local_rows, shard, 0, False),
            lax.dynamic_index_in_dim(local_cols, shard, 0, False),
            lax.dynamic_index_in_dim(local_live, shard, 0, False),
        )

    partial_sum = term(features, me_blk)

    def advance(step, carry):
        block, total = carry
        block = passed_along(block, "blk", 1)
        return (block, total + term(block, (me_blk - step) % nblk))

    moved, partial_sum = lax.fori_loop(1, nblk, advance, (features, partial_sum))
    aggregated = lax.psum_scatter(partial_sum, "rep", scatter_dimension=0, tiled=True)
    agg_rounded = aggregated.astype(jnp.bfloat16)
    pre = jnp.dot(agg_rounded, weight, preferred_element_type=jnp.float32) + bias[None, :]
    sigma = jax.nn.sigmoid(pre)
    output = (pre * sigma).astype(jnp.bfloat16)
    slope = sigma * (1.0 + pre * (1.0 - sigma))
    delta = cotangent.astype(jnp.float32) * label_mask.astype(jnp.float32)[:, None] * slope
    delta_rounded = delta.astype(jnp.bfloat16)
    local_gw = lax.dot_general(
        agg_rounded, delta_rounded, (((0,), (0,)), ((), ())), preferred_element_type=jnp.float32
    )
    local_gb = jnp.sum(delta, axis=0)
    grad_weight, grad_bias = lax.psum((local_gw, local_gb), ("blk", "rep"))
    return (output, grad_weight, grad_bias)


def solution(mesh):
    placed = (
        P("blk", None),
        P(),
        P(),
        P("blk", "rep", None, None, None, None),
        P("blk", "rep", None, None),
        P("blk", "rep", None, None),
        P("blk", "rep", None),
        P(("blk", "rep")),
        P(("blk", "rep"), None),
    )
    return jax.shard_map(
        shards,
        mesh=mesh,
        in_specs=placed,
        out_specs=(P(("blk", "rep"), None), P(), P()),
        check_vma=False,
    )
```

profile of v0, /device:TPU:0, one launch (start us, length us, event | category | flops | bytes accessed | tf_op | source)
XLA Modules:
  0.0 254.4 jit_solution(2856160983162691468)
XLA Ops:
  7.2 1.0 copy.39
  8.2 0.7 copy-done.4
  9.1 0.6 copy-done.7
  10.4 0.6 iota_compare_fusion.3
  11.6 1.2 fusion.24
  12.7 0.8 fusion.22
  13.9 88.1 %while.17 = (s32[]{:T(128)}, bf16[1024,128]{1,0:T(8,128)(2,1)S(1)}, f32[1024,128]{1,0:T(8,128)S(1)}, s32[]{:T(128)}, s32[8,4]{1,0:T(8,128)S(1)}, /*index=5*/s32[...) while((s32[]{:T(128)}, bf16[1024,128]{1,0:T(8,128)(2,1)S(1)}, ...), condition=%wide.region_1.3_spmd, body=%wide.region_0.2_spmd.sunk | while | flops 23266444 | bytes 5771732 | solution.py:50
  13.9 2.9 %collective-permute-start = (bf16[1024,128]{1,0:T(8,128)(2,1)S(1)}, bf16[1024,128]{1,0:T(8,128)(2,1)S(1)}, u32[]{:S(2)}, u32[]{:S(2)}) collective-permute-start(bf16[1024,128]{1,0:T(8,128)(2,1)S(1)} %get-tuple-element.312), channel_id=1, source_target_pairs={{0,4},{4,8},{8,12},{12,16},{16,20},{20,24},{24,28},{28,0},{1,5},{5... | collective-permute-start | bytes 786440 | tf_op jit(solution)/shard_map/while/body/eval_jaxpr/ppermute | solution.py:9
  17.4 0.6 iota_compare_fusion.5
  18.1 8.0 %collective-permute-done = bf16[1024,128]{1,0:T(8,128)(2,1)S(1)} collective-permute-done((bf16[1024,128]{1,0:T(8,128)(2,1)S(1)}, bf16[1024,128]{1,0:T(8,128)(2,1)S(1)}, u32[]{:S(2)}, u32[]{:S(2)}) %collective-permute-start) | collective-permute-done | bytes 262176 | tf_op jit(solution)/shard_map/while/body/eval_jaxpr/ppermute | solution.py:9
  26.7 1.2 fusion.60
  27.9 0.8 fusion.62
  29.0 0.6 dynamic_slice.84
  29.6 0.6 iota_compare_fusion.5
  30.3 8.9 %collective-permute-done = bf16[1024,128]{1,0:T(8,128)(2,1)S(1)} collective-permute-done((bf16[1024,128]{1,0:T(8,128)(2,1)S(1)}, bf16[1024,128]{1,0:T(8,128)(2,1)S(1)}, u32[]{:S(2)}, u32[]{:S(2)}) %collective-permute-start) | collective-permute-done | bytes 262176 | tf_op jit(solution)/shard_map/while/body/eval_jaxpr/ppermute | solution.py:9
  39.8 1.2 fusion.60
  40.9 0.8 fusion.62
  42.1 0.6 dynamic_slice.84
  42.7 0.6 iota_compare_fusion.5
  43.4 7.9 %collective-permute-done = bf16[1024,128]{1,0:T(8,128)(2,1)S(1)} collective-permute-done((bf16[1024,128]{1,0:T(8,128)(2,1)S(1)}, bf16[1024,128]{1,0:T(8,128)(2,1)S(1)}, u32[]{:S(2)}, u32[]{:S(2)}) %collective-permute-start) | collective-permute-done | bytes 262176 | tf_op jit(solution)/shard_map/while/body/eval_jaxpr/ppermute | solution.py:9
  51.9 1.2 fusion.60
  53.1 0.8 fusion.62
  54.2 0.6 dynamic_slice.84
  54.8 0.6 iota_compare_fusion.5
  55.5 7.7 %collective-permute-done = bf16[1024,128]{1,0:T(8,128)(2,1)S(1)} collective-permute-done((bf16[1024,128]{1,0:T(8,128)(2,1)S(1)}, bf16[1024,128]{1,0:T(8,128)(2,1)S(1)}, u32[]{:S(2)}, u32[]{:S(2)}) %collective-permute-start) | collective-permute-done | bytes 262176 | tf_op jit(solution)/shard_map/while/body/eval_jaxpr/ppermute | solution.py:9
  63.9 1.2 fusion.60
  65.0 0.8 fusion.62
  66.2 0.6 dynamic_slice.84
  66.8 0.6 iota_compare_fusion.5
  67.5 7.7 %collective-permute-done = bf16[1024,128]{1,0:T(8,128)(2,1)S(1)} collective-permute-done((bf16[1024,128]{1,0:T(8,128)(2,1)S(1)}, bf16[1024,128]{1,0:T(8,128)(2,1)S(1)}, u32[]{:S(2)}, u32[]{:S(2)}) %collective-permute-start) | collective-permute-done | bytes 262176 | tf_op jit(solution)/shard_map/while/body/eval_jaxpr/ppermute | solution.py:9
  75.8 1.2 fusion.60
  77.0 0.8 fusion.62
  78.1 0.6 dynamic_slice.84
  78.7 0.6 iota_compare_fusion.5
  79.4 7.7 %collective-permute-done = bf16[1024,128]{1,0:T(8,128)(2,1)S(1)} collective-permute-done((bf16[1024,128]{1,0:T(8,128)(2,1)S(1)}, bf16[1024,128]{1,0:T(8,128)(2,1)S(1)}, u32[]{:S(2)}, u32[]{:S(2)}) %collective-permute-start) | collective-permute-done | bytes 262176 | tf_op jit(solution)/shard_map/while/body/eval_jaxpr/ppermute | solution.py:9
  87.7 1.2 fusion.60
  88.9 0.8 fusion.62
  90.7 0.6 iota_compare_fusion.5
  91.4 7.7 %collective-permute-done = bf16[1024,128]{1,0:T(8,128)(2,1)S(1)} collective-permute-done((bf16[1024,128]{1,0:T(8,128)(2,1)S(1)}, bf16[1024,128]{1,0:T(8,128)(2,1)S(1)}, u32[]{:S(2)}, u32[]{:S(2)}) %collective-permute-start) | collective-permute-done | bytes 262176 | tf_op jit(solution)/shard_map/while/body/eval_jaxpr/ppermute | solution.py:9
  99.7 1.2 fusion.60
  100.8 0.8 fusion.62
  102.0 0.8 copy-done.1
  102.8 18.6 %reduce-scatter.2.cloned.1.call-done = f32[256,128]{1,0:T(8,128)} async-done(((f32[1024,128]{1,0:T(8,128)}), f32[256,128]{1,0:T(8,128)}) %reduce-scatter.2.cloned.1.call-update) | async-done | bytes 131088 | tf_op jit(solution)/shard_map/reduce_scatter | solution.py:51
  121.4 1.8 fusion.46
  123.3 0.8 fusion.30
  124.1 39.4 %psum.15 = f32[128]{0:T(128)} all-reduce(f32[128]{0:T(128)S(1)} %get-tuple-element.238), channel_id=1, replica_groups=mesh['blk'=8,'rep'=4] {'blk','rep'}, use_global_device_ids=true, to_apply=%region_5.7 | all-reduce | flops 128 | bytes 1024 | tf_op jit(solution)/shard_map/psum | solution.py:63
  163.5 82.6 %all-reduce.2.cloned.1.call-done = f32[128,128]{1,0:T(8,128)} async-done(((f32[128,128]{1,0:T(8,128)}), f32[128,128]{1,0:T(8,128)}) %all-reduce.2.cloned.1.call-update) | async-done | bytes 65552 | tf_op jit(solution)/shard_map/psum | solution.py:63
  246.1 1.5 copy.40
  (86 shorter events, 8.9 us)
Async XLA Ops:
  7.2 114.3 %copy-start = (bf16[128,128]{1,0:T(8,128)(2,1)S(1)}, bf16[128,128]{1,0:T(8,128)(2,1)}, u32[]{:S(2)}) copy-start(bf16[128,128]{1,0:T(8,128)(2,1)} %param.14) | copy-start | bytes 98308
  7.2 114.2 %reduce-scatter.2.cloned.1.call-start = ((), (), s32[]{:S(2)}) async-start(), calls=%async_computation.1 | async-start | bytes 655360 | tf_op jit(solution)/shard_map/reduce_scatter | solution.py:51
  8.2 0.7 copy-start.4
  8.2 0.7 copy-start.3
  9.1 0.7 copy-start.7
  13.9 12.3 %collective-permute-start = (bf16[1024,128]{1,0:T(8,128)(2,1)S(1)}, bf16[1024,128]{1,0:T(8,128)(2,1)S(1)}, u32[]{:S(2)}, u32[]{:S(2)}) collective-permute-start(bf16[1024,128]{1,0:T(8,128)(2,1)S(1)} %get-tuple-element.312), channel_id=1, source_target_pairs={{0,4},{4,8},{8,12},{12,16},{16,20},{20,24},{24,28},{28,0},{1,5},{5... | collective-permute-start | bytes 786440 | tf_op jit(solution)/shard_map/while/body/eval_jaxpr/ppermute | solution.py:9
  29.0 10.2 %collective-permute-start = (bf16[1024,128]{1,0:T(8,128)(2,1)S(1)}, bf16[1024,128]{1,0:T(8,128)(2,1)S(1)}, u32[]{:S(2)}, u32[]{:S(2)}) collective-permute-start(bf16[1024,128]{1,0:T(8,128)(2,1)S(1)} %get-tuple-element.312), channel_id=1, source_target_pairs={{0,4},{4,8},{8,12},{12,16},{16,20},{20,24},{24,28},{28,0},{1,5},{5... | collective-permute-start | bytes 786440 | tf_op jit(solution)/shard_map/while/body/eval_jaxpr/ppermute | solution.py:9
  42.0 9.3 %collective-permute-start = (bf16[1024,128]{1,0:T(8,128)(2,1)S(1)}, bf16[1024,128]{1,0:T(8,128)(2,1)S(1)}, u32[]{:S(2)}, u32[]{:S(2)}) collective-permute-start(bf16[1024,128]{1,0:T(8,128)(2,1)S(1)} %get-tuple-element.312), channel_id=1, source_target_pairs={{0,4},{4,8},{8,12},{12,16},{16,20},{20,24},{24,28},{28,0},{1,5},{5... | collective-permute-start | bytes 786440 | tf_op jit(solution)/shard_map/while/body/eval_jaxpr/ppermute | solution.py:9
  54.2 9.1 %collective-permute-start = (bf16[1024,128]{1,0:T(8,128)(2,1)S(1)}, bf16[1024,128]{1,0:T(8,128)(2,1)S(1)}, u32[]{:S(2)}, u32[]{:S(2)}) collective-permute-start(bf16[1024,128]{1,0:T(8,128)(2,1)S(1)} %get-tuple-element.312), channel_id=1, source_target_pairs={{0,4},{4,8},{8,12},{12,16},{16,20},{20,24},{24,28},{28,0},{1,5},{5... | collective-permute-start | bytes 786440 | tf_op jit(solution)/shard_map/while/body/eval_jaxpr/ppermute | solution.py:9
  66.1 9.1 %collective-permute-start = (bf16[1024,128]{1,0:T(8,128)(2,1)S(1)}, bf16[1024,128]{1,0:T(8,128)(2,1)S(1)}, u32[]{:S(2)}, u32[]{:S(2)}) collective-permute-start(bf16[1024,128]{1,0:T(8,128)(2,1)S(1)} %get-tuple-element.312), channel_id=1, source_target_pairs={{0,4},{4,8},{8,12},{12,16},{16,20},{20,24},{24,28},{28,0},{1,5},{5... | collective-permute-start | bytes 786440 | tf_op jit(solution)/shard_map/while/body/eval_jaxpr/ppermute | solution.py:9
  78.0 9.1 %collective-permute-start = (bf16[1024,128]{1,0:T(8,128)(2,1)S(1)}, bf16[1024,128]{1,0:T(8,128)(2,1)S(1)}, u32[]{:S(2)}, u32[]{:S(2)}) collective-permute-start(bf16[1024,128]{1,0:T(8,128)(2,1)S(1)} %get-tuple-element.312), channel_id=1, source_target_pairs={{0,4},{4,8},{8,12},{12,16},{16,20},{20,24},{24,28},{28,0},{1,5},{5... | collective-permute-start | bytes 786440 | tf_op jit(solution)/shard_map/while/body/eval_jaxpr/ppermute | solution.py:9
  90.0 9.1 %collective-permute-start = (bf16[1024,128]{1,0:T(8,128)(2,1)S(1)}, bf16[1024,128]{1,0:T(8,128)(2,1)S(1)}, u32[]{:S(2)}, u32[]{:S(2)}) collective-permute-start(bf16[1024,128]{1,0:T(8,128)(2,1)S(1)} %get-tuple-element.312), channel_id=1, source_target_pairs={{0,4},{4,8},{8,12},{12,16},{16,20},{20,24},{24,28},{28,0},{1,5},{5... | collective-permute-start | bytes 786440 | tf_op jit(solution)/shard_map/while/body/eval_jaxpr/ppermute | solution.py:9
  101.9 0.8 copy-start.1
  101.9 0.9 copy-start.5
  101.9 19.5 %copy-start.6 = (bf16[256,128]{1,0:T(8,128)(2,1)S(1)}, bf16[256,128]{1,0:T(8,128)(2,1)}, u32[]{:S(2)}) copy-start(bf16[256,128]{1,0:T(8,128)(2,1)} %param.21) | copy-start | bytes 196612
  102.7 18.7 %copy-start.8 = (f32[128]{0:T(128)S(1)}, f32[128]{0:T(128)}, u32[]{:S(2)}) copy-start(f32[128]{0:T(128)} %param.15) | copy-start | bytes 1540
  102.7 143.3 %all-reduce.2.cloned.1.call-start = ((), (), s32[]{:S(2)}) async-start(), calls=%async_computation.2 | async-start | bytes 131072 | tf_op jit(solution)/shard_map/psum | solution.py:63
  121.4 1.8 copy-start.2
Sparse Core Ops, SparseCore 0:
  102.9 18.5 reduce-scatter.1
  128.5 117.5 all-reduce.1
where the time goes:
time: 256 us; the launch traced here: 254 us
  waiting for transfers between devices  157 us (61%)
  blocking collectives  39.4 us (15%)
  matrix products  18.6 us (7%)
  local copies, waits for them, and re-layouts  15.2 us (6%)
  between operations  14.2 us (6%)
  other arithmetic  5.89 us (2%)
  starting transfers between devices  3.37 us (1%)
    psum x1, waiting for transfers between devices, shards(): grad_weight, grad_bias = lax.psum((local_gw, local_gb), ('blk', 'rep'))  82.6 us
    ppermute x7, waiting for transfers between devices, passed_along(): lax.ppermute(array, axis, [(i, (i + by) % length) for i in range(length)])  55.8 us
    psum x1, blocking collectives, shards(): grad_weight, grad_bias = lax.psum((local_gw, local_gb), ('blk', 'rep'))  39.4 us
    reduce_scatter x1, waiting for transfers between devices, shards(): lax.psum_scatter(partial_sum, 'rep', scatter_dimension=0, tiled=True)  18.6 us
    dot_general x8, matrix products, shard_term(): jnp.einsum('kij,kjf->kif', values, picked, preferred_element_type=jnp.flo...  9.24 us
    dot_general x8, matrix products, shard_term(): jnp.einsum('rk,kif->rif', onehot, prod, precision=lax.Precision.HIGHEST)  6.68 us
    lt x8, other arithmetic, shard_term(): alive = jnp.arange(slots, dtype=jnp.int32) < count  5.19 us
  transfers between devices with their start and end apart: 9, of which 9 were waited for; matrix products, arithmetic and copies ran while one was open for 3% of the time, Pallas kernels for 0%

commit v1 on v0

v1 whole, which is shorter than its diff:
```python
import functools

import jax
import jax.numpy as jnp
from jax import lax
from jax.experimental import pallas as pl
from jax.experimental.pallas import tpu as pltpu
from jax.sharding import PartitionSpec as P

VMEM = pl.BlockSpec(memory_space=pltpu.VMEM)
SMEM = pl.BlockSpec(memory_space=pltpu.SMEM)
LIMIT = 48 * 1024 * 1024


def spmm_kernel(nblk, nrep, *refs):
    rows_ref, cols_ref, live_ref, tiles_ref, own_ref = refs[:5]
    near = refs[5 : 5 + nblk - 1]
    far = refs[5 + nblk - 1 : 5 + 2 * (nblk - 1)]
    mine_ref, keep_ref, send_ref, feat, acc = refs[5 + 2 * (nblk - 1) :]
    me = lax.axis_index("blk")
    rep = lax.axis_index("rep")
    core, pair = rep % 2, rep // 2
    npair = nrep // 2
    slots, tile = tiles_ref.shape[1], tiles_ref.shape[2]
    rblk = own_ref.shape[0] // tile
    half = rblk // 2

    acc[...] = jnp.zeros_like(acc)
    feat[0] = own_ref[...].reshape(feat.shape[1:])
    for s in range(1, nblk):
        feat[s, pl.ds(core * half, half)] = near[s - 1][...].reshape((half,) + feat.shape[2:])
        feat[s, pl.ds((1 - core) * half, half)] = far[s - 1][...].reshape((half,) + feat.shape[2:])

    def shard_step(s):
        shard = (me - s + nblk) % nblk
        for k in range(slots):
            prod = jnp.dot(tiles_ref[shard, k], feat[s, cols_ref[shard, k]], preferred_element_type=jnp.float32)
            row = jnp.where(k < live_ref[shard], rows_ref[shard, k], rblk)
            at = pl.ds(pl.multiple_of(row * tile, tile), tile)
            acc[at] = acc[at] + prod

    if nblk <= 8:
        for s in range(nblk):
            shard_step(s)
    else:
        lax.fori_loop(0, nblk, lambda s, c: (shard_step(s), c)[1], 0)

    share = rblk * tile // nrep

    def part(owner):
        return acc[pl.ds(pl.multiple_of(owner * share, share), share)]

    for s in range(npair):
        other = (pair + s) % npair
        send_ref[s] = part(2 * other + 1 - core)
        if s == 0:
            mine_ref[...] = part(2 * other + core)
        else:
            keep_ref[s - 1] = part(2 * other + core)


def tail_kernel(npieces, mine_ref, first_ref, got_ref, weight_ref, bias_ref, cot_ref, out_ref, grad_ref):
    agg = mine_ref[...] + first_ref[0]
    for i in range(got_ref.shape[0]):
        agg = agg + got_ref[i]
    agg = agg.astype(jnp.bfloat16)
    pre = jnp.dot(agg, weight_ref[...], preferred_element_type=jnp.float32) + bias_ref[...]
    sigma = 1.0 / (1.0 + jnp.exp(-pre))
    out_ref[...] = (pre * sigma).astype(jnp.bfloat16)
    delta = cot_ref[...].astype(jnp.float32) * (sigma * (1.0 + pre * (1.0 - sigma)))
    gw = lax.dot_general(
        agg, delta.astype(jnp.bfloat16), (((0,), (0,)), ((), ())), preferred_element_type=jnp.float32
    )
    gb = jnp.sum(delta, axis=0, keepdims=True)
    feat = gw.shape[0]
    grad_ref[pl.ds(0, feat)] = gw
    grad_ref[pl.ds(feat, grad_ref.shape[0] - feat)] = jnp.zeros(
        (grad_ref.shape[0] - feat, gw.shape[1]), jnp.float32
    )
    grad_ref[pl.ds(feat, 1)] = gb


def shards(features, weight, bias, tiles, tile_row, tile_col, tile_live, label_mask, cotangent):
    nblk, nrep = lax.axis_size("blk"), lax.axis_size("rep")
    npair = nrep // 2
    rep = lax.axis_index("rep")
    core = rep % 2
    local, feat_dim = features.shape
    tile = tiles.shape[-1]
    rblk = local // tile
    half = local // 2
    hid = weight.shape[1]
    share = local // nrep
    swap = [(i, i ^ 1) for i in range(nrep)]

    half_own = lax.dynamic_slice_in_dim(features, core * half, half, 0)
    near, far = [], []
    for s in range(1, nblk):
        got = lax.ppermute(half_own, "blk", [(i, (i + s) % nblk) for i in range(nblk)])
        near.append(got)
        far.append(lax.ppermute(got, "rep", swap))

    masked = cotangent * label_mask.astype(jnp.bfloat16)[:, None]

    mine, keep, send = pl.pallas_call(
        functools.partial(spmm_kernel, nblk, nrep),
        out_shape=(
            jax.ShapeDtypeStruct((share, feat_dim), jnp.float32),
            jax.ShapeDtypeStruct((npair - 1, share, feat_dim), jnp.float32),
            jax.ShapeDtypeStruct((npair, share, feat_dim), jnp.float32),
        ),
        in_specs=[SMEM] * 3 + [VMEM] * (2 + 2 * (nblk - 1)),
        out_specs=(VMEM,) * 3,
        scratch_shapes=[
            pltpu.VMEM((nblk, rblk, tile, feat_dim), jnp.bfloat16),
            pltpu.VMEM(((rblk + 1) * tile, feat_dim), jnp.float32),
        ],
        compiler_params=pltpu.CompilerParams(vmem_limit_bytes=LIMIT),
    )(tile_row[0, 0], tile_col[0, 0], tile_live[0, 0], tiles[0, 0], features, *near, *far)

    first = lax.ppermute(send, "rep", swap)
    across = keep + first[1:]
    got = []
    for s in range(1, npair):
        got.append(
            lax.ppermute(across[s - 1], "rep", [(i, (i + 2 * s) % nrep) for i in range(nrep)])
        )
    got = jnp.stack(got)

    ndev = nblk * nrep
    piece = 8 * -(-(feat_dim + 1) // (8 * ndev))
    output, grads = pl.pallas_call(
        functools.partial(tail_kernel, ndev),
        out_shape=(
            jax.ShapeDtypeStruct((share, hid), jnp.bfloat16),
            jax.ShapeDtypeStruct((ndev * piece, hid), jnp.float32),
        ),
        in_specs=[VMEM] * 6,
        out_specs=(VMEM,) * 2,
        compiler_params=pltpu.CompilerParams(vmem_limit_bytes=LIMIT),
    )(mine, first, got, weight, bias[None, :], masked)

    both = ("blk", "rep")
    pieces = lax.all_to_all(grads.reshape(ndev, piece, hid), both, 0, 0)
    total = jnp.sum(pieces, axis=0)
    spread = lax.all_to_all(jnp.broadcast_to(total[None], (ndev, piece, hid)), both, 0, 0)
    spread = spread.reshape(ndev * piece, hid)
    return output, spread[:feat_dim], spread[feat_dim]


def solution(mesh):
    placed = (
        P("blk", None),
        P(),
        P(),
        P("blk", "rep", None, None, None, None),
        P("blk", "rep", None, None),
        P("blk", "rep", None, None),
        P("blk", "rep", None),
        P(("blk", "rep")),
        P(("blk", "rep"), None),
    )
    return jax.shard_map(
        shards,
        mesh=mesh,
        in_specs=placed,
        out_specs=(P(("blk", "rep"), None), P(), P()),
        check_vma=False,
    )
```

time: 256 us -> 68.7 us (0.27)
  waiting for transfers between devices: 157 us -> 15 us
  matrix products: 18.6 us -> 0 us
  starting transfers between devices: 3.37 us -> 20 us
  blocking collectives: 39.4 us -> 24.6 us
  between operations: 14.2 us -> 0.74 us
  local copies, waits for them, and re-layouts: 15.2 us -> 5.73 us
  other arithmetic: 5.89 us -> 0.15 us
    psum x1 -> x0, waiting for transfers between devices: 82.6 us -> none  [shards(): grad_weight, grad_bias = lax.psum((local_gw, local_gb), ('blk', 'rep'))]
    ppermute x7 -> x16, waiting for transfers between devices: 55.8 us -> 15 us  [the longest x7 9.71 us: shards(): lax.ppermute(half_own, 'blk', [(i, (i + s) % nblk) for i in range(nblk)])]
    psum x1 -> x0, blocking collectives: 39.4 us -> none  [shards(): grad_weight, grad_bias = lax.psum((local_gw, local_gb), ('blk', 'rep'))]
    all_to_all x0 -> x2, blocking collectives: none -> 24.6 us  [the longest x1 14.6 us: shards(): pieces = lax.all_to_all(grads.reshape(ndev, piece, hid), both, 0, 0)]
    reduce_scatter x1 -> x0, waiting for transfers between devices: 18.6 us -> none  [shards(): lax.psum_scatter(partial_sum, 'rep', scatter_dimension=0, tiled=True)]
    dot_general x18 -> x0, matrix products: 18.6 us -> none  [the longest x8 9.24 us: shard_term(): jnp.einsum('kij,kjf->kif', values, picked, preferred_element_type=jnp.flo...]
    ppermute x7 -> x16, starting transfers between devices: 3.3 us -> 20 us  [the longest x7 16.6 us: shards(): lax.ppermute(half_own, 'blk', [(i, (i + s) % nblk) for i in range(nblk)])]
    lt x8 -> x0, other arithmetic: 5.19 us -> none  [shard_term(): alive = jnp.arange(slots, dtype=jnp.int32) < count]
  transfers between devices with their start and end apart: 9 -> 16, of which waited for: 9 -> 7; matrix products, arithmetic and copies ran while one was open for 3% -> 0% of each run, Pallas kernels for 0% -> 0%
where the time goes in v1:
time: 68.7 us; the launch traced here: 68.4 us
  blocking collectives  24.6 us (36%)
  starting transfers between devices  20 us (29%)
  waiting for transfers between devices  15 us (22%)
  local copies, waits for them, and re-layouts  5.73 us (8%)
  Pallas kernels  2.15 us (3%)
  between operations  0.74 us (1%)
    ppermute x7, starting transfers between devices, shards(): lax.ppermute(half_own, 'blk', [(i, (i + s) % nblk) for i in range(nblk)])  16.6 us
    all_to_all x1, blocking collectives, shards(): pieces = lax.all_to_all(grads.reshape(ndev, piece, hid), both, 0, 0)  14.6 us
    all_to_all x1, blocking collectives, shards(): lax.all_to_all(jnp.broadcast_to(total[None], (ndev, piece, hid)), both, 0...  10 us
    ppermute x7, waiting for transfers between devices, shards(): lax.ppermute(half_own, 'blk', [(i, (i + s) % nblk) for i in range(nblk)])  9.71 us
    ppermute x1, waiting for transfers between devices, shards(): lax.ppermute(across[s - 1], 'rep', [(i, (i + 2 * s) % nrep) for i in rang...  4.08 us
    unnamed x18, local copies, waits for them, and re-layouts  3.45 us
    ppermute x1, starting transfers between devices, shards(): lax.ppermute(across[s - 1], 'rep', [(i, (i + 2 * s) % nrep) for i in rang...  1.58 us
    ppermute x7, starting transfers between devices, shards(): far.append(lax.ppermute(got, 'rep', swap))  1.47 us
  transfers between devices with their start and end apart: 16, of which 7 were waited for; matrix products, arithmetic and copies ran while one was open for 0% of the time, Pallas kernels for 0%

profile of v1, /device:TPU:0, one launch (start us, length us, event | category | flops | bytes accessed | tf_op | source)
XLA Modules:
  0.0 68.4 jit_solution(4087214676601469058)
XLA Ops:
  0.7 1.0 %constant_dynamic-slice_fusion = bf16[512,128]{1,0:T(8,128)(2,1)S(1)} fusion(bf16[1024,128]{1,0:T(8,128)(2,1)} %refs_4_.1, s32[]{:T(128)S(6)} %select_n.11), kind=kLoop, calls=%fused_computation.5 | loop fusion | bytes 262148 | tf_op jit(solution)/shard_map/dynamic_slice | solution.py:96
  1.6 4.1 %collective-permute-start.3 = (bf16[512,128]{1,0:T(8,128)(2,1)S(1)}, bf16[512,128]{1,0:T(8,128)(2,1)S(1)}, u32[]{:S(2)}, u32[]{:S(2)}) collective-permute-start(bf16[512,128]{1,0:T(8,128)(2,1)S(1)} %constant_dynamic-slice_fusion), channel_id=1, source_target_pairs={{0,16},{4,20},{8,24},{12,28},{16,0},{20,4},{24,8},{28,12},{1,17},{... | collective-permute-start | bytes 393224 | tf_op jit(solution)/shard_map/ppermute | solution.py:99
  5.7 1.3 %collective-permute-start.4 = (bf16[512,128]{1,0:T(8,128)(2,1)S(1)}, bf16[512,128]{1,0:T(8,128)(2,1)S(1)}, u32[]{:S(2)}, u32[]{:S(2)}) collective-permute-start(bf16[512,128]{1,0:T(8,128)(2,1)S(1)} %constant_dynamic-slice_fusion), channel_id=1, source_target_pairs={{0,20},{4,24},{8,28},{12,0},{16,4},{20,8},{24,12},{28,16},{1,21},{... | collective-permute-start | bytes 393224 | tf_op jit(solution)/shard_map/ppermute | solution.py:99
  7.0 3.6 %collective-permute-start.5 = (bf16[512,128]{1,0:T(8,128)(2,1)S(1)}, bf16[512,128]{1,0:T(8,128)(2,1)S(1)}, u32[]{:S(2)}, u32[]{:S(2)}) collective-permute-start(bf16[512,128]{1,0:T(8,128)(2,1)S(1)} %constant_dynamic-slice_fusion), channel_id=1, source_target_pairs={{0,24},{4,28},{8,0},{12,4},{16,8},{20,12},{24,16},{28,20},{1,25},{... | collective-permute-start | bytes 393224 | tf_op jit(solution)/shard_map/ppermute | solution.py:99
  10.6 0.5 collective-permute-start.6
  11.1 1.5 %collective-permute-start = (bf16[512,128]{1,0:T(8,128)(2,1)S(1)}, bf16[512,128]{1,0:T(8,128)(2,1)S(1)}, u32[]{:S(2)}, u32[]{:S(2)}) collective-permute-start(bf16[512,128]{1,0:T(8,128)(2,1)S(1)} %constant_dynamic-slice_fusion), channel_id=1, source_target_pairs={{0,4},{4,8},{8,12},{12,16},{16,20},{20,24},{24,28},{28,0},{1,5},{5... | collective-permute-start | bytes 393224 | tf_op jit(solution)/shard_map/ppermute | solution.py:99
  12.6 3.1 %collective-permute-done.3.refs_8_ = bf16[512,128]{1,0:T(8,128)(2,1)S(1)} collective-permute-done((bf16[512,128]{1,0:T(8,128)(2,1)S(1)}, bf16[512,128]{1,0:T(8,128)(2,1)S(1)}, u32[]{:S(2)}, u32[]{:S(2)}) %collective-permute-start.3) | collective-permute-done | bytes 131104 | tf_op jit(solution)/shard_map/ppermute | solution.py:99
  15.7 5.6 %collective-permute-start.1 = (bf16[512,128]{1,0:T(8,128)(2,1)S(1)}, bf16[512,128]{1,0:T(8,128)(2,1)S(1)}, u32[]{:S(2)}, u32[]{:S(2)}) collective-permute-start(bf16[512,128]{1,0:T(8,128)(2,1)S(1)} %constant_dynamic-slice_fusion), channel_id=1, source_target_pairs={{0,8},{4,12},{8,16},{12,20},{16,24},{20,28},{24,0},{28,4},{1,9},{5... | collective-permute-start | bytes 393224 | tf_op jit(solution)/shard_map/ppermute | solution.py:99
  21.3 0.0 collective-permute-done.4.refs_9_
  21.3 0.0 collective-permute-start.2
  21.3 0.0 collective-permute-done.5.refs_10_
  21.3 0.1 collective-permute-start.10
  21.4 0.0 collective-permute-done.6.refs_11_
  21.4 0.5 collective-permute-start.11
  21.9 0.0 collective-permute-done.refs_5_
  21.9 0.1 collective-permute-start.12
  22.0 6.4 %collective-permute-done.1.refs_6_ = bf16[512,128]{1,0:T(8,128)(2,1)S(1)} collective-permute-done((bf16[512,128]{1,0:T(8,128)(2,1)S(1)}, bf16[512,128]{1,0:T(8,128)(2,1)S(1)}, u32[]{:S(2)}, u32[]{:S(2)}) %collective-permute-start.1) | collective-permute-done | bytes 131104 | tf_op jit(solution)/shard_map/ppermute | solution.py:99
  28.4 0.0 collective-permute-start.13
  28.4 0.2 collective-permute-done.2.refs_7_
  28.6 0.3 collective-permute-start.7
  28.9 0.0 collective-permute-done.10.refs_15_
  28.9 0.2 collective-permute-start.8
  29.1 0.0 collective-permute-done.11.refs_16_
  29.1 0.3 collective-permute-start.9
  29.4 0.1 copy.12.refs_0_
  29.5 0.6 copy-done.7
  30.1 0.1 copy.13.refs_1_
  30.2 0.0 collective-permute-done.12.refs_17_
  30.2 0.0 collective-permute-done.13.refs_18_
  30.2 0.1 collective-permute-done.8.refs_13_
  30.3 0.2 collective-permute-done.9.refs_14_
  30.5 0.7 copy-done.4
  31.1 1.2 %copy-done = bf16[1,1,8,4,128,128]{5,4,3,2,1,0:T(8,128)(2,1)S(1)} copy-done((bf16[1,1,8,4,128,128]{5,4,3,2,1,0:T(8,128)(2,1)S(1)}, bf16[1,1,8,4,128,128]{5,4,3,2,1,0:T(8,128)(2,1)}, u32[]{:S(2)}) %copy-start) | copy-done | bytes 1048600
  32.4 1.3 %shard_map.112 = (f32[256,128]{1,0:T(8,128)S(1)}, f32[1,256,128]{2,1,0:T(8,128)S(1)}, f32[2,256,128]{2,1,0:T(8,128)S(1)}) custom-call(s32[8,4]{1,0:T(8,128)S(1)} %copy.12.refs_0_, s32[8,4]{1,0:T(8,128)S(1)} %copy.13.refs_1_, s32[8]{0:T(128)S(1)} %bitcast.18, bf16[8,4,128,128]{3,2,1,0:T(8,128)(2,1)S(1)} %bitcast.14, bf16[1024,128]{1,0:T(8,128)(2,1)S(1)} %copy-done.1, ...), custom_call_target="tpu_custom_call" | custom-call | tf_op jit(solution)/shard_map/pallas_call | solution.py:105
  33.7 0.0 copy-start.8
  33.7 0.4 collective-permute-start.14
  34.1 0.3 copy-done.8
  34.4 0.9 %collective-permute-done.14.first_ref = f32[2,256,128]{2,1,0:T(8,128)S(1)} collective-permute-done((f32[2,256,128]{2,1,0:T(8,128)S(1)}, f32[2,256,128]{2,1,0:T(8,128)S(1)}, u32[]{:S(2)}, u32[]{:S(2)}) %collective-permute-start.14) | collective-permute-done | bytes 262176 | tf_op jit(solution)/shard_map/ppermute | solution.py:121
  35.3 0.0 copy-start.2
  35.3 1.6 %collective-permute-start.15 = (f32[256,128]{1,0:T(8,128)S(1)}, f32[256,128]{1,0:T(8,128)S(1)}, u32[]{:S(2)}, u32[]{:S(2)}) collective-permute-start(f32[256,128]{1,0:T(8,128)S(1)} %fusion), channel_id=1, source_target_pairs={{0,2},{1,3},{2,0},{3,1},{4,6},{5,7},{6,4},{7,5},{8,10},{9,11},{10,... | collective-permute-start | bytes 393224 | tf_op jit(solution)/shard_map/ppermute | solution.py:126
  36.9 0.1 broadcast_multiply_fusion.cot_ref
  37.0 4.1 %collective-permute-done.15 = f32[256,128]{1,0:T(8,128)S(1)} collective-permute-done((f32[256,128]{1,0:T(8,128)S(1)}, f32[256,128]{1,0:T(8,128)S(1)}, u32[]{:S(2)}, u32[]{:S(2)}) %collective-permute-start.15) | collective-permute-done | bytes 131104 | tf_op jit(solution)/shard_map/ppermute | solution.py:126
  41.1 0.7 copy-done.3
  41.8 0.8 %shard_map.113 = (bf16[256,128]{1,0:T(8,128)(2,1)}, f32[256,128]{1,0:T(8,128)S(1)}) custom-call(f32[256,128]{1,0:T(8,128)S(1)} %get-tuple-element.8.mine_ref, f32[2,256,128]{2,1,0:T(8,128)S(1)} %collective-permute-done.14.first_ref, f32[1,256,128]{2,1,0:T(8,128)S(1)} %bitcast.16, bf16[128,128]{1,0:T(8,128)(2,1)S(1)} %copy-done.2, f32[1,128]{1,0:T(1,128)S(1)} %bitcast.17, ...), custom_call_target="tpu_custom_call" | custom-call | tf_op jit(solution)/shard_map/pallas_call | solution.py:132
  42.6 14.6 %all_to_all.10 = f32[32,8,128]{2,1,0:T(8,128)S(1)} all-to-all(f32[32,8,128]{2,1,0:T(8,128)S(1)} %bitcast.15), channel_id=1, replica_groups=mesh['blk'=8,'rep'=4] {'blk','rep'}, dimensions={0} | all-to-all | bytes 262144 | tf_op jit(solution)/shard_map/all_to_all | solution.py:144
  57.3 10.0 %all_to_all.11 = f32[32,8,128]{2,1,0:T(8,128)S(1)} all-to-all(f32[32,8,128]{2,1,0:T(8,128)S(1)} %broadcast_in_dim.5), channel_id=1, replica_groups=mesh['blk'=8,'rep'=4] {'blk','rep'}, dimensions={0} | all-to-all | bytes 262144 | tf_op jit(solution)/shard_map/all_to_all | solution.py:146
  67.3 0.5 slice_bitcast_fusion.1
  67.8 0.6 slice_bitcast_fusion
  (16 shorter events, 0.1 us)
Async XLA Ops:
  0.6 29.9 %copy-start.1 = (bf16[1024,128]{1,0:T(8,128)(2,1)S(1)}, bf16[1024,128]{1,0:T(8,128)(2,1)}, u32[]{:S(2)}) copy-start(bf16[1024,128]{1,0:T(8,128)(2,1)} %refs_4_.1) | copy-start | bytes 786436
  0.7 28.8 %copy-start.6 = (s32[1,1,8,4]{2,3,1,0:T(4,128)S(1)}, s32[1,1,8,4]{2,3,1,0:T(4,128)}, u32[]{:S(2)}) copy-start(s32[1,1,8,4]{2,3,1,0:T(4,128)} %param.13) | copy-start | bytes 388
  1.6 14.0 %collective-permute-start.3 = (bf16[512,128]{1,0:T(8,128)(2,1)S(1)}, bf16[512,128]{1,0:T(8,128)(2,1)S(1)}, u32[]{:S(2)}, u32[]{:S(2)}) collective-permute-start(bf16[512,128]{1,0:T(8,128)(2,1)S(1)} %constant_dynamic-slice_fusion), channel_id=1, source_target_pairs={{0,16},{4,20},{8,24},{12,28},{16,0},{20,4},{24,8},{28,12},{1,17},{... | collective-permute-start | bytes 393224 | tf_op jit(solution)/shard_map/ppermute | solution.py:99
  5.7 15.6 %collective-permute-start.4 = (bf16[512,128]{1,0:T(8,128)(2,1)S(1)}, bf16[512,128]{1,0:T(8,128)(2,1)S(1)}, u32[]{:S(2)}, u32[]{:S(2)}) collective-permute-start(bf16[512,128]{1,0:T(8,128)(2,1)S(1)} %constant_dynamic-slice_fusion), channel_id=1, source_target_pairs={{0,20},{4,24},{8,28},{12,0},{16,4},{20,8},{24,12},{28,16},{1,21},{... | collective-permute-start | bytes 393224 | tf_op jit(solution)/shard_map/ppermute | solution.py:99
  7.0 14.3 %collective-permute-start.5 = (bf16[512,128]{1,0:T(8,128)(2,1)S(1)}, bf16[512,128]{1,0:T(8,128)(2,1)S(1)}, u32[]{:S(2)}, u32[]{:S(2)}) collective-permute-start(bf16[512,128]{1,0:T(8,128)(2,1)S(1)} %constant_dynamic-slice_fusion), channel_id=1, source_target_pairs={{0,24},{4,28},{8,0},{12,4},{16,8},{20,12},{24,16},{28,20},{1,25},{... | collective-permute-start | bytes 393224 | tf_op jit(solution)/shard_map/ppermute | solution.py:99
  10.6 10.8 %collective-permute-start.6 = (bf16[512,128]{1,0:T(8,128)(2,1)S(1)}, bf16[512,128]{1,0:T(8,128)(2,1)S(1)}, u32[]{:S(2)}, u32[]{:S(2)}) collective-permute-start(bf16[512,128]{1,0:T(8,128)(2,1)S(1)} %constant_dynamic-slice_fusion), channel_id=1, source_target_pairs={{0,28},{4,0},{8,4},{12,8},{16,12},{20,16},{24,20},{28,24},{1,29},{... | collective-permute-start | bytes 393224 | tf_op jit(solution)/shard_map/ppermute | solution.py:99
  11.1 10.7 %collective-permute-start = (bf16[512,128]{1,0:T(8,128)(2,1)S(1)}, bf16[512,128]{1,0:T(8,128)(2,1)S(1)}, u32[]{:S(2)}, u32[]{:S(2)}) collective-permute-start(bf16[512,128]{1,0:T(8,128)(2,1)S(1)} %constant_dynamic-slice_fusion), channel_id=1, source_target_pairs={{0,4},{4,8},{8,12},{12,16},{16,20},{20,24},{24,28},{28,0},{1,5},{5... | collective-permute-start | bytes 393224 | tf_op jit(solution)/shard_map/ppermute | solution.py:99
  15.7 12.7 %collective-permute-start.1 = (bf16[512,128]{1,0:T(8,128)(2,1)S(1)}, bf16[512,128]{1,0:T(8,128)(2,1)S(1)}, u32[]{:S(2)}, u32[]{:S(2)}) collective-permute-start(bf16[512,128]{1,0:T(8,128)(2,1)S(1)} %constant_dynamic-slice_fusion), channel_id=1, source_target_pairs={{0,8},{4,12},{8,16},{12,20},{16,24},{20,28},{24,0},{28,4},{1,9},{5... | collective-permute-start | bytes 393224 | tf_op jit(solution)/shard_map/ppermute | solution.py:99
  21.3 7.3 %collective-permute-start.2 = (bf16[512,128]{1,0:T(8,128)(2,1)S(1)}, bf16[512,128]{1,0:T(8,128)(2,1)S(1)}, u32[]{:S(2)}, u32[]{:S(2)}) collective-permute-start(bf16[512,128]{1,0:T(8,128)(2,1)S(1)} %constant_dynamic-slice_fusion), channel_id=1, source_target_pairs={{0,12},{4,16},{8,20},{12,24},{16,28},{20,0},{24,4},{28,8},{1,13},{... | collective-permute-start | bytes 393224 | tf_op jit(solution)/shard_map/ppermute | solution.py:99
  21.3 7.6 %collective-permute-start.10 = (bf16[512,128]{1,0:T(8,128)(2,1)S(1)}, bf16[512,128]{1,0:T(8,128)(2,1)S(1)}, u32[]{:S(2)}, u32[]{:S(2)}) collective-permute-start(bf16[512,128]{1,0:T(8,128)(2,1)S(1)} %collective-permute-done.3.refs_8_), channel_id=1, source_target_pairs={{0,1},{1,0},{2,3},{3,2},{4,5},{5,4},{6,7},{7,6},{8,9},{9,8},{10,11... | collective-permute-start | bytes 393224 | tf_op jit(solution)/shard_map/ppermute | solution.py:101
  21.4 7.8 %collective-permute-start.11 = (bf16[512,128]{1,0:T(8,128)(2,1)S(1)}, bf16[512,128]{1,0:T(8,128)(2,1)S(1)}, u32[]{:S(2)}, u32[]{:S(2)}) collective-permute-start(bf16[512,128]{1,0:T(8,128)(2,1)S(1)} %collective-permute-done.4.refs_9_), channel_id=1, source_target_pairs={{0,1},{1,0},{2,3},{3,2},{4,5},{5,4},{6,7},{7,6},{8,9},{9,8},{10,11... | collective-permute-start | bytes 393224 | tf_op jit(solution)/shard_map/ppermute | solution.py:101
  21.9 8.3 %collective-permute-start.12 = (bf16[512,128]{1,0:T(8,128)(2,1)S(1)}, bf16[512,128]{1,0:T(8,128)(2,1)S(1)}, u32[]{:S(2)}, u32[]{:S(2)}) collective-permute-start(bf16[512,128]{1,0:T(8,128)(2,1)S(1)} %collective-permute-done.5.refs_10_), channel_id=1, source_target_pairs={{0,1},{1,0},{2,3},{3,2},{4,5},{5,4},{6,7},{7,6},{8,9},{9,8},{10,11... | collective-permute-start | bytes 393224 | tf_op jit(solution)/shard_map/ppermute | solution.py:101
  28.4 1.8 %collective-permute-start.13 = (bf16[512,128]{1,0:T(8,128)(2,1)S(1)}, bf16[512,128]{1,0:T(8,128)(2,1)S(1)}, u32[]{:S(2)}, u32[]{:S(2)}) collective-permute-start(bf16[512,128]{1,0:T(8,128)(2,1)S(1)} %collective-permute-done.6.refs_11_), channel_id=1, source_target_pairs={{0,1},{1,0},{2,3},{3,2},{4,5},{5,4},{6,7},{7,6},{8,9},{9,8},{10,11... | collective-permute-start | bytes 393224 | tf_op jit(solution)/shard_map/ppermute | solution.py:101
  28.6 1.6 %collective-permute-start.7 = (bf16[512,128]{1,0:T(8,128)(2,1)S(1)}, bf16[512,128]{1,0:T(8,128)(2,1)S(1)}, u32[]{:S(2)}, u32[]{:S(2)}) collective-permute-start(bf16[512,128]{1,0:T(8,128)(2,1)S(1)} %collective-permute-done.refs_5_), channel_id=1, source_target_pairs={{0,1},{1,0},{2,3},{3,2},{4,5},{5,4},{6,7},{7,6},{8,9},{9,8},{10,11... | collective-permute-start | bytes 393224 | tf_op jit(solution)/shard_map/ppermute | solution.py:101
  28.9 1.3 %collective-permute-start.8 = (bf16[512,128]{1,0:T(8,128)(2,1)S(1)}, bf16[512,128]{1,0:T(8,128)(2,1)S(1)}, u32[]{:S(2)}, u32[]{:S(2)}) collective-permute-start(bf16[512,128]{1,0:T(8,128)(2,1)S(1)} %collective-permute-done.1.refs_6_), channel_id=1, source_target_pairs={{0,1},{1,0},{2,3},{3,2},{4,5},{5,4},{6,7},{7,6},{8,9},{9,8},{10,11... | collective-permute-start | bytes 393224 | tf_op jit(solution)/shard_map/ppermute | solution.py:101
  29.1 1.3 %collective-permute-start.9 = (bf16[512,128]{1,0:T(8,128)(2,1)S(1)}, bf16[512,128]{1,0:T(8,128)(2,1)S(1)}, u32[]{:S(2)}, u32[]{:S(2)}) collective-permute-start(bf16[512,128]{1,0:T(8,128)(2,1)S(1)} %collective-permute-done.2.refs_7_), channel_id=1, source_target_pairs={{0,1},{1,0},{2,3},{3,2},{4,5},{5,4},{6,7},{7,6},{8,9},{9,8},{10,11... | collective-permute-start | bytes 393224 | tf_op jit(solution)/shard_map/ppermute | solution.py:101
  29.4 0.7 copy-start.7
  30.5 0.7 copy-start.4
  31.1 1.2 %copy-start = (bf16[1,1,8,4,128,128]{5,4,3,2,1,0:T(8,128)(2,1)S(1)}, bf16[1,1,8,4,128,128]{5,4,3,2,1,0:T(8,128)(2,1)}, u32[]{:S(2)}) copy-start(bf16[1,1,8,4,128,128]{5,4,3,2,1,0:T(8,128)(2,1)} %param.12) | copy-start | bytes 3145732
  33.7 0.7 copy-start.8
  33.7 1.6 %collective-permute-start.14 = (f32[2,256,128]{2,1,0:T(8,128)S(1)}, f32[2,256,128]{2,1,0:T(8,128)S(1)}, u32[]{:S(2)}, u32[]{:S(2)}) collective-permute-start(f32[2,256,128]{2,1,0:T(8,128)S(1)} %get-tuple-element.9), channel_id=1, source_target_pairs={{0,1},{1,0},{2,3},{3,2},{4,5},{5,4},{6,7},{7,6},{8,9},{9,8},{10,11... | collective-permute-start | bytes 786440 | tf_op jit(solution)/shard_map/ppermute | solution.py:121
  35.3 1.6 %copy-start.5 = (bf16[256,128]{1,0:T(8,128)(2,1)S(1)}, bf16[256,128]{1,0:T(8,128)(2,1)}, u32[]{:S(2)}) copy-start(bf16[256,128]{1,0:T(8,128)(2,1)} %param.17) | copy-start | bytes 196612
  35.3 5.8 %copy-start.2 = (bf16[128,128]{1,0:T(8,128)(2,1)S(1)}, bf16[128,128]{1,0:T(8,128)(2,1)}, u32[]{:S(2)}) copy-start(bf16[128,128]{1,0:T(8,128)(2,1)} %weight_ref.1) | copy-start | bytes 98308
  35.3 5.8 %collective-permute-start.15 = (f32[256,128]{1,0:T(8,128)S(1)}, f32[256,128]{1,0:T(8,128)S(1)}, u32[]{:S(2)}, u32[]{:S(2)}) collective-permute-start(f32[256,128]{1,0:T(8,128)S(1)} %fusion), channel_id=1, source_target_pairs={{0,2},{1,3},{2,0},{3,1},{4,6},{5,7},{6,4},{7,5},{8,10},{9,11},{10,... | collective-permute-start | bytes 393224 | tf_op jit(solution)/shard_map/ppermute | solution.py:126
  41.1 0.7 copy-start.3

commit v2 on v1

v2 whole, which is shorter than its diff:
```python
import functools

import jax
import jax.numpy as jnp
from jax import lax
from jax.experimental import pallas as pl
from jax.experimental.pallas import tpu as pltpu
from jax.sharding import PartitionSpec as P

VMEM = pl.BlockSpec(memory_space=pltpu.VMEM)
SMEM = pl.BlockSpec(memory_space=pltpu.SMEM)
HBM = pl.BlockSpec(memory_space=pltpu.HBM)
ANY = pl.BlockSpec(memory_space=pl.ANY)
LIMIT = 48 * 1024 * 1024
BOTH = ("blk", "rep")


def stage_kernel(rblk, *refs):
    sources, targets = refs[:9], refs[9:13] + refs[15:20]
    masked_ref, code_ref, sems = refs[13], refs[14], refs[20]
    mask_ref, cot_ref, row_ref, col_ref, live_ref = targets[4:]
    copies = [pltpu.make_async_copy(x, y, sems.at[i]) for i, (x, y) in enumerate(zip(sources, targets))]
    for copy in reversed(copies):
        copy.start()
    for copy in copies[4:]:
        copy.wait()
    share = cot_ref.shape[0]
    eye = lax.broadcasted_iota(jnp.int32, (share, share), 0) == lax.broadcasted_iota(jnp.int32, (share, share), 1)
    column = jnp.sum(jnp.where(eye, mask_ref[...].astype(jnp.float32), 0.0), axis=1, keepdims=True)
    masked_ref[...] = (cot_ref[...].astype(jnp.float32) * column).astype(jnp.bfloat16)
    slot = lax.broadcasted_iota(jnp.int32, code_ref.shape, 0)
    row = jnp.where(slot < live_ref[0], row_ref[0, 0], rblk)
    code_ref[...] = row * rblk + col_ref[0, 0]
    for copy in copies[:4]:
        copy.wait()


def spmm_kernel(nblk, nrep, plan, *refs):
    code_ref, tiles_ref = refs[:2]
    pieces = refs[2 : 2 + len(plan)]
    keep_ref, send_ref, feat, acc = refs[3 + len(plan) :]
    me = lax.axis_index("blk")
    core = lax.axis_index("rep") % 2
    npair = nrep // 2
    slots, tile = tiles_ref.shape[3], tiles_ref.shape[4]
    rblk = feat.shape[1]

    acc[...] = jnp.zeros_like(acc)
    for ref, (off0, off1, rows) in zip(pieces, plan):
        off = jnp.where(core == 0, off0, off1)
        if rows is None:
            feat[off] = ref[...].reshape(feat.shape[1:])
        else:
            half = rblk // 2
            at = jnp.where(core == 0, rows[0], rows[1]) * half
            feat[off, pl.ds(at, half)] = ref[...].reshape((half,) + feat.shape[2:])

    def shard_step(off):
        shard = jnp.bitwise_xor(me, off)
        for k in range(slots):
            code = code_ref[k, shard]
            row, col = code // rblk, code % rblk
            prod = jnp.dot(tiles_ref[0, 0, shard, k], feat[off, col], preferred_element_type=jnp.float32)
            at = pl.ds(pl.multiple_of(row * tile, tile), tile)
            acc[at] = acc[at] + prod

    if nblk <= 8:
        for off in range(nblk):
            shard_step(off)
    else:
        lax.fori_loop(0, nblk, lambda s, c: (shard_step(s), c)[1], 0)

    share = rblk * tile // nrep

    def part(owner):
        return acc[pl.ds(pl.multiple_of(owner * share, share), share)]

    for p in range(npair):
        keep_ref[pl.ds(p * share, share)] = part(2 * p + core)
        send_ref[pl.ds(p * share, share)] = part(2 * p + 1 - core)


def tail_kernel(*refs):
    mine_ref, got_ref = refs[:2]
    weight_ref, bias_ref, cot_ref, out_ref, grad_ref, act = refs[2:]
    share = out_ref.shape[0]
    agg = (mine_ref[...] + got_ref[...]).astype(jnp.bfloat16)
    pre = jnp.dot(agg, weight_ref[...], preferred_element_type=jnp.float32) + bias_ref[...]
    sigma = 1.0 / (1.0 + jnp.exp(-pre))
    act[...] = pre * sigma
    pair = lax.axis_index("rep") // 2
    out_ref[...] = act[pl.ds(pl.multiple_of(pair * share, share), share)].astype(jnp.bfloat16)
    delta = cot_ref[...].astype(jnp.float32) * (sigma * (1.0 + pre * (1.0 - sigma)))
    gw = lax.dot_general(
        agg, delta.astype(jnp.bfloat16), (((0,), (0,)), ((), ())), preferred_element_type=jnp.float32
    )
    gb = jnp.sum(delta, axis=0, keepdims=True)
    feat = gw.shape[0]
    grad_ref[pl.ds(0, feat)] = gw
    grad_ref[pl.ds(feat, 8)] = jnp.broadcast_to(gb, (8, gb.shape[1]))


def last_kernel(a_ref, b_ref, gw_ref, gb_ref):
    feat = gw_ref.shape[0]
    total = a_ref[...] + b_ref[...]
    gw_ref[...] = total[:feat]
    gb_ref[...] = total[feat : feat + 1]


def fence_kernel(x_ref, *refs):
    refs[-1][...] = x_ref[...]


def fence(x, *others):
    return pl.pallas_call(
        fence_kernel,
        out_shape=jax.ShapeDtypeStruct(x.shape, x.dtype),
        in_specs=[VMEM] + [ANY] * len(others),
        out_specs=VMEM,
        compiler_params=params(),
    )(x, *others)


def params():
    return pltpu.CompilerParams(vmem_limit_bytes=LIMIT)


def shards(features, weight, bias, tiles, tile_row, tile_col, tile_live, label_mask, cotangent):
    nblk, nrep = lax.axis_size("blk"), lax.axis_size("rep")
    npair = nrep // 2
    rep = lax.axis_index("rep")
    core = rep % 2
    local, feat_dim = features.shape
    tile = tiles.shape[-1]
    rblk = local // tile
    half = local // 2
    hid = weight.shape[1]
    share = local // nrep

    def blk_swap(x, off):
        return lax.ppermute(x, "blk", [(i, i ^ off) for i in range(nblk)])

    def rep_swap(x, off):
        return lax.ppermute(x, "rep", [(i, i ^ off) for i in range(nrep)])

    def two_ways(x, off0, off1):
        return lax.ppermute(
            x,
            BOTH,
            [(b * nrep + r, (b ^ (off1 if r % 2 else off0)) * nrep + r) for b in range(nblk) for r in range(nrep)],
        )

    arrays, plan = [], []

    def add(array, off0, off1, rows=None):
        arrays.append(array)
        plan.append((off0, off1, rows))

    def stage():
        return pl.pallas_call(
            functools.partial(stage_kernel, rblk),
            out_shape=(
                jax.ShapeDtypeStruct(tiles.shape, tiles.dtype),
                jax.ShapeDtypeStruct(features.shape, features.dtype),
                jax.ShapeDtypeStruct(weight.shape, weight.dtype),
                jax.ShapeDtypeStruct((1, hid), bias.dtype),
                jax.ShapeDtypeStruct(cotangent.shape, cotangent.dtype),
                jax.ShapeDtypeStruct((tile_row.shape[3], tile_row.shape[2]), jnp.int32),
            ),
            in_specs=[HBM] * 9,
            out_specs=(VMEM,) * 6,
            scratch_shapes=[
                pltpu.VMEM((1, share), label_mask.dtype),
                pltpu.VMEM(cotangent.shape, cotangent.dtype),
                pltpu.VMEM((1, 1, tile_row.shape[3], tile_row.shape[2]), jnp.int32),
                pltpu.VMEM((1, 1, tile_row.shape[3], tile_row.shape[2]), jnp.int32),
                pltpu.VMEM(tile_live.shape, jnp.int32),
                pltpu.SemaphoreType.DMA((9,)),
            ],
            compiler_params=params(),
            cost_estimate=pl.CostEstimate(flops=0, bytes_accessed=2 * tiles.size * 2, transcendentals=0),
        )(
            tiles,
            features,
            weight,
            bias[None, :],
            label_mask[None, :],
            cotangent,
            jnp.swapaxes(tile_row, 2, 3),
            jnp.swapaxes(tile_col, 2, 3),
            tile_live,
        )

    known = [(features, 0)]
    far = nblk // 2
    while far > 4:
        known += [(blk_swap(x, far), off ^ far) for x, off in known]
        far //= 2
    for own, base in known:
        second = two_ways(own, 2, 3)
        first = two_ways(own, 4, 1)
        if base == 0:
            tiles_v, own, weight_v, bias_v, masked, code = stage()
            first = fence(first, second, masked)
        first_x = rep_swap(first, 1)
        across = jnp.where(core == 0, first, first_x)
        third = two_ways(across, 1, 2)
        fourth = blk_swap(lax.dynamic_slice_in_dim(across, core * half, half, 0), 3)
        add(own, base, base)
        second_x = rep_swap(second, 1)
        third_x = rep_swap(third, 1)
        fourth_x = rep_swap(fourth, 1)
        add(first, base ^ 4, base ^ 1)
        add(first_x, base ^ 1, base ^ 4)
        add(second, base ^ 2, base ^ 3)
        add(second_x, base ^ 3, base ^ 2)
        add(third, base ^ 5, base ^ 6)
        add(third_x, base ^ 6, base ^ 5)
        add(fourth, base ^ 7, base ^ 7, (0, 1))
        add(fourth_x, base ^ 7, base ^ 7, (1, 0))

    cots = [(masked, 0)]
    for i in range(1, npair):
        cots.append((rep_swap(masked, 2 * i), i))
    if npair == 2:
        mine, other = cots[0][0], cots[1][0]
        low = rep // 2 == 0
        cot = jnp.concatenate([jnp.where(low, mine, other), jnp.where(low, other, mine)], axis=0)
    else:
        stacked = jnp.stack([x for x, _ in cots])
        order = jnp.arange(npair, dtype=jnp.int32) ^ (rep // 2)
        cot = jnp.take(stacked, order, axis=0).reshape(npair * share, hid)

    keep, send = pl.pallas_call(
        functools.partial(spmm_kernel, nblk, nrep, tuple(plan)),
        out_shape=(jax.ShapeDtypeStruct((npair * share, feat_dim), jnp.float32),) * 2,
        in_specs=[SMEM] + [VMEM] * (1 + len(arrays)) + [ANY],
        out_specs=(VMEM,) * 2,
        scratch_shapes=[
            pltpu.VMEM((nblk, rblk, tile, feat_dim), jnp.bfloat16),
            pltpu.VMEM(((rblk + 1) * tile, feat_dim), jnp.float32),
        ],
        compiler_params=params(),
    )(code, tiles_v, *arrays, cot)

    total, got = keep, rep_swap(send, 1)
    bit = 1
    while bit < npair:
        total = total + got
        got = rep_swap(total, 2 * bit)
        bit *= 2

    output, grads = pl.pallas_call(
        tail_kernel,
        out_shape=(
            jax.ShapeDtypeStruct((share, hid), jnp.bfloat16),
            jax.ShapeDtypeStruct((feat_dim + 8, hid), jnp.float32),
        ),
        in_specs=[VMEM] * 5,
        out_specs=(VMEM,) * 2,
        scratch_shapes=[pltpu.VMEM((npair * share, hid), jnp.float32)],
        compiler_params=params(),
    )(total, got, weight_v, bias_v, cot)

    got = rep_swap(grads, 1)
    bit = 1
    while bit < nblk:
        grads = grads + got
        got = blk_swap(grads, bit)
        bit *= 2
    grad_weight, grad_bias = pl.pallas_call(
        last_kernel,
        out_shape=(
            jax.ShapeDtypeStruct((feat_dim, hid), jnp.float32),
            jax.ShapeDtypeStruct((1, hid), jnp.float32),
        ),
        in_specs=[VMEM] * 2,
        out_specs=(VMEM,) * 2,
        compiler_params=params(),
    )(grads, got)
    return output, grad_weight, grad_bias.reshape(hid)


def solution(mesh):
    placed = (
        P("blk", None),
        P(),
        P(),
        P("blk", "rep", None, None, None, None),
        P("blk", "rep", None, None),
        P("blk", "rep", None, None),
        P("blk", "rep", None),
        P(BOTH),
        P(BOTH, None),
    )
    return jax.shard_map(
        shards,
        mesh=mesh,
        in_specs=placed,
        out_specs=(P(BOTH, None), P(), P()),
        check_vma=False,
    )
```

time: 68.7 us -> 55.7 us (0.81)
  blocking collectives: 24.6 us -> 0 us
  waiting for transfers between devices: 15 us -> 26.1 us
  local copies, waits for them, and re-layouts: 5.73 us -> 4.49 us
  Pallas kernels: 2.15 us -> 3.31 us
    all_to_all x2 -> x0, blocking collectives: 24.6 us -> none  [the longest x1 14.6 us: shards(): pieces = lax.all_to_all(grads.reshape(ndev, piece, hid), both, 0, 0)]
    ppermute x16 -> x15, waiting for transfers between devices: 15 us -> 26.1 us  [the longest x8 12.4 us: rep_swap(): return lax.ppermute(x, 'rep', [(i, i ^ off) for i in range(nrep)])]
    pallas_call x2 -> x5, Pallas kernels: 2.15 us -> 3.31 us  [the longest x1 1.33 us: shards(): pl.pallas_call(functools.partial(spmm_kernel, nblk, nrep, tuple(plan)), o...]
    unnamed x18, local copies, waits for them, and re-layouts: 3.45 us -> 4.48 us
    dynamic_slice x1, local copies, waits for them, and re-layouts: 0.96 us -> 0.01 us  [shards(): fourth = blk_swap(lax.dynamic_slice_in_dim(across, core * half, half, 0), 3)]
    ppermute x16 -> x15, starting transfers between devices: 20 us -> 20.6 us  [the longest x4 9.76 us: blk_swap(): return lax.ppermute(x, 'blk', [(i, i ^ off) for i in range(nblk)])]
  transfers between devices with their start and end apart: 16 -> 15, of which waited for: 7 -> 11; matrix products, arithmetic and copies ran while one was open for 0% -> 0% of each run, Pallas kernels for 0% -> 1%
where the time goes in v2:
time: 55.7 us; the launch traced here: 55.4 us
  waiting for transfers between devices  26.1 us (47%)
  starting transfers between devices  20.6 us (37%)
  local copies, waits for them, and re-layouts  4.49 us (8%)
  Pallas kernels  3.31 us (6%)
  between operations  0.75 us (1%)
    ppermute x8, waiting for transfers between devices, rep_swap(): return lax.ppermute(x, 'rep', [(i, i ^ off) for i in range(nrep)])  12.4 us
    ppermute x4, waiting for transfers between devices, blk_swap(): return lax.ppermute(x, 'blk', [(i, i ^ off) for i in range(nblk)])  11.3 us
    ppermute x4, starting transfers between devices, blk_swap(): return lax.ppermute(x, 'blk', [(i, i ^ off) for i in range(nblk)])  9.76 us
    ppermute x3, starting transfers between devices, two_ways(): lax.ppermute(x, BOTH, [(b * nrep + r, (b ^ (off1 if r % 2 else off0)) * n...  6.89 us
    unnamed x18, local copies, waits for them, and re-layouts  4.48 us
    ppermute x8, starting transfers between devices, rep_swap(): return lax.ppermute(x, 'rep', [(i, i ^ off) for i in range(nrep)])  3.96 us
    ppermute x3, waiting for transfers between devices, two_ways(): lax.ppermute(x, BOTH, [(b * nrep + r, (b ^ (off1 if r % 2 else off0)) * n...  2.43 us
    pallas_call x1, Pallas kernels, shards(): pl.pallas_call(functools.partial(spmm_kernel, nblk, nrep, tuple(plan)), o...  1.33 us
  transfers between devices with their start and end apart: 15, of which 11 were waited for; matrix products, arithmetic and copies ran while one was open for 0% of the time, Pallas kernels for 1%

profile of v2, /device:TPU:0, one launch (start us, length us, event | category | flops | bytes accessed | tf_op | source)
XLA Modules:
  0.0 55.4 jit_solution(5515400141694103747)
XLA Ops:
  0.6 3.1 %collective-permute-start.1 = (bf16[1024,128]{1,0:T(8,128)(2,1)}, bf16[1024,128]{1,0:T(8,128)(2,1)S(1)}, u32[]{:S(2)}, u32[]{:S(2)}) collective-permute-start(bf16[1024,128]{1,0:T(8,128)(2,1)} %refs_1_.1), channel_id=1, source_target_pairs={{0,8},{1,13},{2,10},{3,15},{4,12},{5,9},{6,14},{7,11},{8,0},{9,5},... | collective-permute-start | bytes 786440 | tf_op jit(solution)/shard_map/ppermute | solution.py:147
  3.7 2.6 %collective-permute-start = (bf16[1024,128]{1,0:T(8,128)(2,1)}, bf16[1024,128]{1,0:T(8,128)(2,1)S(1)}, u32[]{:S(2)}, u32[]{:S(2)}) collective-permute-start(bf16[1024,128]{1,0:T(8,128)(2,1)} %refs_1_.1), channel_id=1, source_target_pairs={{0,16},{1,5},{2,18},{3,7},{4,20},{5,1},{6,22},{7,3},{8,24},{9,13},... | collective-permute-start | bytes 786440 | tf_op jit(solution)/shard_map/ppermute | solution.py:147
  6.3 0.0 copy-start.8
  6.3 0.0 copy-start.5
  6.3 0.0 copy-start.4
  6.3 0.0 copy-start.6
  6.3 0.0 copy-start.7
  6.3 0.6 %copy-done.8 = s32[1,1,8]{2,1,0:T(1,128)S(1)} copy-done((s32[1,1,8]{2,1,0:T(1,128)S(1)}, s32[1,1,8]{2,1,0:T(1,128)}, u32[]{:S(2)}) %copy-start.8) | copy-done | bytes 56
  7.0 0.0 copy-done.5
  7.0 0.0 copy-done.4
  7.0 0.0 copy-done.6
  7.0 0.0 copy-done.7
  7.0 1.2 %copy-done = bf16[1,1,8,4,128,128]{5,4,3,2,1,0:T(8,128)(2,1)S(1)} copy-done((bf16[1,1,8,4,128,128]{5,4,3,2,1,0:T(8,128)(2,1)S(1)}, bf16[1,1,8,4,128,128]{5,4,3,2,1,0:T(8,128)(2,1)}, u32[]{:S(2)}) %copy-start) | copy-done | bytes 1048600
  8.3 0.9 %copy-done.1 = bf16[1024,128]{1,0:T(8,128)(2,1)S(1)} copy-done((bf16[1024,128]{1,0:T(8,128)(2,1)S(1)}, bf16[1024,128]{1,0:T(8,128)(2,1)}, u32[]{:S(2)}) %copy-start.1) | copy-done | bytes 262168
  9.2 0.8 %copy-done.2 = bf16[256,128]{1,0:T(8,128)(2,1)S(1)} copy-done((bf16[256,128]{1,0:T(8,128)(2,1)S(1)}, bf16[256,128]{1,0:T(8,128)(2,1)}, u32[]{:S(2)}) %copy-start.2) | copy-done | bytes 65560
  10.1 0.8 %copy-done.3 = bf16[128,128]{1,0:T(8,128)(2,1)S(1)} copy-done((bf16[128,128]{1,0:T(8,128)(2,1)S(1)}, bf16[128,128]{1,0:T(8,128)(2,1)}, u32[]{:S(2)}) %copy-start.3) | copy-done | bytes 32792
  10.8 0.4 shard_map.112
  11.2 2.4 %collective-permute-done.1.refs_0_.refs_5_ = bf16[1024,128]{1,0:T(8,128)(2,1)S(1)} collective-permute-done((bf16[1024,128]{1,0:T(8,128)(2,1)}, bf16[1024,128]{1,0:T(8,128)(2,1)S(1)}, u32[]{:S(2)}, u32[]{:S(2)}) %collective-permute-start.1) | collective-permute-done | bytes 262176 | tf_op jit(solution)/shard_map/ppermute | solution.py:147
  13.7 0.0 collective-permute-done.x_ref
  13.7 0.1 collective-permute-start.2
  13.8 1.5 %collective-permute-done.2.refs_4_ = bf16[1024,128]{1,0:T(8,128)(2,1)S(1)} collective-permute-done((bf16[1024,128]{1,0:T(8,128)(2,1)S(1)}, bf16[1024,128]{1,0:T(8,128)(2,1)S(1)}, u32[]{:S(2)}, u32[]{:S(2)}) %collective-permute-start.2) | collective-permute-done | bytes 262176 | tf_op jit(solution)/shard_map/ppermute | solution.py:144
  15.3 1.2 %collective-permute-start.4 = (bf16[1024,128]{1,0:T(8,128)(2,1)S(1)}, bf16[1024,128]{1,0:T(8,128)(2,1)S(1)}, u32[]{:S(2)}, u32[]{:S(2)}) collective-permute-start(bf16[1024,128]{1,0:T(8,128)(2,1)S(1)} %broadcast_select_fusion), channel_id=1, source_target_pairs={{0,4},{1,9},{2,6},{3,11},{4,0},{5,13},{6,2},{7,15},{8,12},{9,1},{1... | collective-permute-start | bytes 786440 | tf_op jit(solution)/shard_map/ppermute | solution.py:147
  16.5 3.4 %collective-permute-start.6 = (bf16[512,128]{1,0:T(8,128)(2,1)S(1)}, bf16[512,128]{1,0:T(8,128)(2,1)S(1)}, u32[]{:S(2)}, u32[]{:S(2)}) collective-permute-start(bf16[512,128]{1,0:T(8,128)(2,1)S(1)} %constant_dynamic-slice_fusion), channel_id=1, source_target_pairs={{0,12},{4,8},{8,4},{12,0},{16,28},{20,24},{24,20},{28,16},{1,13},{... | collective-permute-start | bytes 393224 | tf_op jit(solution)/shard_map/ppermute | solution.py:141
  20.0 1.5 %collective-permute-start.8 = (bf16[256,128]{1,0:T(8,128)(2,1)S(1)}, bf16[256,128]{1,0:T(8,128)(2,1)S(1)}, u32[]{:S(2)}, u32[]{:S(2)}) collective-permute-start(bf16[256,128]{1,0:T(8,128)(2,1)S(1)} %get-tuple-element.18.refs_1_), channel_id=1, source_target_pairs={{0,2},{1,3},{2,0},{3,1},{4,6},{5,7},{6,4},{7,5},{8,10},{9,11},{10,... | collective-permute-start | bytes 196616 | tf_op jit(solution)/shard_map/ppermute | solution.py:144
  21.5 0.0 collective-permute-start.3
  21.5 2.9 %collective-permute-done.6.refs_9_ = bf16[512,128]{1,0:T(8,128)(2,1)S(1)} collective-permute-done((bf16[512,128]{1,0:T(8,128)(2,1)S(1)}, bf16[512,128]{1,0:T(8,128)(2,1)S(1)}, u32[]{:S(2)}, u32[]{:S(2)}) %collective-permute-start.6) | collective-permute-done | bytes 131104 | tf_op jit(solution)/shard_map/ppermute | solution.py:141
  24.4 0.4 collective-permute-start.7
  24.8 0.0 collective-permute-done.4.refs_7_
  24.9 0.1 collective-permute-start.5
  24.9 0.0 collective-permute-done.8
  25.0 0.0 collective-permute-done.3.refs_6_
  25.0 0.9 %collective-permute-done.7.refs_10_ = bf16[512,128]{1,0:T(8,128)(2,1)S(1)} collective-permute-done((bf16[512,128]{1,0:T(8,128)(2,1)S(1)}, bf16[512,128]{1,0:T(8,128)(2,1)S(1)}, u32[]{:S(2)}, u32[]{:S(2)}) %collective-permute-start.7) | collective-permute-done | bytes 131104 | tf_op jit(solution)/shard_map/ppermute | solution.py:144
  25.8 0.6 collective-permute-done.5.refs_8_
  26.4 1.3 %shard_map.114 = (f32[512,128]{1,0:T(8,128)S(1)}, f32[512,128]{1,0:T(8,128)S(1)}) custom-call(s32[4,8]{1,0:T(4,128)S(1)} %get-tuple-element.15.refs_0_, bf16[1,1,8,4,128,128]{5,4,3,2,1,0:T(8,128)(2,1)S(1)} %get-tuple-element.16.refs_1_, bf16[1024,128]{1,0:T(8,128)(2,1)S(1)} %get-tuple-element.17.refs_2_, bf16[1024,128]{1,0:T(8,128)(2,1)S(1)} %shard_map.113.refs_3_, ...), custom_call_target="tpu_custom_call" | custom-call | tf_op jit(solution)/shard_map/pallas_call | solution.py:234
  27.7 0.3 collective-permute-start.9
  28.0 1.4 %collective-permute-done.9 = f32[512,128]{1,0:T(8,128)S(1)} collective-permute-done((f32[512,128]{1,0:T(8,128)S(1)}, f32[512,128]{1,0:T(8,128)S(1)}, u32[]{:S(2)}, u32[]{:S(2)}) %collective-permute-start.9) | collective-permute-done | bytes 262176 | tf_op jit(solution)/shard_map/ppermute | solution.py:144
  29.4 1.6 %collective-permute-start.10 = (f32[512,128]{1,0:T(8,128)S(1)}, f32[512,128]{1,0:T(8,128)S(1)}, u32[]{:S(2)}, u32[]{:S(2)}) collective-permute-start(f32[512,128]{1,0:T(8,128)S(1)} %add.22.refs_0_), channel_id=1, source_target_pairs={{0,2},{1,3},{2,0},{3,1},{4,6},{5,7},{6,4},{7,5},{8,10},{9,11},{10,... | collective-permute-start | bytes 786440 | tf_op jit(solution)/shard_map/ppermute | solution.py:144
  31.0 6.9 %collective-permute-done.10.refs_1_ = f32[512,128]{1,0:T(8,128)S(1)} collective-permute-done((f32[512,128]{1,0:T(8,128)S(1)}, f32[512,128]{1,0:T(8,128)S(1)}, u32[]{:S(2)}, u32[]{:S(2)}) %collective-permute-start.10) | collective-permute-done | bytes 262176 | tf_op jit(solution)/shard_map/ppermute | solution.py:144
  37.8 0.9 %shard_map.115 = (bf16[256,128]{1,0:T(8,128)(2,1)}, f32[136,128]{1,0:T(8,128)S(1)}) custom-call(f32[512,128]{1,0:T(8,128)S(1)} %add.22.refs_0_, f32[512,128]{1,0:T(8,128)S(1)} %collective-permute-done.10.refs_1_, bf16[128,128]{1,0:T(8,128)(2,1)S(1)} %get-tuple-element.21.refs_2_, f32[1,128]{1,0:T(1,128)S(1)} %get-tuple-element.22.refs_3_, ...), custom_call_target="tpu_custom_call" | custom-call | tf_op jit(solution)/shard_map/pallas_call | solution.py:253
  38.7 0.0 collective-permute-start.11
  38.7 1.3 %collective-permute-done.11 = f32[136,128]{1,0:T(8,128)S(1)} collective-permute-done((f32[136,128]{1,0:T(8,128)S(1)}, f32[136,128]{1,0:T(8,128)S(1)}, u32[]{:S(2)}, u32[]{:S(2)}) %collective-permute-start.11) | collective-permute-done | bytes 69664 | tf_op jit(solution)/shard_map/ppermute | solution.py:144
  40.0 1.6 %collective-permute-start.12 = (f32[136,128]{1,0:T(8,128)S(1)}, f32[136,128]{1,0:T(8,128)S(1)}, u32[]{:S(2)}, u32[]{:S(2)}) collective-permute-start(f32[136,128]{1,0:T(8,128)S(1)} %add.23), channel_id=1, source_target_pairs={{0,4},{4,0},{8,12},{12,8},{16,20},{20,16},{24,28},{28,24},{1,5},{5... | collective-permute-start | bytes 208904 | tf_op jit(solution)/shard_map/ppermute | solution.py:141
  41.6 2.8 %collective-permute-done.12 = f32[136,128]{1,0:T(8,128)S(1)} collective-permute-done((f32[136,128]{1,0:T(8,128)S(1)}, f32[136,128]{1,0:T(8,128)S(1)}, u32[]{:S(2)}, u32[]{:S(2)}) %collective-permute-start.12) | collective-permute-done | bytes 69664 | tf_op jit(solution)/shard_map/ppermute | solution.py:141
  44.4 2.8 %collective-permute-start.13 = (f32[136,128]{1,0:T(8,128)S(1)}, f32[136,128]{1,0:T(8,128)S(1)}, u32[]{:S(2)}, u32[]{:S(2)}) collective-permute-start(f32[136,128]{1,0:T(8,128)S(1)} %add.24), channel_id=1, source_target_pairs={{0,8},{4,12},{8,0},{12,4},{16,24},{20,28},{24,16},{28,20},{1,9},{5... | collective-permute-start | bytes 208904 | tf_op jit(solution)/shard_map/ppermute | solution.py:141
  47.2 2.3 %collective-permute-done.13 = f32[136,128]{1,0:T(8,128)S(1)} collective-permute-done((f32[136,128]{1,0:T(8,128)S(1)}, f32[136,128]{1,0:T(8,128)S(1)}, u32[]{:S(2)}, u32[]{:S(2)}) %collective-permute-start.13) | collective-permute-done | bytes 69664 | tf_op jit(solution)/shard_map/ppermute | solution.py:141
  49.5 2.0 %collective-permute-start.14 = (f32[136,128]{1,0:T(8,128)S(1)}, f32[136,128]{1,0:T(8,128)S(1)}, u32[]{:S(2)}, u32[]{:S(2)}) collective-permute-start(f32[136,128]{1,0:T(8,128)S(1)} %add.25.a_ref), channel_id=1, source_target_pairs={{0,16},{4,20},{8,24},{12,28},{16,0},{20,4},{24,8},{28,12},{1,17},{... | collective-permute-start | bytes 208904 | tf_op jit(solution)/shard_map/ppermute | solution.py:141
  51.5 3.3 %collective-permute-done.14.b_ref = f32[136,128]{1,0:T(8,128)S(1)} collective-permute-done((f32[136,128]{1,0:T(8,128)S(1)}, f32[136,128]{1,0:T(8,128)S(1)}, u32[]{:S(2)}, u32[]{:S(2)}) %collective-permute-start.14) | collective-permute-done | bytes 69664 | tf_op jit(solution)/shard_map/ppermute | solution.py:141
  54.8 0.6 %shard_map.116 = (f32[128,128]{1,0:T(8,128)}, f32[1,128]{1,0:T(1,128)}) custom-call(f32[136,128]{1,0:T(8,128)S(1)} %add.25.a_ref, f32[136,128]{1,0:T(8,128)S(1)} %collective-permute-done.14.b_ref), custom_call_target="tpu_custom_call" | custom-call | tf_op jit(solution)/shard_map/pallas_call | solution.py:271
  (13 shorter events, 0.2 us)
Async XLA Ops:
  0.6 13.0 %collective-permute-start.1 = (bf16[1024,128]{1,0:T(8,128)(2,1)}, bf16[1024,128]{1,0:T(8,128)(2,1)S(1)}, u32[]{:S(2)}, u32[]{:S(2)}) collective-permute-start(bf16[1024,128]{1,0:T(8,128)(2,1)} %refs_1_.1), channel_id=1, source_target_pairs={{0,8},{1,13},{2,10},{3,15},{4,12},{5,9},{6,14},{7,11},{8,0},{9,5},... | collective-permute-start | bytes 786440 | tf_op jit(solution)/shard_map/ppermute | solution.py:147
  3.7 9.9 %collective-permute-start = (bf16[1024,128]{1,0:T(8,128)(2,1)}, bf16[1024,128]{1,0:T(8,128)(2,1)S(1)}, u32[]{:S(2)}, u32[]{:S(2)}) collective-permute-start(bf16[1024,128]{1,0:T(8,128)(2,1)} %refs_1_.1), channel_id=1, source_target_pairs={{0,16},{1,5},{2,18},{3,7},{4,20},{5,1},{6,22},{7,3},{8,24},{9,13},... | collective-permute-start | bytes 786440 | tf_op jit(solution)/shard_map/ppermute | solution.py:147
  6.3 0.7 %copy-start.8 = (s32[1,1,8]{2,1,0:T(1,128)S(1)}, s32[1,1,8]{2,1,0:T(1,128)}, u32[]{:S(2)}) copy-start(s32[1,1,8]{2,1,0:T(1,128)} %refs_8_.1) | copy-start | bytes 100
  6.3 0.7 %copy-start.5 = (s32[1,1,8,4]{2,3,1,0:T(4,128)S(1)}, s32[1,1,8,4]{2,3,1,0:T(4,128)}, u32[]{:S(2)}) copy-start(s32[1,1,8,4]{2,3,1,0:T(4,128)} %param.14) | copy-start | bytes 388
  6.3 0.7 %copy-start.4 = (s32[1,1,8,4]{2,3,1,0:T(4,128)S(1)}, s32[1,1,8,4]{2,3,1,0:T(4,128)}, u32[]{:S(2)}) copy-start(s32[1,1,8,4]{2,3,1,0:T(4,128)} %param.13) | copy-start | bytes 388
  6.3 0.7 %copy-start.6 = (s32[256]{0:T(256)S(1)}, s32[256]{0:T(256)}, u32[]{:S(2)}) copy-start(s32[256]{0:T(256)} %param.16) | copy-start | bytes 3076
  6.3 0.7 %copy-start.7 = (f32[128]{0:T(128)S(1)}, f32[128]{0:T(128)}, u32[]{:S(2)}) copy-start(f32[128]{0:T(128)} %param.11) | copy-start | bytes 1540
  7.0 1.2 %copy-start = (bf16[1,1,8,4,128,128]{5,4,3,2,1,0:T(8,128)(2,1)S(1)}, bf16[1,1,8,4,128,128]{5,4,3,2,1,0:T(8,128)(2,1)}, u32[]{:S(2)}) copy-start(bf16[1,1,8,4,128,128]{5,4,3,2,1,0:T(8,128)(2,1)} %refs_0_.1) | copy-start | bytes 3145732
  8.3 0.9 %copy-start.1 = (bf16[1024,128]{1,0:T(8,128)(2,1)S(1)}, bf16[1024,128]{1,0:T(8,128)(2,1)}, u32[]{:S(2)}) copy-start(bf16[1024,128]{1,0:T(8,128)(2,1)} %refs_1_.1) | copy-start | bytes 786436
  9.2 0.8 %copy-start.2 = (bf16[256,128]{1,0:T(8,128)(2,1)S(1)}, bf16[256,128]{1,0:T(8,128)(2,1)}, u32[]{:S(2)}) copy-start(bf16[256,128]{1,0:T(8,128)(2,1)} %refs_5_.1) | copy-start | bytes 196612
  10.1 0.8 %copy-start.3 = (bf16[128,128]{1,0:T(8,128)(2,1)S(1)}, bf16[128,128]{1,0:T(8,128)(2,1)}, u32[]{:S(2)}) copy-start(bf16[128,128]{1,0:T(8,128)(2,1)} %refs_2_.1) | copy-start | bytes 98308
  13.7 1.6 %collective-permute-start.2 = (bf16[1024,128]{1,0:T(8,128)(2,1)S(1)}, bf16[1024,128]{1,0:T(8,128)(2,1)S(1)}, u32[]{:S(2)}, u32[]{:S(2)}) collective-permute-start(bf16[1024,128]{1,0:T(8,128)(2,1)S(1)} %shard_map.113.refs_3_), channel_id=1, source_target_pairs={{0,1},{1,0},{2,3},{3,2},{4,5},{5,4},{6,7},{7,6},{8,9},{9,8},{10,11... | collective-permute-start | bytes 786440 | tf_op jit(solution)/shard_map/ppermute | solution.py:144
  15.3 9.5 %collective-permute-start.4 = (bf16[1024,128]{1,0:T(8,128)(2,1)S(1)}, bf16[1024,128]{1,0:T(8,128)(2,1)S(1)}, u32[]{:S(2)}, u32[]{:S(2)}) collective-permute-start(bf16[1024,128]{1,0:T(8,128)(2,1)S(1)} %broadcast_select_fusion), channel_id=1, source_target_pairs={{0,4},{1,9},{2,6},{3,11},{4,0},{5,13},{6,2},{7,15},{8,12},{9,1},{1... | collective-permute-start | bytes 786440 | tf_op jit(solution)/shard_map/ppermute | solution.py:147
  16.5 7.9 %collective-permute-start.6 = (bf16[512,128]{1,0:T(8,128)(2,1)S(1)}, bf16[512,128]{1,0:T(8,128)(2,1)S(1)}, u32[]{:S(2)}, u32[]{:S(2)}) collective-permute-start(bf16[512,128]{1,0:T(8,128)(2,1)S(1)} %constant_dynamic-slice_fusion), channel_id=1, source_target_pairs={{0,12},{4,8},{8,4},{12,0},{16,28},{20,24},{24,20},{28,16},{1,13},{... | collective-permute-start | bytes 393224 | tf_op jit(solution)/shard_map/ppermute | solution.py:141
  20.0 4.9 %collective-permute-start.8 = (bf16[256,128]{1,0:T(8,128)(2,1)S(1)}, bf16[256,128]{1,0:T(8,128)(2,1)S(1)}, u32[]{:S(2)}, u32[]{:S(2)}) collective-permute-start(bf16[256,128]{1,0:T(8,128)(2,1)S(1)} %get-tuple-element.18.refs_1_), channel_id=1, source_target_pairs={{0,2},{1,3},{2,0},{3,1},{4,6},{5,7},{6,4},{7,5},{8,10},{9,11},{10,... | collective-permute-start | bytes 196616 | tf_op jit(solution)/shard_map/ppermute | solution.py:144
  21.5 3.5 %collective-permute-start.3 = (bf16[1024,128]{1,0:T(8,128)(2,1)S(1)}, bf16[1024,128]{1,0:T(8,128)(2,1)S(1)}, u32[]{:S(2)}, u32[]{:S(2)}) collective-permute-start(bf16[1024,128]{1,0:T(8,128)(2,1)S(1)} %collective-permute-done.1.refs_0_.refs_5_), channel_id=1, source_target_pairs={{0,1},{1,0},{2,3},{3,2},{4,5},{5,4},{6,7},{7,6},{8,9},{9,8},{10,11... | collective-permute-start | bytes 786440 | tf_op jit(solution)/shard_map/ppermute | solution.py:144
  24.4 1.4 %collective-permute-start.7 = (bf16[512,128]{1,0:T(8,128)(2,1)S(1)}, bf16[512,128]{1,0:T(8,128)(2,1)S(1)}, u32[]{:S(2)}, u32[]{:S(2)}) collective-permute-start(bf16[512,128]{1,0:T(8,128)(2,1)S(1)} %collective-permute-done.6.refs_9_), channel_id=1, source_target_pairs={{0,1},{1,0},{2,3},{3,2},{4,5},{5,4},{6,7},{7,6},{8,9},{9,8},{10,11... | collective-permute-start | bytes 393224 | tf_op jit(solution)/shard_map/ppermute | solution.py:144
  24.9 1.5 %collective-permute-start.5 = (bf16[1024,128]{1,0:T(8,128)(2,1)S(1)}, bf16[1024,128]{1,0:T(8,128)(2,1)S(1)}, u32[]{:S(2)}, u32[]{:S(2)}) collective-permute-start(bf16[1024,128]{1,0:T(8,128)(2,1)S(1)} %collective-permute-done.4.refs_7_), channel_id=1, source_target_pairs={{0,1},{1,0},{2,3},{3,2},{4,5},{5,4},{6,7},{7,6},{8,9},{9,8},{10,11... | collective-permute-start | bytes 786440 | tf_op jit(solution)/shard_map/ppermute | solution.py:144
  27.7 1.6 %collective-permute-start.9 = (f32[512,128]{1,0:T(8,128)S(1)}, f32[512,128]{1,0:T(8,128)S(1)}, u32[]{:S(2)}, u32[]{:S(2)}) collective-permute-start(f32[512,128]{1,0:T(8,128)S(1)} %get-tuple-element.20), channel_id=1, source_target_pairs={{0,1},{1,0},{2,3},{3,2},{4,5},{5,4},{6,7},{7,6},{8,9},{9,8},{10,11... | collective-permute-start | bytes 786440 | tf_op jit(solution)/shard_map/ppermute | solution.py:144
  29.4 8.5 %collective-permute-start.10 = (f32[512,128]{1,0:T(8,128)S(1)}, f32[512,128]{1,0:T(8,128)S(1)}, u32[]{:S(2)}, u32[]{:S(2)}) collective-permute-start(f32[512,128]{1,0:T(8,128)S(1)} %add.22.refs_0_), channel_id=1, source_target_pairs={{0,2},{1,3},{2,0},{3,1},{4,6},{5,7},{6,4},{7,5},{8,10},{9,11},{10,... | collective-permute-start | bytes 786440 | tf_op jit(solution)/shard_map/ppermute | solution.py:144
  38.7 1.3 %collective-permute-start.11 = (f32[136,128]{1,0:T(8,128)S(1)}, f32[136,128]{1,0:T(8,128)S(1)}, u32[]{:S(2)}, u32[]{:S(2)}) collective-permute-start(f32[136,128]{1,0:T(8,128)S(1)} %get-tuple-element.24), channel_id=1, source_target_pairs={{0,1},{1,0},{2,3},{3,2},{4,5},{5,4},{6,7},{7,6},{8,9},{9,8},{10,11... | collective-permute-start | bytes 208904 | tf_op jit(solution)/shard_map/ppermute | solution.py:144
  40.0 4.4 %collective-permute-start.12 = (f32[136,128]{1,0:T(8,128)S(1)}, f32[136,128]{1,0:T(8,128)S(1)}, u32[]{:S(2)}, u32[]{:S(2)}) collective-permute-start(f32[136,128]{1,0:T(8,128)S(1)} %add.23), channel_id=1, source_target_pairs={{0,4},{4,0},{8,12},{12,8},{16,20},{20,16},{24,28},{28,24},{1,5},{5... | collective-permute-start | bytes 208904 | tf_op jit(solution)/shard_map/ppermute | solution.py:141
  44.4 5.1 %collective-permute-start.13 = (f32[136,128]{1,0:T(8,128)S(1)}, f32[136,128]{1,0:T(8,128)S(1)}, u32[]{:S(2)}, u32[]{:S(2)}) collective-permute-start(f32[136,128]{1,0:T(8,128)S(1)} %add.24), channel_id=1, source_target_pairs={{0,8},{4,12},{8,0},{12,4},{16,24},{20,28},{24,16},{28,20},{1,9},{5... | collective-permute-start | bytes 208904 | tf_op jit(solution)/shard_map/ppermute | solution.py:141
  49.5 5.3 %collective-permute-start.14 = (f32[136,128]{1,0:T(8,128)S(1)}, f32[136,128]{1,0:T(8,128)S(1)}, u32[]{:S(2)}, u32[]{:S(2)}) collective-permute-start(f32[136,128]{1,0:T(8,128)S(1)} %add.25.a_ref), channel_id=1, source_target_pairs={{0,16},{4,20},{8,24},{12,28},{16,0},{20,4},{24,8},{28,12},{1,17},{... | collective-permute-start | bytes 208904 | tf_op jit(solution)/shard_map/ppermute | solution.py:141

commit v3 on v2

--- a/solution.py
+++ b/solution.py
@@ -46,14 +46,8 @@
     rblk = feat.shape[1]
 
     acc[...] = jnp.zeros_like(acc)
-    for ref, (off0, off1, rows) in zip(pieces, plan):
-        off = jnp.where(core == 0, off0, off1)
-        if rows is None:
-            feat[off] = ref[...].reshape(feat.shape[1:])
-        else:
-            half = rblk // 2
-            at = jnp.where(core == 0, rows[0], rows[1]) * half
-            feat[off, pl.ds(at, half)] = ref[...].reshape((half,) + feat.shape[2:])
+    for ref, (off0, off1) in zip(pieces, plan):
+        feat[jnp.where(core == 0, off0, off1)] = ref[...].reshape(feat.shape[1:])
 
     def shard_step(off):
         shard = jnp.bitwise_xor(me, off)
@@ -81,10 +75,9 @@
 
 
 def tail_kernel(*refs):
-    mine_ref, got_ref = refs[:2]
-    weight_ref, bias_ref, cot_ref, out_ref, grad_ref, act = refs[2:]
+    agg_ref, weight_ref, bias_ref, cot_ref, out_ref, keep_ref, send_ref, act, grad = refs
     share = out_ref.shape[0]
-    agg = (mine_ref[...] + got_ref[...]).astype(jnp.bfloat16)
+    agg = agg_ref[...]
     pre = jnp.dot(agg, weight_ref[...], preferred_element_type=jnp.float32) + bias_ref[...]
     sigma = 1.0 / (1.0 + jnp.exp(-pre))
     act[...] = pre * sigma
@@ -95,16 +88,20 @@
         agg, delta.astype(jnp.bfloat16), (((0,), (0,)), ((), ())), preferred_element_type=jnp.float32
     )
     gb = jnp.sum(delta, axis=0, keepdims=True)
-    feat = gw.shape[0]
-    grad_ref[pl.ds(0, feat)] = gw
-    grad_ref[pl.ds(feat, 8)] = jnp.broadcast_to(gb, (8, gb.shape[1]))
-
-
-def last_kernel(a_ref, b_ref, gw_ref, gb_ref):
-    feat = gw_ref.shape[0]
-    total = a_ref[...] + b_ref[...]
-    gw_ref[...] = total[:feat]
-    gb_ref[...] = total[feat : feat + 1]
+    half = gw.shape[0] // 2
+    core = lax.axis_index("rep") % 2
+    grad[...] = gw
+    for ref, which in ((keep_ref, core), (send_ref, 1 - core)):
+        ref[pl.ds(0, half)] = grad[pl.ds(pl.multiple_of(which * half, half), half)]
+        ref[pl.ds(half, 8)] = jnp.broadcast_to(gb, (8, gb.shape[1]))
+
+
+def last_kernel(mine_ref, other_ref, gw_ref, gb_ref):
+    half = gw_ref.shape[0] // 2
+    core = lax.axis_index("rep") % 2
+    gw_ref[pl.ds(pl.multiple_of(core * half, half), half)] = mine_ref[pl.ds(0, half)]
+    gw_ref[pl.ds(pl.multiple_of((1 - core) * half, half), half)] = other_ref[pl.ds(0, half)]
+    gb_ref[...] = mine_ref[pl.ds(half, 1)]
 
 
 def fence_kernel(x_ref, *refs):
@@ -130,6 +127,7 @@
     npair = nrep // 2
     rep = lax.axis_index("rep")
     core = rep % 2
+    side = (rep // 2) % 2
     local, feat_dim = features.shape
     tile = tiles.shape[-1]
     rblk = local // tile
@@ -150,11 +148,18 @@
             [(b * nrep + r, (b ^ (off1 if r % 2 else off0)) * nrep + r) for b in range(nblk) for r in range(nrep)],
         )
 
+    def one_core(x, axis, off, which):
+        if axis == "blk":
+            return lax.ppermute(
+                x, BOTH, [(b * nrep + r, (b ^ off) * nrep + r) for b in range(nblk) for r in range(which, nrep, 2)]
+            )
+        return lax.ppermute(x, "rep", [(r, r ^ off) for r in range(which, nrep, 2)])
+
     arrays, plan = [], []
 
-    def add(array, off0, off1, rows=None):
+    def add(array, off0, off1):
         arrays.append(array)
-        plan.append((off0, off1, rows))
+        plan.append((off0, off1))
 
     def stage():
         return pl.pallas_call(
@@ -197,37 +202,40 @@
         known += [(blk_swap(x, far), off ^ far) for x, off in known]
         far //= 2
     for own, base in known:
-        second = two_ways(own, 2, 3)
         first = two_ways(own, 4, 1)
+        own_half = lax.dynamic_slice_in_dim(own, side * half, half, 0)
+        second = two_ways(own_half, 3, 2)
+        packed = second
         if base == 0:
             tiles_v, own, weight_v, bias_v, masked, code = stage()
             first = fence(first, second, masked)
+            packed = jnp.concatenate([second, masked], axis=0)
         first_x = rep_swap(first, 1)
+        third = one_core(first, "blk", 3, 0)
         across = jnp.where(core == 0, first, first_x)
-        third = two_ways(across, 1, 2)
-        fourth = blk_swap(lax.dynamic_slice_in_dim(across, core * half, half, 0), 3)
+        fourth = two_ways(across, 2, 1)
+        packed_y = rep_swap(fence(packed, across), 2)
+        if base == 0:
+            other = packed_y[half:]
+        second_y = packed_y[:half]
+        low = side == 0
+        near = jnp.concatenate([jnp.where(low, second, second_y), jnp.where(low, second_y, second)], axis=0)
+        near_x = rep_swap(near, 1)
+        third_x = one_core(third, "rep", 1, 0)
+        fourth_x = rep_swap(fourth, 1)
         add(own, base, base)
-        second_x = rep_swap(second, 1)
-        third_x = rep_swap(third, 1)
-        fourth_x = rep_swap(fourth, 1)
         add(first, base ^ 4, base ^ 1)
         add(first_x, base ^ 1, base ^ 4)
-        add(second, base ^ 2, base ^ 3)
-        add(second_x, base ^ 3, base ^ 2)
-        add(third, base ^ 5, base ^ 6)
-        add(third_x, base ^ 6, base ^ 5)
-        add(fourth, base ^ 7, base ^ 7, (0, 1))
-        add(fourth_x, base ^ 7, base ^ 7, (1, 0))
-
-    cots = [(masked, 0)]
-    for i in range(1, npair):
-        cots.append((rep_swap(masked, 2 * i), i))
+        add(near, base ^ 3, base ^ 2)
+        add(near_x, base ^ 2, base ^ 3)
+        add(jnp.where(core == 0, third, third_x), base ^ 7, base ^ 7)
+        add(fourth, base ^ 6, base ^ 5)
+        add(fourth_x, base ^ 5, base ^ 6)
+
     if npair == 2:
-        mine, other = cots[0][0], cots[1][0]
-        low = rep // 2 == 0
-        cot = jnp.concatenate([jnp.where(low, mine, other), jnp.where(low, other, mine)], axis=0)
+        cot = jnp.concatenate([jnp.where(side == 0, masked, other), jnp.where(side == 0, other, masked)], axis=0)
     else:
-        stacked = jnp.stack([x for x, _ in cots])
+        stacked = jnp.stack([masked] + [rep_swap(masked, 2 * i) for i in range(1, npair)])
         order = jnp.arange(npair, dtype=jnp.int32) ^ (rep // 2)
         cot = jnp.take(stacked, order, axis=0).reshape(npair * share, hid)
 
@@ -244,29 +252,38 @@
     )(code, tiles_v, *arrays, cot)
 
     total, got = keep, rep_swap(send, 1)
-    bit = 1
-    while bit < npair:
-        total = total + got
-        got = rep_swap(total, 2 * bit)
-        bit *= 2
-
-    output, grads = pl.pallas_call(
+    total = total + got
+    if npair == 2:
+        sent = lax.optimization_barrier((4.0 * total).astype(jnp.float16))
+        total = sent.astype(jnp.float32) + rep_swap(sent, 2).astype(jnp.float32)
+        total = (0.25 * total).astype(jnp.bfloat16)
+    else:
+        bit = 1
+        while bit < npair:
+            total = total + rep_swap(total, 2 * bit)
+            bit *= 2
+        total = total.astype(jnp.bfloat16)
+
+    output, grads, send = pl.pallas_call(
         tail_kernel,
         out_shape=(
             jax.ShapeDtypeStruct((share, hid), jnp.bfloat16),
-            jax.ShapeDtypeStruct((feat_dim + 8, hid), jnp.float32),
+            jax.ShapeDtypeStruct((feat_dim // 2 + 8, hid), jnp.float32),
+            jax.ShapeDtypeStruct((feat_dim // 2 + 8, hid), jnp.float32),
         ),
-        in_specs=[VMEM] * 5,
-        out_specs=(VMEM,) * 2,
-        scratch_shapes=[pltpu.VMEM((npair * share, hid), jnp.float32)],
+        in_specs=[VMEM] * 4,
+        out_specs=(VMEM,) * 3,
+        scratch_shapes=[
+            pltpu.VMEM((npair * share, hid), jnp.float32),
+            pltpu.VMEM((feat_dim, hid), jnp.float32),
+        ],
         compiler_params=params(),
-    )(total, got, weight_v, bias_v, cot)
-
-    got = rep_swap(grads, 1)
+    )(total, weight_v, bias_v, cot)
+
+    grads = grads + rep_swap(send, 1)
     bit = 1
     while bit < nblk:
-        grads = grads + got
-        got = blk_swap(grads, bit)
+        grads = grads + blk_swap(grads, bit)
         bit *= 2
     grad_weight, grad_bias = pl.pallas_call(
         last_kernel,
@@ -277,7 +294,7 @@
         in_specs=[VMEM] * 2,
         out_specs=(VMEM,) * 2,
         compiler_params=params(),
-    )(grads, got)
+    )(grads, rep_swap(grads, 1))
     return output, grad_weight, grad_bias.reshape(hid)
 
 

time: 55.7 us -> 52.3 us (0.939)
  waiting for transfers between devices: 26.1 us -> 23.3 us
  local copies, waits for them, and re-layouts: 4.49 us -> 3.65 us
    ppermute x0 -> x2, starting transfers between devices: none -> 5.83 us  [the longest x1 4.54 us: one_core(): lax.ppermute(x, BOTH, [(b * nrep + r, (b ^ off) * nrep + r) for b in rang...]
    ppermute x4 -> x3, starting transfers between devices: 9.76 us -> 4.19 us  [blk_swap(): return lax.ppermute(x, 'blk', [(i, i ^ off) for i in range(nblk)])]
    ppermute x8, waiting for transfers between devices: 12.4 us -> 9.49 us  [rep_swap(): return lax.ppermute(x, 'rep', [(i, i ^ off) for i in range(nrep)])]
    ppermute x4 -> x3, waiting for transfers between devices: 11.3 us -> 8.58 us  [blk_swap(): return lax.ppermute(x, 'blk', [(i, i ^ off) for i in range(nblk)])]
    ppermute x0 -> x2, waiting for transfers between devices: none -> 2.4 us  [the longest x1 2.4 us: one_core(): lax.ppermute(x, BOTH, [(b * nrep + r, (b ^ off) * nrep + r) for b in rang...]
    unnamed x18, local copies, waits for them, and re-layouts: 4.48 us -> 2.67 us
    dynamic_slice x1, local copies, waits for them, and re-layouts: 0.01 us -> 0.98 us  [shards(): own_half = lax.dynamic_slice_in_dim(own, side * half, half, 0)]
    ppermute x8, starting transfers between devices: 3.96 us -> 3.33 us  [rep_swap(): return lax.ppermute(x, 'rep', [(i, i ^ off) for i in range(nrep)])]
  transfers between devices with their start and end apart: 15 -> 16, of which waited for: 11 -> 11; matrix products, arithmetic and copies ran while one was open for 0% -> 2% of each run, Pallas kernels for 1% -> 1%
where the time goes in v3:
time: 52.3 us; the launch traced here: 52 us
  waiting for transfers between devices  23.3 us (45%)
  starting transfers between devices  20.7 us (40%)
  local copies, waits for them, and re-layouts  3.65 us (7%)
  Pallas kernels  3.32 us (6%)
  between operations  0.86 us (2%)
    ppermute x8, waiting for transfers between devices, rep_swap(): return lax.ppermute(x, 'rep', [(i, i ^ off) for i in range(nrep)])  9.49 us
    ppermute x3, waiting for transfers between devices, blk_swap(): return lax.ppermute(x, 'blk', [(i, i ^ off) for i in range(nblk)])  8.58 us
    ppermute x3, starting transfers between devices, two_ways(): lax.ppermute(x, BOTH, [(b * nrep + r, (b ^ (off1 if r % 2 else off0)) * n...  7.34 us
    ppermute x1, starting transfers between devices, one_core(): lax.ppermute(x, BOTH, [(b * nrep + r, (b ^ off) * nrep + r) for b in rang...  4.54 us
    ppermute x3, starting transfers between devices, blk_swap(): return lax.ppermute(x, 'blk', [(i, i ^ off) for i in range(nblk)])  4.19 us
    ppermute x8, starting transfers between devices, rep_swap(): return lax.ppermute(x, 'rep', [(i, i ^ off) for i in range(nrep)])  3.33 us
    ppermute x3, waiting for transfers between devices, two_ways(): lax.ppermute(x, BOTH, [(b * nrep + r, (b ^ (off1 if r % 2 else off0)) * n...  2.77 us
    unnamed x18, local copies, waits for them, and re-layouts  2.67 us
  transfers between devices with their start and end apart: 16, of which 11 were waited for; matrix products, arithmetic and copies ran while one was open for 2% of the time, Pallas kernels for 1%

profile of v3, /device:TPU:0, one launch (start us, length us, event | category | flops | bytes accessed | tf_op | source)
XLA Modules:
  0.0 52.0 jit_solution(15327418775995251174)
XLA Ops:
  0.6 0.0 copy-start.1
  0.6 4.1 %collective-permute-start = (bf16[1024,128]{1,0:T(8,128)(2,1)}, bf16[1024,128]{1,0:T(8,128)(2,1)S(1)}, u32[]{:S(2)}, u32[]{:S(2)}) collective-permute-start(bf16[1024,128]{1,0:T(8,128)(2,1)} %refs_1_.1), channel_id=1, source_target_pairs={{0,16},{1,5},{2,18},{3,7},{4,20},{5,1},{6,22},{7,3},{8,24},{9,13},... | collective-permute-start | bytes 786440 | tf_op jit(solution)/shard_map/ppermute | solution.py:145
  4.7 0.0 copy-start.2
  4.7 1.0 %constant_dynamic-slice_fusion = bf16[512,128]{1,0:T(8,128)(2,1)S(1)} fusion(bf16[1024,128]{1,0:T(8,128)(2,1)} %refs_1_.1, s32[]{:T(128)S(6)} %select_n.56), kind=kLoop, calls=%fused_computation.11 | loop fusion | bytes 262148 | tf_op jit(solution)/shard_map/dynamic_slice | solution.py:206
  5.7 2.6 %collective-permute-start.1 = (bf16[512,128]{1,0:T(8,128)(2,1)S(1)}, bf16[512,128]{1,0:T(8,128)(2,1)S(1)}, u32[]{:S(2)}, u32[]{:S(2)}) collective-permute-start(bf16[512,128]{1,0:T(8,128)(2,1)S(1)} %constant_dynamic-slice_fusion), channel_id=1, source_target_pairs={{0,12},{1,9},{2,14},{3,11},{4,8},{5,13},{6,10},{7,15},{8,4},{9,1},... | collective-permute-start | bytes 393224 | tf_op jit(solution)/shard_map/ppermute | solution.py:145
  8.3 0.0 copy-done.1
  8.3 0.0 copy-done.2
  8.3 0.0 copy-done.8
  8.3 0.6 %copy-done.5 = s32[1,1,8,4]{2,3,1,0:T(4,128)S(1)} copy-done((s32[1,1,8,4]{2,3,1,0:T(4,128)S(1)}, s32[1,1,8,4]{2,3,1,0:T(4,128)}, u32[]{:S(2)}) %copy-start.5) | copy-done | bytes 152
  9.0 0.0 copy-done.4
  9.0 0.0 copy-done.6
  9.0 0.0 copy-done.7
  9.0 1.2 %copy-done = bf16[1,1,8,4,128,128]{5,4,3,2,1,0:T(8,128)(2,1)S(1)} copy-done((bf16[1,1,8,4,128,128]{5,4,3,2,1,0:T(8,128)(2,1)S(1)}, bf16[1,1,8,4,128,128]{5,4,3,2,1,0:T(8,128)(2,1)}, u32[]{:S(2)}) %copy-start) | copy-done | bytes 1048600
  10.2 0.8 %copy-done.3 = bf16[128,128]{1,0:T(8,128)(2,1)S(1)} copy-done((bf16[128,128]{1,0:T(8,128)(2,1)S(1)}, bf16[128,128]{1,0:T(8,128)(2,1)}, u32[]{:S(2)}) %copy-start.3) | copy-done | bytes 32792
  11.0 0.4 shard_map.112
  11.4 0.9 %collective-permute-done.1.refs_0_ = bf16[512,128]{1,0:T(8,128)(2,1)S(1)} collective-permute-done((bf16[512,128]{1,0:T(8,128)(2,1)S(1)}, bf16[512,128]{1,0:T(8,128)(2,1)S(1)}, u32[]{:S(2)}, u32[]{:S(2)}) %collective-permute-start.1) | collective-permute-done | bytes 131104 | tf_op jit(solution)/shard_map/ppermute | solution.py:145
  12.4 0.0 collective-permute-done.x_ref
  12.4 0.1 collective-permute-start.2
  12.5 4.5 %collective-permute-start.5 = (bf16[1024,128]{1,0:T(8,128)(2,1)S(1)}, bf16[1024,128]{1,0:T(8,128)(2,1)S(1)}, u32[]{:S(2)}, u32[]{:S(2)}) collective-permute-start(bf16[1024,128]{1,0:T(8,128)(2,1)S(1)} %shard_map.113.refs_3_), channel_id=1, source_target_pairs={{0,12},{2,14},{4,8},{6,10},{8,4},{10,6},{12,0},{14,2},{16,28},{18,... | collective-permute-start | bytes 786440 | tf_op jit(solution)/shard_map/ppermute | solution.py:153
  17.0 0.0 collective-permute-done.2.refs_4_
  17.1 1.6 %collective-permute-start.3 = (bf16[768,128]{1,0:T(8,128)(2,1)S(1)}, bf16[768,128]{1,0:T(8,128)(2,1)S(1)}, u32[]{:S(2)}, u32[]{:S(2)}) collective-permute-start(bf16[768,128]{1,0:T(8,128)(2,1)S(1)} %shard_map.114), channel_id=1, source_target_pairs={{0,2},{1,3},{2,0},{3,1},{4,6},{5,7},{6,4},{7,5},{8,10},{9,11},{10,... | collective-permute-start | bytes 589832 | tf_op jit(solution)/shard_map/ppermute | solution.py:142
  18.7 0.7 %collective-permute-start.7 = (bf16[1024,128]{1,0:T(8,128)(2,1)S(1)}, bf16[1024,128]{1,0:T(8,128)(2,1)S(1)}, u32[]{:S(2)}, u32[]{:S(2)}) collective-permute-start(bf16[1024,128]{1,0:T(8,128)(2,1)S(1)} %broadcast_select_fusion.1.refs_0_), channel_id=1, source_target_pairs={{0,8},{1,5},{2,10},{3,7},{4,12},{5,1},{6,14},{7,3},{8,0},{9,13},{1... | collective-permute-start | bytes 786440 | tf_op jit(solution)/shard_map/ppermute | solution.py:145
  19.4 2.4 %collective-permute-done.5 = bf16[1024,128]{1,0:T(8,128)(2,1)S(1)} collective-permute-done((bf16[1024,128]{1,0:T(8,128)(2,1)S(1)}, bf16[1024,128]{1,0:T(8,128)(2,1)S(1)}, u32[]{:S(2)}, u32[]{:S(2)}) %collective-permute-start.5) | collective-permute-done | bytes 262176 | tf_op jit(solution)/shard_map/ppermute | solution.py:153
  21.8 1.3 %collective-permute-start.6 = (bf16[1024,128]{1,0:T(8,128)(2,1)S(1)}, bf16[1024,128]{1,0:T(8,128)(2,1)S(1)}, u32[]{:S(2)}, u32[]{:S(2)}) collective-permute-start(bf16[1024,128]{1,0:T(8,128)(2,1)S(1)} %collective-permute-done.5), channel_id=1, source_target_pairs={{0,1},{2,3},{4,5},{6,7},{8,9},{10,11},{12,13},{14,15},{16,17},{18,... | collective-permute-start | bytes 786440 | tf_op jit(solution)/shard_map/ppermute | solution.py:156
  23.1 0.0 collective-permute-done.3
  23.1 0.1 collective-permute-start.4
  23.2 1.8 %collective-permute-done.7.refs_8_ = bf16[1024,128]{1,0:T(8,128)(2,1)S(1)} collective-permute-done((bf16[1024,128]{1,0:T(8,128)(2,1)S(1)}, bf16[1024,128]{1,0:T(8,128)(2,1)S(1)}, u32[]{:S(2)}, u32[]{:S(2)}) %collective-permute-start.7) | collective-permute-done | bytes 262176 | tf_op jit(solution)/shard_map/ppermute | solution.py:145
  25.1 0.0 collective-permute-start.8
  25.1 0.0 collective-permute-done.6
  25.1 0.0 collective-permute-done.4.refs_6_
  25.1 1.5 %collective-permute-done.8.refs_9_ = bf16[1024,128]{1,0:T(8,128)(2,1)S(1)} collective-permute-done((bf16[1024,128]{1,0:T(8,128)(2,1)S(1)}, bf16[1024,128]{1,0:T(8,128)(2,1)S(1)}, u32[]{:S(2)}, u32[]{:S(2)}) %collective-permute-start.8) | collective-permute-done | bytes 262176 | tf_op jit(solution)/shard_map/ppermute | solution.py:142
  26.6 1.3 %shard_map.115 = (f32[512,128]{1,0:T(8,128)S(1)}, f32[512,128]{1,0:T(8,128)S(1)}) custom-call(s32[4,8]{1,0:T(4,128)S(1)} %get-tuple-element.16.refs_0_, bf16[1,1,8,4,128,128]{5,4,3,2,1,0:T(8,128)(2,1)S(1)} %get-tuple-element.17.refs_1_, bf16[1024,128]{1,0:T(8,128)(2,1)S(1)} %get-tuple-element.18.refs_2_, bf16[1024,128]{1,0:T(8,128)(2,1)S(1)} %shard_map.113.refs_3_, ...), custom_call_target="tpu_custom_call" | custom-call | tf_op jit(solution)/shard_map/pallas_call | solution.py:242
  27.9 0.2 collective-permute-start.9
  28.1 1.4 %collective-permute-done.9 = f32[512,128]{1,0:T(8,128)S(1)} collective-permute-done((f32[512,128]{1,0:T(8,128)S(1)}, f32[512,128]{1,0:T(8,128)S(1)}, u32[]{:S(2)}, u32[]{:S(2)}) %collective-permute-start.9) | collective-permute-done | bytes 262176 | tf_op jit(solution)/shard_map/ppermute | solution.py:142
  29.6 1.4 %collective-permute-start.10 = (f16[512,128]{1,0:T(8,128)(2,1)S(1)}, f16[512,128]{1,0:T(8,128)(2,1)S(1)}, u32[]{:S(2)}, u32[]{:S(2)}) collective-permute-start(f16[512,128]{1,0:T(8,128)(2,1)S(1)} %multiply_convert_fusion.1), channel_id=1, source_target_pairs={{0,2},{1,3},{2,0},{3,1},{4,6},{5,7},{6,4},{7,5},{8,10},{9,11},{10,... | collective-permute-start | bytes 393224 | tf_op jit(solution)/shard_map/ppermute | solution.py:142
  31.0 4.2 %collective-permute-done.10 = f16[512,128]{1,0:T(8,128)(2,1)S(1)} collective-permute-done((f16[512,128]{1,0:T(8,128)(2,1)S(1)}, f16[512,128]{1,0:T(8,128)(2,1)S(1)}, u32[]{:S(2)}, u32[]{:S(2)}) %collective-permute-start.10) | collective-permute-done | bytes 131104 | tf_op jit(solution)/shard_map/ppermute | solution.py:142
  35.2 0.9 %shard_map.116 = (bf16[256,128]{1,0:T(8,128)(2,1)}, f32[72,128]{1,0:T(8,128)S(1)}, f32[72,128]{1,0:T(8,128)S(1)}) custom-call(bf16[512,128]{1,0:T(8,128)(2,1)S(1)} %multiply_convert_fusion.refs_0_, bf16[128,128]{1,0:T(8,128)(2,1)S(1)} %get-tuple-element.22.refs_1_, f32[1,128]{1,0:T(1,128)S(1)} %get-tuple-element.23.refs_2_, ...), custom_call_target="tpu_custom_call" | custom-call | tf_op jit(solution)/shard_map/pallas_call | solution.py:267
  36.2 0.0 collective-permute-start.11
  36.2 1.2 %collective-permute-done.11 = f32[72,128]{1,0:T(8,128)S(1)} collective-permute-done((f32[72,128]{1,0:T(8,128)S(1)}, f32[72,128]{1,0:T(8,128)S(1)}, u32[]{:S(2)}, u32[]{:S(2)}) %collective-permute-start.11) | collective-permute-done | bytes 36896 | tf_op jit(solution)/shard_map/ppermute | solution.py:142
  37.4 0.5 %collective-permute-start.12 = (f32[72,128]{1,0:T(8,128)S(1)}, f32[72,128]{1,0:T(8,128)S(1)}, u32[]{:S(2)}, u32[]{:S(2)}) collective-permute-start(f32[72,128]{1,0:T(8,128)S(1)} %add.34), channel_id=1, source_target_pairs={{0,4},{4,0},{8,12},{12,8},{16,20},{20,16},{24,28},{28,24},{1,5},{5... | collective-permute-start | bytes 110600 | tf_op jit(solution)/shard_map/ppermute | solution.py:139
  37.9 3.4 %collective-permute-done.12 = f32[72,128]{1,0:T(8,128)S(1)} collective-permute-done((f32[72,128]{1,0:T(8,128)S(1)}, f32[72,128]{1,0:T(8,128)S(1)}, u32[]{:S(2)}, u32[]{:S(2)}) %collective-permute-start.12) | collective-permute-done | bytes 36896 | tf_op jit(solution)/shard_map/ppermute | solution.py:139
  41.3 1.2 %collective-permute-start.13 = (f32[72,128]{1,0:T(8,128)S(1)}, f32[72,128]{1,0:T(8,128)S(1)}, u32[]{:S(2)}, u32[]{:S(2)}) collective-permute-start(f32[72,128]{1,0:T(8,128)S(1)} %add.35), channel_id=1, source_target_pairs={{0,8},{4,12},{8,0},{12,4},{16,24},{20,28},{24,16},{28,20},{1,9},{5... | collective-permute-start | bytes 110600 | tf_op jit(solution)/shard_map/ppermute | solution.py:139
  42.5 2.8 %collective-permute-done.13 = f32[72,128]{1,0:T(8,128)S(1)} collective-permute-done((f32[72,128]{1,0:T(8,128)S(1)}, f32[72,128]{1,0:T(8,128)S(1)}, u32[]{:S(2)}, u32[]{:S(2)}) %collective-permute-start.13) | collective-permute-done | bytes 36896 | tf_op jit(solution)/shard_map/ppermute | solution.py:139
  45.3 2.5 %collective-permute-start.14 = (f32[72,128]{1,0:T(8,128)S(1)}, f32[72,128]{1,0:T(8,128)S(1)}, u32[]{:S(2)}, u32[]{:S(2)}) collective-permute-start(f32[72,128]{1,0:T(8,128)S(1)} %add.36), channel_id=1, source_target_pairs={{0,16},{4,20},{8,24},{12,28},{16,0},{20,4},{24,8},{28,12},{1,17},{... | collective-permute-start | bytes 110600 | tf_op jit(solution)/shard_map/ppermute | solution.py:139
  47.8 2.4 %collective-permute-done.14 = f32[72,128]{1,0:T(8,128)S(1)} collective-permute-done((f32[72,128]{1,0:T(8,128)S(1)}, f32[72,128]{1,0:T(8,128)S(1)}, u32[]{:S(2)}, u32[]{:S(2)}) %collective-permute-start.14) | collective-permute-done | bytes 36896 | tf_op jit(solution)/shard_map/ppermute | solution.py:139
  50.2 0.0 collective-permute-start.15
  50.2 1.2 %collective-permute-done.15.other_ref = f32[72,128]{1,0:T(8,128)S(1)} collective-permute-done((f32[72,128]{1,0:T(8,128)S(1)}, f32[72,128]{1,0:T(8,128)S(1)}, u32[]{:S(2)}, u32[]{:S(2)}) %collective-permute-start.15) | collective-permute-done | bytes 36896 | tf_op jit(solution)/shard_map/ppermute | solution.py:142
  51.4 0.6 %shard_map.117 = (f32[128,128]{1,0:T(8,128)}, f32[1,128]{1,0:T(1,128)}) custom-call(f32[72,128]{1,0:T(8,128)S(1)} %add.37.mine_ref, f32[72,128]{1,0:T(8,128)S(1)} %collective-permute-done.15.other_ref), custom_call_target="tpu_custom_call" | custom-call | tf_op jit(solution)/shard_map/pallas_call | solution.py:288
  (22 shorter events, 0.3 us)
Async XLA Ops:
  0.6 7.7 %copy-start.1 = (bf16[1024,128]{1,0:T(8,128)(2,1)S(1)}, bf16[1024,128]{1,0:T(8,128)(2,1)}, u32[]{:S(2)}) copy-start(bf16[1024,128]{1,0:T(8,128)(2,1)} %refs_1_.1) | copy-start | bytes 786436
  0.6 11.7 %collective-permute-start = (bf16[1024,128]{1,0:T(8,128)(2,1)}, bf16[1024,128]{1,0:T(8,128)(2,1)S(1)}, u32[]{:S(2)}, u32[]{:S(2)}) collective-permute-start(bf16[1024,128]{1,0:T(8,128)(2,1)} %refs_1_.1), channel_id=1, source_target_pairs={{0,16},{1,5},{2,18},{3,7},{4,20},{5,1},{6,22},{7,3},{8,24},{9,13},... | collective-permute-start | bytes 786440 | tf_op jit(solution)/shard_map/ppermute | solution.py:145
  4.7 3.6 %copy-start.2 = (bf16[256,128]{1,0:T(8,128)(2,1)S(1)}, bf16[256,128]{1,0:T(8,128)(2,1)}, u32[]{:S(2)}) copy-start(bf16[256,128]{1,0:T(8,128)(2,1)} %refs_5_.1) | copy-start | bytes 196612
  4.7 3.6 %copy-start.8 = (s32[1,1,8]{2,1,0:T(1,128)S(1)}, s32[1,1,8]{2,1,0:T(1,128)}, u32[]{:S(2)}) copy-start(s32[1,1,8]{2,1,0:T(1,128)} %refs_8_.1) | copy-start | bytes 100
  5.7 6.6 %collective-permute-start.1 = (bf16[512,128]{1,0:T(8,128)(2,1)S(1)}, bf16[512,128]{1,0:T(8,128)(2,1)S(1)}, u32[]{:S(2)}, u32[]{:S(2)}) collective-permute-start(bf16[512,128]{1,0:T(8,128)(2,1)S(1)} %constant_dynamic-slice_fusion), channel_id=1, source_target_pairs={{0,12},{1,9},{2,14},{3,11},{4,8},{5,13},{6,10},{7,15},{8,4},{9,1},... | collective-permute-start | bytes 393224 | tf_op jit(solution)/shard_map/ppermute | solution.py:145
  8.3 0.7 %copy-start.5 = (s32[1,1,8,4]{2,3,1,0:T(4,128)S(1)}, s32[1,1,8,4]{2,3,1,0:T(4,128)}, u32[]{:S(2)}) copy-start(s32[1,1,8,4]{2,3,1,0:T(4,128)} %param.14) | copy-start | bytes 388
  8.3 0.7 %copy-start.4 = (s32[1,1,8,4]{2,3,1,0:T(4,128)S(1)}, s32[1,1,8,4]{2,3,1,0:T(4,128)}, u32[]{:S(2)}) copy-start(s32[1,1,8,4]{2,3,1,0:T(4,128)} %param.13) | copy-start | bytes 388
  8.3 0.7 %copy-start.6 = (s32[256]{0:T(256)S(1)}, s32[256]{0:T(256)}, u32[]{:S(2)}) copy-start(s32[256]{0:T(256)} %param.16) | copy-start | bytes 3076
  8.3 0.7 %copy-start.7 = (f32[128]{0:T(128)S(1)}, f32[128]{0:T(128)}, u32[]{:S(2)}) copy-start(f32[128]{0:T(128)} %param.11) | copy-start | bytes 1540
  9.0 1.2 %copy-start = (bf16[1,1,8,4,128,128]{5,4,3,2,1,0:T(8,128)(2,1)S(1)}, bf16[1,1,8,4,128,128]{5,4,3,2,1,0:T(8,128)(2,1)}, u32[]{:S(2)}) copy-start(bf16[1,1,8,4,128,128]{5,4,3,2,1,0:T(8,128)(2,1)} %refs_0_.1) | copy-start | bytes 3145732
  10.2 0.8 %copy-start.3 = (bf16[128,128]{1,0:T(8,128)(2,1)S(1)}, bf16[128,128]{1,0:T(8,128)(2,1)}, u32[]{:S(2)}) copy-start(bf16[128,128]{1,0:T(8,128)(2,1)} %refs_2_.1) | copy-start | bytes 98308
  12.4 4.7 %collective-permute-start.2 = (bf16[1024,128]{1,0:T(8,128)(2,1)S(1)}, bf16[1024,128]{1,0:T(8,128)(2,1)S(1)}, u32[]{:S(2)}, u32[]{:S(2)}) collective-permute-start(bf16[1024,128]{1,0:T(8,128)(2,1)S(1)} %shard_map.113.refs_3_), channel_id=1, source_target_pairs={{0,1},{1,0},{2,3},{3,2},{4,5},{5,4},{6,7},{7,6},{8,9},{9,8},{10,11... | collective-permute-start | bytes 786440 | tf_op jit(solution)/shard_map/ppermute | solution.py:142
  12.5 9.3 %collective-permute-start.5 = (bf16[1024,128]{1,0:T(8,128)(2,1)S(1)}, bf16[1024,128]{1,0:T(8,128)(2,1)S(1)}, u32[]{:S(2)}, u32[]{:S(2)}) collective-permute-start(bf16[1024,128]{1,0:T(8,128)(2,1)S(1)} %shard_map.113.refs_3_), channel_id=1, source_target_pairs={{0,12},{2,14},{4,8},{6,10},{8,4},{10,6},{12,0},{14,2},{16,28},{18,... | collective-permute-start | bytes 786440 | tf_op jit(solution)/shard_map/ppermute | solution.py:153
  17.1 6.0 %collective-permute-start.3 = (bf16[768,128]{1,0:T(8,128)(2,1)S(1)}, bf16[768,128]{1,0:T(8,128)(2,1)S(1)}, u32[]{:S(2)}, u32[]{:S(2)}) collective-permute-start(bf16[768,128]{1,0:T(8,128)(2,1)S(1)} %shard_map.114), channel_id=1, source_target_pairs={{0,2},{1,3},{2,0},{3,1},{4,6},{5,7},{6,4},{7,5},{8,10},{9,11},{10,... | collective-permute-start | bytes 589832 | tf_op jit(solution)/shard_map/ppermute | solution.py:142
  18.7 6.4 %collective-permute-start.7 = (bf16[1024,128]{1,0:T(8,128)(2,1)S(1)}, bf16[1024,128]{1,0:T(8,128)(2,1)S(1)}, u32[]{:S(2)}, u32[]{:S(2)}) collective-permute-start(bf16[1024,128]{1,0:T(8,128)(2,1)S(1)} %broadcast_select_fusion.1.refs_0_), channel_id=1, source_target_pairs={{0,8},{1,5},{2,10},{3,7},{4,12},{5,1},{6,14},{7,3},{8,0},{9,13},{1... | collective-permute-start | bytes 786440 | tf_op jit(solution)/shard_map/ppermute | solution.py:145
  21.8 3.3 %collective-permute-start.6 = (bf16[1024,128]{1,0:T(8,128)(2,1)S(1)}, bf16[1024,128]{1,0:T(8,128)(2,1)S(1)}, u32[]{:S(2)}, u32[]{:S(2)}) collective-permute-start(bf16[1024,128]{1,0:T(8,128)(2,1)S(1)} %collective-permute-done.5), channel_id=1, source_target_pairs={{0,1},{2,3},{4,5},{6,7},{8,9},{10,11},{12,13},{14,15},{16,17},{18,... | collective-permute-start | bytes 786440 | tf_op jit(solution)/shard_map/ppermute | solution.py:156
  23.1 2.0 %collective-permute-start.4 = (bf16[1024,128]{1,0:T(8,128)(2,1)S(1)}, bf16[1024,128]{1,0:T(8,128)(2,1)S(1)}, u32[]{:S(2)}, u32[]{:S(2)}) collective-permute-start(bf16[1024,128]{1,0:T(8,128)(2,1)S(1)} %pad_maximum_fusion.refs_5_), channel_id=1, source_target_pairs={{0,1},{1,0},{2,3},{3,2},{4,5},{5,4},{6,7},{7,6},{8,9},{9,8},{10,11... | collective-permute-start | bytes 786440 | tf_op jit(solution)/shard_map/ppermute | solution.py:142
  25.1 1.5 %collective-permute-start.8 = (bf16[1024,128]{1,0:T(8,128)(2,1)S(1)}, bf16[1024,128]{1,0:T(8,128)(2,1)S(1)}, u32[]{:S(2)}, u32[]{:S(2)}) collective-permute-start(bf16[1024,128]{1,0:T(8,128)(2,1)S(1)} %collective-permute-done.7.refs_8_), channel_id=1, source_target_pairs={{0,1},{1,0},{2,3},{3,2},{4,5},{5,4},{6,7},{7,6},{8,9},{9,8},{10,11... | collective-permute-start | bytes 786440 | tf_op jit(solution)/shard_map/ppermute | solution.py:142
  27.9 1.6 %collective-permute-start.9 = (f32[512,128]{1,0:T(8,128)S(1)}, f32[512,128]{1,0:T(8,128)S(1)}, u32[]{:S(2)}, u32[]{:S(2)}) collective-permute-start(f32[512,128]{1,0:T(8,128)S(1)} %get-tuple-element.21), channel_id=1, source_target_pairs={{0,1},{1,0},{2,3},{3,2},{4,5},{5,4},{6,7},{7,6},{8,9},{9,8},{10,11... | collective-permute-start | bytes 786440 | tf_op jit(solution)/shard_map/ppermute | solution.py:142
  29.6 5.6 %collective-permute-start.10 = (f16[512,128]{1,0:T(8,128)(2,1)S(1)}, f16[512,128]{1,0:T(8,128)(2,1)S(1)}, u32[]{:S(2)}, u32[]{:S(2)}) collective-permute-start(f16[512,128]{1,0:T(8,128)(2,1)S(1)} %multiply_convert_fusion.1), channel_id=1, source_target_pairs={{0,2},{1,3},{2,0},{3,1},{4,6},{5,7},{6,4},{7,5},{8,10},{9,11},{10,... | collective-permute-start | bytes 393224 | tf_op jit(solution)/shard_map/ppermute | solution.py:142
  36.2 1.2 %collective-permute-start.11 = (f32[72,128]{1,0:T(8,128)S(1)}, f32[72,128]{1,0:T(8,128)S(1)}, u32[]{:S(2)}, u32[]{:S(2)}) collective-permute-start(f32[72,128]{1,0:T(8,128)S(1)} %get-tuple-element.26), channel_id=1, source_target_pairs={{0,1},{1,0},{2,3},{3,2},{4,5},{5,4},{6,7},{7,6},{8,9},{9,8},{10,11... | collective-permute-start | bytes 110600 | tf_op jit(solution)/shard_map/ppermute | solution.py:142
  37.4 4.0 %collective-permute-start.12 = (f32[72,128]{1,0:T(8,128)S(1)}, f32[72,128]{1,0:T(8,128)S(1)}, u32[]{:S(2)}, u32[]{:S(2)}) collective-permute-start(f32[72,128]{1,0:T(8,128)S(1)} %add.34), channel_id=1, source_target_pairs={{0,4},{4,0},{8,12},{12,8},{16,20},{20,16},{24,28},{28,24},{1,5},{5... | collective-permute-start | bytes 110600 | tf_op jit(solution)/shard_map/ppermute | solution.py:139
  41.3 4.0 %collective-permute-start.13 = (f32[72,128]{1,0:T(8,128)S(1)}, f32[72,128]{1,0:T(8,128)S(1)}, u32[]{:S(2)}, u32[]{:S(2)}) collective-permute-start(f32[72,128]{1,0:T(8,128)S(1)} %add.35), channel_id=1, source_target_pairs={{0,8},{4,12},{8,0},{12,4},{16,24},{20,28},{24,16},{28,20},{1,9},{5... | collective-permute-start | bytes 110600 | tf_op jit(solution)/shard_map/ppermute | solution.py:139
  45.3 4.9 %collective-permute-start.14 = (f32[72,128]{1,0:T(8,128)S(1)}, f32[72,128]{1,0:T(8,128)S(1)}, u32[]{:S(2)}, u32[]{:S(2)}) collective-permute-start(f32[72,128]{1,0:T(8,128)S(1)} %add.36), channel_id=1, source_target_pairs={{0,16},{4,20},{8,24},{12,28},{16,0},{20,4},{24,8},{28,12},{1,17},{... | collective-permute-start | bytes 110600 | tf_op jit(solution)/shard_map/ppermute | solution.py:139
  50.2 1.2 %collective-permute-start.15 = (f32[72,128]{1,0:T(8,128)S(1)}, f32[72,128]{1,0:T(8,128)S(1)}, u32[]{:S(2)}, u32[]{:S(2)}) collective-permute-start(f32[72,128]{1,0:T(8,128)S(1)} %add.37.mine_ref), channel_id=1, source_target_pairs={{0,1},{1,0},{2,3},{3,2},{4,5},{5,4},{6,7},{7,6},{8,9},{9,8},{10,11... | collective-permute-start | bytes 110600 | tf_op jit(solution)/shard_map/ppermute | solution.py:142

commit v4 on v3

--- a/solution.py
+++ b/solution.py
@@ -15,14 +15,24 @@
 BOTH = ("blk", "rep")
 
 
-def stage_kernel(rblk, *refs):
-    sources, targets = refs[:9], refs[9:13] + refs[15:20]
-    masked_ref, code_ref, sems = refs[13], refs[14], refs[20]
-    mask_ref, cot_ref, row_ref, col_ref, live_ref = targets[4:]
+def shard_of(which, plan, j):
+    return jnp.bitwise_xor(lax.axis_index("blk"), jnp.where(which == 0, plan[j][0], plan[j][1]))
+
+
+def stage_kernel(rblk, plan, *refs):
+    tiles_in, keep_ref, send_ref = refs[0], refs[8], refs[9]
+    sources, targets = refs[1:8], refs[10:12] + refs[14:19]
+    masked_ref, code_ref, tile_sems, sems = refs[12], refs[13], refs[19], refs[20]
+    mask_ref, cot_ref, row_ref, col_ref, live_ref = targets[2:]
     copies = [pltpu.make_async_copy(x, y, sems.at[i]) for i, (x, y) in enumerate(zip(sources, targets))]
-    for copy in reversed(copies):
+    core = lax.axis_index("rep") % 2
+    for j in range(len(plan)):
+        for i, (which, ref) in enumerate(((core, keep_ref), (1 - core, send_ref))):
+            shard = shard_of(which, plan, j)
+            copies.append(pltpu.make_async_copy(tiles_in.at[0, 0, shard], ref.at[j], tile_sems.at[2 * j + i]))
+    for copy in copies:
         copy.start()
-    for copy in copies[4:]:
+    for copy in copies[2:7]:
         copy.wait()
     share = cot_ref.shape[0]
     eye = lax.broadcasted_iota(jnp.int32, (share, share), 0) == lax.broadcasted_iota(jnp.int32, (share, share), 1)
@@ -31,38 +41,29 @@
     slot = lax.broadcasted_iota(jnp.int32, code_ref.shape, 0)
     row = jnp.where(slot < live_ref[0], row_ref[0, 0], rblk)
     code_ref[...] = row * rblk + col_ref[0, 0]
-    for copy in copies[:4]:
+    for copy in copies[:2] + copies[7:]:
         copy.wait()
 
 
-def spmm_kernel(nblk, nrep, plan, *refs):
-    code_ref, tiles_ref = refs[:2]
-    pieces = refs[2 : 2 + len(plan)]
-    keep_ref, send_ref, feat, acc = refs[3 + len(plan) :]
-    me = lax.axis_index("blk")
+def spmm_kernel(nrep, rblk, plan, *refs):
+    codes, tiles = refs[:2], refs[2:4]
+    pieces = refs[4 : 4 + len(plan)]
+    keep_ref, send_ref, acc = refs[5 + len(plan) :]
     core = lax.axis_index("rep") % 2
     npair = nrep // 2
-    slots, tile = tiles_ref.shape[3], tiles_ref.shape[4]
-    rblk = feat.shape[1]
+    slots, tile = tiles[0].shape[1], tiles[0].shape[2]
 
     acc[...] = jnp.zeros_like(acc)
-    for ref, (off0, off1) in zip(pieces, plan):
-        feat[jnp.where(core == 0, off0, off1)] = ref[...].reshape(feat.shape[1:])
-
-    def shard_step(off):
-        shard = jnp.bitwise_xor(me, off)
-        for k in range(slots):
-            code = code_ref[k, shard]
-            row, col = code // rblk, code % rblk
-            prod = jnp.dot(tiles_ref[0, 0, shard, k], feat[off, col], preferred_element_type=jnp.float32)
-            at = pl.ds(pl.multiple_of(row * tile, tile), tile)
-            acc[at] = acc[at] + prod
-
-    if nblk <= 8:
-        for off in range(nblk):
-            shard_step(off)
-    else:
-        lax.fori_loop(0, nblk, lambda s, c: (shard_step(s), c)[1], 0)
+    for j, piece in enumerate(pieces):
+        shard = shard_of(core, plan, j)
+        for code_ref, tiles_ref in zip(codes, tiles):
+            for k in range(slots):
+                code = code_ref[k, shard]
+                row, col = code // rblk, code % rblk
+                block = piece[pl.ds(pl.multiple_of(col * tile, tile), tile)]
+                prod = jnp.dot(tiles_ref[j, k], block, preferred_element_type=jnp.float32)
+                at = pl.ds(pl.multiple_of(row * tile, tile), tile)
+                acc[at] = acc[at] + prod
 
     share = rblk * tile // nrep
 
@@ -75,14 +76,11 @@
 
 
 def tail_kernel(*refs):
-    agg_ref, weight_ref, bias_ref, cot_ref, out_ref, keep_ref, send_ref, act, grad = refs
-    share = out_ref.shape[0]
+    agg_ref, weight_ref, bias_ref, cot_ref, act_ref, keep_ref, send_ref, grad = refs
     agg = agg_ref[...]
     pre = jnp.dot(agg, weight_ref[...], preferred_element_type=jnp.float32) + bias_ref[...]
     sigma = 1.0 / (1.0 + jnp.exp(-pre))
-    act[...] = pre * sigma
-    pair = lax.axis_index("rep") // 2
-    out_ref[...] = act[pl.ds(pl.multiple_of(pair * share, share), share)].astype(jnp.bfloat16)
+    act_ref[...] = pre * sigma
     delta = cot_ref[...].astype(jnp.float32) * (sigma * (1.0 + pre * (1.0 - sigma)))
     gw = lax.dot_general(
         agg, delta.astype(jnp.bfloat16), (((0,), (0,)), ((), ())), preferred_element_type=jnp.float32
@@ -155,24 +153,19 @@
             )
         return lax.ppermute(x, "rep", [(r, r ^ off) for r in range(which, nrep, 2)])
 
-    arrays, plan = [], []
-
-    def add(array, off0, off1):
-        arrays.append(array)
-        plan.append((off0, off1))
-
-    def stage():
+    def stage(plan):
+        dealt = (len(plan),) + tiles.shape[3:]
         return pl.pallas_call(
-            functools.partial(stage_kernel, rblk),
+            functools.partial(stage_kernel, rblk, plan),
             out_shape=(
-                jax.ShapeDtypeStruct(tiles.shape, tiles.dtype),
-                jax.ShapeDtypeStruct(features.shape, features.dtype),
+                jax.ShapeDtypeStruct(dealt, tiles.dtype),
+                jax.ShapeDtypeStruct(dealt, tiles.dtype),
                 jax.ShapeDtypeStruct(weight.shape, weight.dtype),
                 jax.ShapeDtypeStruct((1, hid), bias.dtype),
                 jax.ShapeDtypeStruct(cotangent.shape, cotangent.dtype),
                 jax.ShapeDtypeStruct((tile_row.shape[3], tile_row.shape[2]), jnp.int32),
             ),
-            in_specs=[HBM] * 9,
+            in_specs=[HBM] * 8,
             out_specs=(VMEM,) * 6,
             scratch_shapes=[
                 pltpu.VMEM((1, share), label_mask.dtype),
@@ -180,13 +173,13 @@
                 pltpu.VMEM((1, 1, tile_row.shape[3], tile_row.shape[2]), jnp.int32),
                 pltpu.VMEM((1, 1, tile_row.shape[3], tile_row.shape[2]), jnp.int32),
                 pltpu.VMEM(tile_live.shape, jnp.int32),
-                pltpu.SemaphoreType.DMA((9,)),
+                pltpu.SemaphoreType.DMA((2 * len(plan),)),
+                pltpu.SemaphoreType.DMA((7,)),
             ],
             compiler_params=params(),
             cost_estimate=pl.CostEstimate(flops=0, bytes_accessed=2 * tiles.size * 2, transcendentals=0),
         )(
             tiles,
-            features,
             weight,
             bias[None, :],
             label_mask[None, :],
@@ -201,13 +194,20 @@
     while far > 4:
         known += [(blk_swap(x, far), off ^ far) for x, off in known]
         far //= 2
+    plan = tuple(
+        pair
+        for _, base in known
+        for pair in ((base ^ 4, base ^ 1), (base ^ 3, base ^ 2), (base ^ 7, base), (base ^ 6, base ^ 5))
+    )
+    pieces = []
+    low = side == 0
     for own, base in known:
         first = two_ways(own, 4, 1)
         own_half = lax.dynamic_slice_in_dim(own, side * half, half, 0)
         second = two_ways(own_half, 3, 2)
         packed = second
         if base == 0:
-            tiles_v, own, weight_v, bias_v, masked, code = stage()
+            tiles_keep, tiles_send, weight_v, bias_v, masked, code = stage(plan)
             first = fence(first, second, masked)
             packed = jnp.concatenate([second, masked], axis=0)
         first_x = rep_swap(first, 1)
@@ -216,22 +216,11 @@
         fourth = two_ways(across, 2, 1)
         packed_y = rep_swap(fence(packed, across), 2)
         if base == 0:
+            tiles_x, code_x = rep_swap(fence(tiles_send, across), 1), rep_swap(fence(code, across), 1)
             other = packed_y[half:]
         second_y = packed_y[:half]
-        low = side == 0
         near = jnp.concatenate([jnp.where(low, second, second_y), jnp.where(low, second_y, second)], axis=0)
-        near_x = rep_swap(near, 1)
-        third_x = one_core(third, "rep", 1, 0)
-        fourth_x = rep_swap(fourth, 1)
-        add(own, base, base)
-        add(first, base ^ 4, base ^ 1)
-        add(first_x, base ^ 1, base ^ 4)
-        add(near, base ^ 3, base ^ 2)
-        add(near_x, base ^ 2, base ^ 3)
-        add(jnp.where(core == 0, third, third_x), base ^ 7, base ^ 7)
-        add(fourth, base ^ 6, base ^ 5)
-        add(fourth_x, base ^ 5, base ^ 6)
-
+        pieces += [first, near, jnp.where(core == 0, third, own), fourth]
     if npair == 2:
         cot = jnp.concatenate([jnp.where(side == 0, masked, other), jnp.where(side == 0, other, masked)], axis=0)
     else:
@@ -240,16 +229,13 @@
         cot = jnp.take(stacked, order, axis=0).reshape(npair * share, hid)
 
     keep, send = pl.pallas_call(
-        functools.partial(spmm_kernel, nblk, nrep, tuple(plan)),
+        functools.partial(spmm_kernel, nrep, rblk, plan),
         out_shape=(jax.ShapeDtypeStruct((npair * share, feat_dim), jnp.float32),) * 2,
-        in_specs=[SMEM] + [VMEM] * (1 + len(arrays)) + [ANY],
+        in_specs=[SMEM] * 2 + [VMEM] * (2 + len(pieces)) + [ANY],
         out_specs=(VMEM,) * 2,
-        scratch_shapes=[
-            pltpu.VMEM((nblk, rblk, tile, feat_dim), jnp.bfloat16),
-            pltpu.VMEM(((rblk + 1) * tile, feat_dim), jnp.float32),
-        ],
+        scratch_shapes=[pltpu.VMEM(((rblk + 1) * tile, feat_dim), jnp.float32)],
         compiler_params=params(),
-    )(code, tiles_v, *arrays, cot)
+    )(code, code_x, tiles_keep, tiles_x, *pieces, cot)
 
     total, got = keep, rep_swap(send, 1)
     total = total + got
@@ -264,22 +250,20 @@
             bit *= 2
         total = total.astype(jnp.bfloat16)
 
-    output, grads, send = pl.pallas_call(
+    act, grads, send = pl.pallas_call(
         tail_kernel,
         out_shape=(
-            jax.ShapeDtypeStruct((share, hid), jnp.bfloat16),
+            jax.ShapeDtypeStruct((npair * share, hid), jnp.float32),
             jax.ShapeDtypeStruct((feat_dim // 2 + 8, hid), jnp.float32),
             jax.ShapeDtypeStruct((feat_dim // 2 + 8, hid), jnp.float32),
         ),
         in_specs=[VMEM] * 4,
         out_specs=(VMEM,) * 3,
-        scratch_shapes=[
-            pltpu.VMEM((npair * share, hid), jnp.float32),
-            pltpu.VMEM((feat_dim, hid), jnp.float32),
-        ],
+        scratch_shapes=[pltpu.VMEM((feat_dim, hid), jnp.float32)],
         compiler_params=params(),
     )(total, weight_v, bias_v, cot)
 
+    output = lax.dynamic_slice_in_dim(act, rep // 2 * share, share, 0).astype(jnp.bfloat16)
     grads = grads + rep_swap(send, 1)
     bit = 1
     while bit < nblk:

time: 52.3 us -> 49.7 us (0.950)
  waiting for transfers between devices: 23.3 us -> 20.6 us
  Pallas kernels: 3.32 us -> 3.99 us
    ppermute x1 -> x0, starting transfers between devices: 1.29 us -> none  [one_core(): return lax.ppermute(x, 'rep', [(r, r ^ off) for r in range(which, nrep, 2)])]
    ppermute x3, waiting for transfers between devices: 2.77 us -> 1.56 us  [two_ways(): lax.ppermute(x, BOTH, [(b * nrep + r, (b ^ (off1 if r % 2 else off0)) * n...]
    ppermute x8, starting transfers between devices: 3.33 us -> 4.39 us  [rep_swap(): return lax.ppermute(x, 'rep', [(i, i ^ off) for i in range(nrep)])]
    ppermute x8, waiting for transfers between devices: 9.49 us -> 8.66 us  [rep_swap(): return lax.ppermute(x, 'rep', [(i, i ^ off) for i in range(nrep)])]
    unnamed x18, local copies, waits for them, and re-layouts: 2.67 us -> 1.92 us
    ppermute x1, waiting for transfers between devices: 2.4 us -> 1.69 us  [one_core(): lax.ppermute(x, BOTH, [(b * nrep + r, (b ^ off) * nrep + r) for b in rang...]
    convert_element_type x0 -> x1, local copies, waits for them, and re-layouts: none -> 0.65 us  [shards(): lax.dynamic_slice_in_dim(act, rep // 2 * share, share, 0)]
    pallas_call x3, Pallas kernels: 2.65 us -> 3.29 us  [the longest x1 1.73 us: stage(): pl.pallas_call(functools.partial(stage_kernel, rblk, plan), out_shape=(ja...]
  transfers between devices with their start and end apart: 16 -> 15, of which waited for: 11 -> 11; matrix products, arithmetic and copies ran while one was open for 2% -> 4% of each run, Pallas kernels for 1% -> 4%
where the time goes in v4:
time: 49.7 us; the launch traced here: 49.5 us
  waiting for transfers between devices  20.6 us (41%)
  starting transfers between devices  20.2 us (41%)
  Pallas kernels  3.99 us (8%)
  local copies, waits for them, and re-layouts  3.54 us (7%)
  between operations  0.85 us (2%)
    ppermute x3, waiting for transfers between devices, blk_swap(): return lax.ppermute(x, 'blk', [(i, i ^ off) for i in range(nblk)])  8.72 us
    ppermute x8, waiting for transfers between devices, rep_swap(): return lax.ppermute(x, 'rep', [(i, i ^ off) for i in range(nrep)])  8.66 us
    ppermute x3, starting transfers between devices, two_ways(): lax.ppermute(x, BOTH, [(b * nrep + r, (b ^ (off1 if r % 2 else off0)) * n...  7.19 us
    ppermute x1, starting transfers between devices, one_core(): lax.ppermute(x, BOTH, [(b * nrep + r, (b ^ off) * nrep + r) for b in rang...  4.54 us
    ppermute x8, starting transfers between devices, rep_swap(): return lax.ppermute(x, 'rep', [(i, i ^ off) for i in range(nrep)])  4.39 us
    ppermute x3, starting transfers between devices, blk_swap(): return lax.ppermute(x, 'blk', [(i, i ^ off) for i in range(nblk)])  4.05 us
    unnamed x18, local copies, waits for them, and re-layouts  1.92 us
    pallas_call x1, Pallas kernels, stage(): pl.pallas_call(functools.partial(stage_kernel, rblk, plan), out_shape=(ja...  1.73 us
  transfers between devices with their start and end apart: 15, of which 11 were waited for; matrix products, arithmetic and copies ran while one was open for 4% of the time, Pallas kernels for 4%

profile of v4, /device:TPU:0, one launch (start us, length us, event | category | flops | bytes accessed | tf_op | source)
XLA Modules:
  0.0 49.5 jit_solution(11294599232144297925)
XLA Ops:
  0.6 4.1 %collective-permute-start = (bf16[1024,128]{1,0:T(8,128)(2,1)}, bf16[1024,128]{1,0:T(8,128)(2,1)S(1)}, u32[]{:S(2)}, u32[]{:S(2)}) collective-permute-start(bf16[1024,128]{1,0:T(8,128)(2,1)} %param.9), channel_id=1, source_target_pairs={{0,16},{1,5},{2,18},{3,7},{4,20},{5,1},{6,22},{7,3},{8,24},{9,13},... | collective-permute-start | bytes 786440 | tf_op jit(solution)/shard_map/ppermute | solution.py:143
  4.7 0.0 copy-start.1
  4.7 0.0 copy-start.2
  4.7 1.0 %constant_dynamic-slice_fusion = bf16[512,128]{1,0:T(8,128)(2,1)S(1)} fusion(bf16[1024,128]{1,0:T(8,128)(2,1)} %param.9, s32[]{:T(128)S(6)} %select_n.62), kind=kLoop, calls=%fused_computation.12 | loop fusion | bytes 262148 | tf_op jit(solution)/shard_map/dynamic_slice | solution.py:206
  5.7 2.6 %collective-permute-start.1 = (bf16[512,128]{1,0:T(8,128)(2,1)S(1)}, bf16[512,128]{1,0:T(8,128)(2,1)S(1)}, u32[]{:S(2)}, u32[]{:S(2)}) collective-permute-start(bf16[512,128]{1,0:T(8,128)(2,1)S(1)} %constant_dynamic-slice_fusion), channel_id=1, source_target_pairs={{0,12},{1,9},{2,14},{3,11},{4,8},{5,13},{6,10},{7,15},{8,4},{9,1},... | collective-permute-start | bytes 393224 | tf_op jit(solution)/shard_map/ppermute | solution.py:143
  8.3 0.0 copy-done.1
  8.3 0.0 copy-done.2
  8.3 0.0 copy-done.7
  8.3 0.6 %copy-done.4 = s32[1,1,8,4]{2,3,1,0:T(4,128)S(1)} copy-done((s32[1,1,8,4]{2,3,1,0:T(4,128)S(1)}, s32[1,1,8,4]{2,3,1,0:T(4,128)}, u32[]{:S(2)}) %copy-start.4) | copy-done | bytes 152
  9.0 0.0 copy-done.3
  9.0 0.0 copy-done.5
  9.0 0.0 copy-done.6
  9.0 1.2 %copy-done = bf16[1,1,8,4,128,128]{5,4,3,2,1,0:T(8,128)(2,1)S(1)} copy-done((bf16[1,1,8,4,128,128]{5,4,3,2,1,0:T(8,128)(2,1)S(1)}, bf16[1,1,8,4,128,128]{5,4,3,2,1,0:T(8,128)(2,1)}, u32[]{:S(2)}) %copy-start) | copy-done | bytes 1048600
  10.2 1.7 %shard_map.112 = (bf16[4,4,128,128]{3,2,1,0:T(8,128)(2,1)S(1)}, bf16[4,4,128,128]{3,2,1,0:T(8,128)(2,1)S(1)}, bf16[128,128]{1,0:T(8,128)(2,1)S(1)}, f32[1,128]{1...) custom-call(bf16[1,1,8,4,128,128]{5,4,3,2,1,0:T(8,128)(2,1)S(1)} %copy-done, ...), custom_call_target="tpu_custom_call" | custom-call | bytes 2097152 | tf_op jit(solution)/shard_map/pallas_call | solution.py:158
  12.0 0.4 collective-permute-done.1.refs_0_
  12.3 0.0 collective-permute-done.x_ref
  12.4 0.1 collective-permute-start.2
  12.5 4.5 %collective-permute-start.6 = (bf16[1024,128]{1,0:T(8,128)(2,1)S(1)}, bf16[1024,128]{1,0:T(8,128)(2,1)S(1)}, u32[]{:S(2)}, u32[]{:S(2)}) collective-permute-start(bf16[1024,128]{1,0:T(8,128)(2,1)S(1)} %shard_map.113.refs_4_), channel_id=1, source_target_pairs={{0,12},{2,14},{4,8},{6,10},{8,4},{10,6},{12,0},{14,2},{16,28},{18,... | collective-permute-start | bytes 786440 | tf_op jit(solution)/shard_map/ppermute | solution.py:151
  17.0 0.0 collective-permute-done.2
  17.1 0.5 %collective-permute-start.7 = (bf16[1024,128]{1,0:T(8,128)(2,1)S(1)}, bf16[1024,128]{1,0:T(8,128)(2,1)S(1)}, u32[]{:S(2)}, u32[]{:S(2)}) collective-permute-start(bf16[1024,128]{1,0:T(8,128)(2,1)S(1)} %broadcast_select_fusion.1.refs_0_), channel_id=1, source_target_pairs={{0,8},{1,5},{2,10},{3,7},{4,12},{5,1},{6,14},{7,3},{8,0},{9,13},{1... | collective-permute-start | bytes 786440 | tf_op jit(solution)/shard_map/ppermute | solution.py:143
  17.6 1.8 %collective-permute-start.5 = (bf16[768,128]{1,0:T(8,128)(2,1)S(1)}, bf16[768,128]{1,0:T(8,128)(2,1)S(1)}, u32[]{:S(2)}, u32[]{:S(2)}) collective-permute-start(bf16[768,128]{1,0:T(8,128)(2,1)S(1)} %shard_map.116), channel_id=1, source_target_pairs={{0,2},{1,3},{2,0},{3,1},{4,6},{5,7},{6,4},{7,5},{8,10},{9,11},{10,... | collective-permute-start | bytes 589832 | tf_op jit(solution)/shard_map/ppermute | solution.py:140
  19.5 0.0 copy-start.8
  19.5 0.1 collective-permute-start.4
  19.6 0.5 collective-permute-start.3
  20.1 1.7 %collective-permute-done.6 = bf16[1024,128]{1,0:T(8,128)(2,1)S(1)} collective-permute-done((bf16[1024,128]{1,0:T(8,128)(2,1)S(1)}, bf16[1024,128]{1,0:T(8,128)(2,1)S(1)}, u32[]{:S(2)}, u32[]{:S(2)}) %collective-permute-start.6) | collective-permute-done | bytes 262176 | tf_op jit(solution)/shard_map/ppermute | solution.py:151
  21.7 0.0 copy-done.8
  21.8 1.6 %collective-permute-done.5 = bf16[768,128]{1,0:T(8,128)(2,1)S(1)} collective-permute-done((bf16[768,128]{1,0:T(8,128)(2,1)S(1)}, bf16[768,128]{1,0:T(8,128)(2,1)S(1)}, u32[]{:S(2)}, u32[]{:S(2)}) %collective-permute-start.5) | collective-permute-done | bytes 196640 | tf_op jit(solution)/shard_map/ppermute | solution.py:140
  23.5 0.0 collective-permute-done.3.refs_1_
  23.5 1.2 %collective-permute-done.7.refs_7_ = bf16[1024,128]{1,0:T(8,128)(2,1)S(1)} collective-permute-done((bf16[1024,128]{1,0:T(8,128)(2,1)S(1)}, bf16[1024,128]{1,0:T(8,128)(2,1)S(1)}, u32[]{:S(2)}, u32[]{:S(2)}) %collective-permute-start.7) | collective-permute-done | bytes 262176 | tf_op jit(solution)/shard_map/ppermute | solution.py:143
  24.6 0.0 collective-permute-done.4.refs_3_
  24.6 1.1 %shard_map.117 = (f32[512,128]{1,0:T(8,128)S(1)}, f32[512,128]{1,0:T(8,128)S(1)}) custom-call(s32[4,8]{1,0:T(4,128)S(1)} %get-tuple-element.16.x_ref.refs_0_, s32[4,8]{1,0:T(4,128)S(1)} %collective-permute-done.3.refs_1_, bf16[4,4,128,128]{3,2,1,0:T(8,128)(2,1)S(1)} %get-tuple-element.18.refs_2_, ...), custom_call_target="tpu_custom_call" | custom-call | tf_op jit(solution)/shard_map/pallas_call | solution.py:231
  25.8 0.1 collective-permute-start.8
  25.9 1.5 %collective-permute-done.8 = f32[512,128]{1,0:T(8,128)S(1)} collective-permute-done((f32[512,128]{1,0:T(8,128)S(1)}, f32[512,128]{1,0:T(8,128)S(1)}, u32[]{:S(2)}, u32[]{:S(2)}) %collective-permute-start.8) | collective-permute-done | bytes 262176 | tf_op jit(solution)/shard_map/ppermute | solution.py:140
  27.4 1.8 %collective-permute-start.9 = (f16[512,128]{1,0:T(8,128)(2,1)S(1)}, f16[512,128]{1,0:T(8,128)(2,1)S(1)}, u32[]{:S(2)}, u32[]{:S(2)}) collective-permute-start(f16[512,128]{1,0:T(8,128)(2,1)S(1)} %multiply_convert_fusion.1), channel_id=1, source_target_pairs={{0,2},{1,3},{2,0},{3,1},{4,6},{5,7},{6,4},{7,5},{8,10},{9,11},{10,... | collective-permute-start | bytes 393224 | tf_op jit(solution)/shard_map/ppermute | solution.py:140
  29.2 3.8 %collective-permute-done.9 = f16[512,128]{1,0:T(8,128)(2,1)S(1)} collective-permute-done((f16[512,128]{1,0:T(8,128)(2,1)S(1)}, f16[512,128]{1,0:T(8,128)(2,1)S(1)}, u32[]{:S(2)}, u32[]{:S(2)}) %collective-permute-start.9) | collective-permute-done | bytes 131104 | tf_op jit(solution)/shard_map/ppermute | solution.py:140
  33.1 0.4 shard_map.118
  33.5 0.1 collective-permute-start.10
  33.6 1.2 %collective-permute-done.10 = f32[72,128]{1,0:T(8,128)S(1)} collective-permute-done((f32[72,128]{1,0:T(8,128)S(1)}, f32[72,128]{1,0:T(8,128)S(1)}, u32[]{:S(2)}, u32[]{:S(2)}) %collective-permute-start.10) | collective-permute-done | bytes 36896 | tf_op jit(solution)/shard_map/ppermute | solution.py:140
  34.8 0.4 collective-permute-start.11
  35.2 3.5 %collective-permute-done.11 = f32[72,128]{1,0:T(8,128)S(1)} collective-permute-done((f32[72,128]{1,0:T(8,128)S(1)}, f32[72,128]{1,0:T(8,128)S(1)}, u32[]{:S(2)}, u32[]{:S(2)}) %collective-permute-start.11) | collective-permute-done | bytes 36896 | tf_op jit(solution)/shard_map/ppermute | solution.py:137
  38.8 1.6 %collective-permute-start.12 = (f32[72,128]{1,0:T(8,128)S(1)}, f32[72,128]{1,0:T(8,128)S(1)}, u32[]{:S(2)}, u32[]{:S(2)}) collective-permute-start(f32[72,128]{1,0:T(8,128)S(1)} %add.39), channel_id=1, source_target_pairs={{0,8},{4,12},{8,0},{12,4},{16,24},{20,28},{24,16},{28,20},{1,9},{5... | collective-permute-start | bytes 110600 | tf_op jit(solution)/shard_map/ppermute | solution.py:137
  40.3 2.4 %collective-permute-done.12 = f32[72,128]{1,0:T(8,128)S(1)} collective-permute-done((f32[72,128]{1,0:T(8,128)S(1)}, f32[72,128]{1,0:T(8,128)S(1)}, u32[]{:S(2)}, u32[]{:S(2)}) %collective-permute-start.12) | collective-permute-done | bytes 36896 | tf_op jit(solution)/shard_map/ppermute | solution.py:137
  42.7 2.1 %collective-permute-start.13 = (f32[72,128]{1,0:T(8,128)S(1)}, f32[72,128]{1,0:T(8,128)S(1)}, u32[]{:S(2)}, u32[]{:S(2)}) collective-permute-start(f32[72,128]{1,0:T(8,128)S(1)} %add.40), channel_id=1, source_target_pairs={{0,16},{4,20},{8,24},{12,28},{16,0},{20,4},{24,8},{28,12},{1,17},{... | collective-permute-start | bytes 110600 | tf_op jit(solution)/shard_map/ppermute | solution.py:137
  44.8 2.8 %collective-permute-done.13 = f32[72,128]{1,0:T(8,128)S(1)} collective-permute-done((f32[72,128]{1,0:T(8,128)S(1)}, f32[72,128]{1,0:T(8,128)S(1)}, u32[]{:S(2)}, u32[]{:S(2)}) %collective-permute-start.13) | collective-permute-done | bytes 36896 | tf_op jit(solution)/shard_map/ppermute | solution.py:137
  47.6 0.0 collective-permute-start.14
  47.6 0.6 %dynamic-slice_convert_fusion = bf16[256,128]{1,0:T(8,128)(2,1)} fusion(f32[512,128]{1,0:T(8,128)S(1)} %get-tuple-element.24, s32[]{:T(128)S(6)} %select_n.71), kind=kLoop, calls=%fused_computation.7 | loop fusion | bytes 131076 | tf_op jit(solution)/shard_map/convert_element_type | solution.py:266
  48.3 0.6 %collective-permute-done.14.other_ref = f32[72,128]{1,0:T(8,128)S(1)} collective-permute-done((f32[72,128]{1,0:T(8,128)S(1)}, f32[72,128]{1,0:T(8,128)S(1)}, u32[]{:S(2)}, u32[]{:S(2)}) %collective-permute-start.14) | collective-permute-done | bytes 36896 | tf_op jit(solution)/shard_map/ppermute | solution.py:140
  48.8 0.6 %shard_map.119 = (f32[128,128]{1,0:T(8,128)}, f32[1,128]{1,0:T(1,128)}) custom-call(f32[72,128]{1,0:T(8,128)S(1)} %add.41.mine_ref, f32[72,128]{1,0:T(8,128)S(1)} %collective-permute-done.14.other_ref), custom_call_target="tpu_custom_call" | custom-call | tf_op jit(solution)/shard_map/pallas_call | solution.py:272
  (23 shorter events, 0.3 us)
Async XLA Ops:
  0.6 11.7 %collective-permute-start = (bf16[1024,128]{1,0:T(8,128)(2,1)}, bf16[1024,128]{1,0:T(8,128)(2,1)S(1)}, u32[]{:S(2)}, u32[]{:S(2)}) collective-permute-start(bf16[1024,128]{1,0:T(8,128)(2,1)} %param.9), channel_id=1, source_target_pairs={{0,16},{1,5},{2,18},{3,7},{4,20},{5,1},{6,22},{7,3},{8,24},{9,13},... | collective-permute-start | bytes 786440 | tf_op jit(solution)/shard_map/ppermute | solution.py:143
  4.7 3.6 %copy-start.1 = (bf16[256,128]{1,0:T(8,128)(2,1)S(1)}, bf16[256,128]{1,0:T(8,128)(2,1)}, u32[]{:S(2)}) copy-start(bf16[256,128]{1,0:T(8,128)(2,1)} %refs_4_.1) | copy-start | bytes 196612
  4.7 3.6 %copy-start.2 = (bf16[128,128]{1,0:T(8,128)(2,1)S(1)}, bf16[128,128]{1,0:T(8,128)(2,1)}, u32[]{:S(2)}) copy-start(bf16[128,128]{1,0:T(8,128)(2,1)} %refs_1_.1) | copy-start | bytes 98308
  4.7 3.6 %copy-start.7 = (s32[1,1,8]{2,1,0:T(1,128)S(1)}, s32[1,1,8]{2,1,0:T(1,128)}, u32[]{:S(2)}) copy-start(s32[1,1,8]{2,1,0:T(1,128)} %refs_7_.1) | copy-start | bytes 100
  5.7 6.6 %collective-permute-start.1 = (bf16[512,128]{1,0:T(8,128)(2,1)S(1)}, bf16[512,128]{1,0:T(8,128)(2,1)S(1)}, u32[]{:S(2)}, u32[]{:S(2)}) collective-permute-start(bf16[512,128]{1,0:T(8,128)(2,1)S(1)} %constant_dynamic-slice_fusion), channel_id=1, source_target_pairs={{0,12},{1,9},{2,14},{3,11},{4,8},{5,13},{6,10},{7,15},{8,4},{9,1},... | collective-permute-start | bytes 393224 | tf_op jit(solution)/shard_map/ppermute | solution.py:143
  8.3 0.7 %copy-start.4 = (s32[1,1,8,4]{2,3,1,0:T(4,128)S(1)}, s32[1,1,8,4]{2,3,1,0:T(4,128)}, u32[]{:S(2)}) copy-start(s32[1,1,8,4]{2,3,1,0:T(4,128)} %param.14) | copy-start | bytes 388
  8.3 0.7 %copy-start.3 = (s32[1,1,8,4]{2,3,1,0:T(4,128)S(1)}, s32[1,1,8,4]{2,3,1,0:T(4,128)}, u32[]{:S(2)}) copy-start(s32[1,1,8,4]{2,3,1,0:T(4,128)} %param.13) | copy-start | bytes 388
  8.3 0.7 %copy-start.5 = (s32[256]{0:T(256)S(1)}, s32[256]{0:T(256)}, u32[]{:S(2)}) copy-start(s32[256]{0:T(256)} %param.16) | copy-start | bytes 3076
  8.3 0.7 %copy-start.6 = (f32[128]{0:T(128)S(1)}, f32[128]{0:T(128)}, u32[]{:S(2)}) copy-start(f32[128]{0:T(128)} %param.11) | copy-start | bytes 1540
  9.0 1.2 %copy-start = (bf16[1,1,8,4,128,128]{5,4,3,2,1,0:T(8,128)(2,1)S(1)}, bf16[1,1,8,4,128,128]{5,4,3,2,1,0:T(8,128)(2,1)}, u32[]{:S(2)}) copy-start(bf16[1,1,8,4,128,128]{5,4,3,2,1,0:T(8,128)(2,1)} %refs_0_.1) | copy-start | bytes 3145732
  12.4 4.7 %collective-permute-start.2 = (bf16[1024,128]{1,0:T(8,128)(2,1)S(1)}, bf16[1024,128]{1,0:T(8,128)(2,1)S(1)}, u32[]{:S(2)}, u32[]{:S(2)}) collective-permute-start(bf16[1024,128]{1,0:T(8,128)(2,1)S(1)} %shard_map.113.refs_4_), channel_id=1, source_target_pairs={{0,1},{1,0},{2,3},{3,2},{4,5},{5,4},{6,7},{7,6},{8,9},{9,8},{10,11... | collective-permute-start | bytes 786440 | tf_op jit(solution)/shard_map/ppermute | solution.py:140
  12.5 9.3 %collective-permute-start.6 = (bf16[1024,128]{1,0:T(8,128)(2,1)S(1)}, bf16[1024,128]{1,0:T(8,128)(2,1)S(1)}, u32[]{:S(2)}, u32[]{:S(2)}) collective-permute-start(bf16[1024,128]{1,0:T(8,128)(2,1)S(1)} %shard_map.113.refs_4_), channel_id=1, source_target_pairs={{0,12},{2,14},{4,8},{6,10},{8,4},{10,6},{12,0},{14,2},{16,28},{18,... | collective-permute-start | bytes 786440 | tf_op jit(solution)/shard_map/ppermute | solution.py:151
  17.1 7.6 %collective-permute-start.7 = (bf16[1024,128]{1,0:T(8,128)(2,1)S(1)}, bf16[1024,128]{1,0:T(8,128)(2,1)S(1)}, u32[]{:S(2)}, u32[]{:S(2)}) collective-permute-start(bf16[1024,128]{1,0:T(8,128)(2,1)S(1)} %broadcast_select_fusion.1.refs_0_), channel_id=1, source_target_pairs={{0,8},{1,5},{2,10},{3,7},{4,12},{5,1},{6,14},{7,3},{8,0},{9,13},{1... | collective-permute-start | bytes 786440 | tf_op jit(solution)/shard_map/ppermute | solution.py:143
  17.6 5.7 %collective-permute-start.5 = (bf16[768,128]{1,0:T(8,128)(2,1)S(1)}, bf16[768,128]{1,0:T(8,128)(2,1)S(1)}, u32[]{:S(2)}, u32[]{:S(2)}) collective-permute-start(bf16[768,128]{1,0:T(8,128)(2,1)S(1)} %shard_map.116), channel_id=1, source_target_pairs={{0,2},{1,3},{2,0},{3,1},{4,6},{5,7},{6,4},{7,5},{8,10},{9,11},{10,... | collective-permute-start | bytes 589832 | tf_op jit(solution)/shard_map/ppermute | solution.py:140
  19.5 2.3 %copy-start.8 = (bf16[1024,128]{1,0:T(8,128)(2,1)S(1)}, bf16[1024,128]{1,0:T(8,128)(2,1)}, u32[]{:S(2)}) copy-start(bf16[1024,128]{1,0:T(8,128)(2,1)} %param.9) | copy-start | bytes 786436
  19.5 5.2 %collective-permute-start.4 = (bf16[4,4,128,128]{3,2,1,0:T(8,128)(2,1)S(1)}, bf16[4,4,128,128]{3,2,1,0:T(8,128)(2,1)S(1)}, u32[]{:S(2)}, u32[]{:S(2)}) collective-permute-start(bf16[4,4,128,128]{3,2,1,0:T(8,128)(2,1)S(1)} %shard_map.115), channel_id=1, source_target_pairs={{0,1},{1,0},{2,3},{3,2},{4,5},{5,4},{6,7},{7,6},{8,9},{9,8},{10,11... | collective-permute-start | bytes 1572872 | tf_op jit(solution)/shard_map/ppermute | solution.py:140
  19.6 3.9 %collective-permute-start.3 = (s32[4,8]{1,0:T(4,128)S(1)}, s32[4,8]{1,0:T(4,128)S(1)}, u32[]{:S(2)}, u32[]{:S(2)}) collective-permute-start(s32[4,8]{1,0:T(4,128)S(1)} %shard_map.114), channel_id=1, source_target_pairs={{0,1},{1,0},{2,3},{3,2},{4,5},{5,4},{6,7},{7,6},{8,9},{9,8},{10,11... | collective-permute-start | bytes 392 | tf_op jit(solution)/shard_map/ppermute | solution.py:140
  25.8 1.6 %collective-permute-start.8 = (f32[512,128]{1,0:T(8,128)S(1)}, f32[512,128]{1,0:T(8,128)S(1)}, u32[]{:S(2)}, u32[]{:S(2)}) collective-permute-start(f32[512,128]{1,0:T(8,128)S(1)} %get-tuple-element.21), channel_id=1, source_target_pairs={{0,1},{1,0},{2,3},{3,2},{4,5},{5,4},{6,7},{7,6},{8,9},{9,8},{10,11... | collective-permute-start | bytes 786440 | tf_op jit(solution)/shard_map/ppermute | solution.py:140
  27.4 5.6 %collective-permute-start.9 = (f16[512,128]{1,0:T(8,128)(2,1)S(1)}, f16[512,128]{1,0:T(8,128)(2,1)S(1)}, u32[]{:S(2)}, u32[]{:S(2)}) collective-permute-start(f16[512,128]{1,0:T(8,128)(2,1)S(1)} %multiply_convert_fusion.1), channel_id=1, source_target_pairs={{0,2},{1,3},{2,0},{3,1},{4,6},{5,7},{6,4},{7,5},{8,10},{9,11},{10,... | collective-permute-start | bytes 393224 | tf_op jit(solution)/shard_map/ppermute | solution.py:140
  33.5 1.3 %collective-permute-start.10 = (f32[72,128]{1,0:T(8,128)S(1)}, f32[72,128]{1,0:T(8,128)S(1)}, u32[]{:S(2)}, u32[]{:S(2)}) collective-permute-start(f32[72,128]{1,0:T(8,128)S(1)} %get-tuple-element.26), channel_id=1, source_target_pairs={{0,1},{1,0},{2,3},{3,2},{4,5},{5,4},{6,7},{7,6},{8,9},{9,8},{10,11... | collective-permute-start | bytes 110600 | tf_op jit(solution)/shard_map/ppermute | solution.py:140
  34.8 4.0 %collective-permute-start.11 = (f32[72,128]{1,0:T(8,128)S(1)}, f32[72,128]{1,0:T(8,128)S(1)}, u32[]{:S(2)}, u32[]{:S(2)}) collective-permute-start(f32[72,128]{1,0:T(8,128)S(1)} %add.38), channel_id=1, source_target_pairs={{0,4},{4,0},{8,12},{12,8},{16,20},{20,16},{24,28},{28,24},{1,5},{5... | collective-permute-start | bytes 110600 | tf_op jit(solution)/shard_map/ppermute | solution.py:137
  38.8 4.0 %collective-permute-start.12 = (f32[72,128]{1,0:T(8,128)S(1)}, f32[72,128]{1,0:T(8,128)S(1)}, u32[]{:S(2)}, u32[]{:S(2)}) collective-permute-start(f32[72,128]{1,0:T(8,128)S(1)} %add.39), channel_id=1, source_target_pairs={{0,8},{4,12},{8,0},{12,4},{16,24},{20,28},{24,16},{28,20},{1,9},{5... | collective-permute-start | bytes 110600 | tf_op jit(solution)/shard_map/ppermute | solution.py:137
  42.7 4.9 %collective-permute-start.13 = (f32[72,128]{1,0:T(8,128)S(1)}, f32[72,128]{1,0:T(8,128)S(1)}, u32[]{:S(2)}, u32[]{:S(2)}) collective-permute-start(f32[72,128]{1,0:T(8,128)S(1)} %add.40), channel_id=1, source_target_pairs={{0,16},{4,20},{8,24},{12,28},{16,0},{20,4},{24,8},{28,12},{1,17},{... | collective-permute-start | bytes 110600 | tf_op jit(solution)/shard_map/ppermute | solution.py:137
  47.6 1.2 %collective-permute-start.14 = (f32[72,128]{1,0:T(8,128)S(1)}, f32[72,128]{1,0:T(8,128)S(1)}, u32[]{:S(2)}, u32[]{:S(2)}) collective-permute-start(f32[72,128]{1,0:T(8,128)S(1)} %add.41.mine_ref), channel_id=1, source_target_pairs={{0,1},{1,0},{2,3},{3,2},{4,5},{5,4},{6,7},{7,6},{8,9},{9,8},{10,11... | collective-permute-start | bytes 110600 | tf_op jit(solution)/shard_map/ppermute | solution.py:140

commit v5 on v4

--- a/solution.py
+++ b/solution.py
@@ -99,7 +99,7 @@
     core = lax.axis_index("rep") % 2
     gw_ref[pl.ds(pl.multiple_of(core * half, half), half)] = mine_ref[pl.ds(0, half)]
     gw_ref[pl.ds(pl.multiple_of((1 - core) * half, half), half)] = other_ref[pl.ds(0, half)]
-    gb_ref[...] = mine_ref[pl.ds(half, 1)]
+    gb_ref[...] = jnp.where(core == 0, mine_ref[pl.ds(half, 1)], other_ref[pl.ds(half, 1)])
 
 
 def fence_kernel(x_ref, *refs):
@@ -265,10 +265,9 @@
 
     output = lax.dynamic_slice_in_dim(act, rep // 2 * share, share, 0).astype(jnp.bfloat16)
     grads = grads + rep_swap(send, 1)
-    bit = 1
-    while bit < nblk:
-        grads = grads + blk_swap(grads, bit)
-        bit *= 2
+    bits = [1 << i for i in range(nblk.bit_length() - 1)]
+    for bit0, bit1 in zip(bits, bits[1:] + bits[:1]):
+        grads = grads + two_ways(grads, bit0, bit1)
     grad_weight, grad_bias = pl.pallas_call(
         last_kernel,
         out_shape=(

time: 49.7 us -> 49.7 us (level)
    ppermute x3 -> x0, waiting for transfers between devices: 8.72 us -> none  [blk_swap(): return lax.ppermute(x, 'blk', [(i, i ^ off) for i in range(nblk)])]
    ppermute x3 -> x6, waiting for transfers between devices: 1.56 us -> 10.3 us  [two_ways(): lax.ppermute(x, BOTH, [(b * nrep + r, (b ^ (off1 if r % 2 else off0)) * n...]
    ppermute x3 -> x6, starting transfers between devices: 7.19 us -> 11.2 us  [two_ways(): lax.ppermute(x, BOTH, [(b * nrep + r, (b ^ (off1 if r % 2 else off0)) * n...]
    ppermute x3 -> x0, starting transfers between devices: 4.05 us -> none  [blk_swap(): return lax.ppermute(x, 'blk', [(i, i ^ off) for i in range(nblk)])]
where the time goes in v5:
time: 49.7 us; the launch traced here: 49.5 us
  waiting for transfers between devices  20.6 us (41%)
  starting transfers between devices  20.2 us (41%)
  Pallas kernels  4 us (8%)
  local copies, waits for them, and re-layouts  3.54 us (7%)
  between operations  0.85 us (2%)
    ppermute x6, starting transfers between devices, two_ways(): lax.ppermute(x, BOTH, [(b * nrep + r, (b ^ (off1 if r % 2 else off0)) * n...  11.2 us
    ppermute x6, waiting for transfers between devices, two_ways(): lax.ppermute(x, BOTH, [(b * nrep + r, (b ^ (off1 if r % 2 else off0)) * n...  10.3 us
    ppermute x8, waiting for transfers between devices, rep_swap(): return lax.ppermute(x, 'rep', [(i, i ^ off) for i in range(nrep)])  8.66 us
    ppermute x1, starting transfers between devices, one_core(): lax.ppermute(x, BOTH, [(b * nrep + r, (b ^ off) * nrep + r) for b in rang...  4.54 us
    ppermute x8, starting transfers between devices, rep_swap(): return lax.ppermute(x, 'rep', [(i, i ^ off) for i in range(nrep)])  4.39 us
    unnamed x18, local copies, waits for them, and re-layouts  1.92 us
    pallas_call x1, Pallas kernels, stage(): pl.pallas_call(functools.partial(stage_kernel, rblk, plan), out_shape=(ja...  1.73 us
    ppermute x1, waiting for transfers between devices, one_core(): lax.ppermute(x, BOTH, [(b * nrep + r, (b ^ off) * nrep + r) for b in rang...  1.69 us
  transfers between devices with their start and end apart: 15, of which 11 were waited for; matrix products, arithmetic and copies ran while one was open for 4% of the time, Pallas kernels for 4%

profile of v5, /device:TPU:0, one launch (start us, length us, event | category | flops | bytes accessed | tf_op | source)
XLA Modules:
  0.0 49.5 jit_solution(35701441389545128)
XLA Ops:
  0.6 4.1 %collective-permute-start = (bf16[1024,128]{1,0:T(8,128)(2,1)}, bf16[1024,128]{1,0:T(8,128)(2,1)S(1)}, u32[]{:S(2)}, u32[]{:S(2)}) collective-permute-start(bf16[1024,128]{1,0:T(8,128)(2,1)} %param.9), channel_id=1, source_target_pairs={{0,16},{1,5},{2,18},{3,7},{4,20},{5,1},{6,22},{7,3},{8,24},{9,13},... | collective-permute-start | bytes 786440 | tf_op jit(solution)/shard_map/ppermute | solution.py:143
  4.7 0.0 copy-start.1
  4.7 0.0 copy-start.2
  4.7 1.0 %constant_dynamic-slice_fusion = bf16[512,128]{1,0:T(8,128)(2,1)S(1)} fusion(bf16[1024,128]{1,0:T(8,128)(2,1)} %param.9, s32[]{:T(128)S(6)} %select_n.62), kind=kLoop, calls=%fused_computation.12 | loop fusion | bytes 262148 | tf_op jit(solution)/shard_map/dynamic_slice | solution.py:206
  5.7 2.6 %collective-permute-start.1 = (bf16[512,128]{1,0:T(8,128)(2,1)S(1)}, bf16[512,128]{1,0:T(8,128)(2,1)S(1)}, u32[]{:S(2)}, u32[]{:S(2)}) collective-permute-start(bf16[512,128]{1,0:T(8,128)(2,1)S(1)} %constant_dynamic-slice_fusion), channel_id=1, source_target_pairs={{0,12},{1,9},{2,14},{3,11},{4,8},{5,13},{6,10},{7,15},{8,4},{9,1},... | collective-permute-start | bytes 393224 | tf_op jit(solution)/shard_map/ppermute | solution.py:143
  8.3 0.0 copy-done.1
  8.3 0.0 copy-done.2
  8.3 0.0 copy-done.7
  8.3 0.6 %copy-done.4 = s32[1,1,8,4]{2,3,1,0:T(4,128)S(1)} copy-done((s32[1,1,8,4]{2,3,1,0:T(4,128)S(1)}, s32[1,1,8,4]{2,3,1,0:T(4,128)}, u32[]{:S(2)}) %copy-start.4) | copy-done | bytes 152
  9.0 0.0 copy-done.3
  9.0 0.0 copy-done.5
  9.0 0.0 copy-done.6
  9.0 1.2 %copy-done = bf16[1,1,8,4,128,128]{5,4,3,2,1,0:T(8,128)(2,1)S(1)} copy-done((bf16[1,1,8,4,128,128]{5,4,3,2,1,0:T(8,128)(2,1)S(1)}, bf16[1,1,8,4,128,128]{5,4,3,2,1,0:T(8,128)(2,1)}, u32[]{:S(2)}) %copy-start) | copy-done | bytes 1048600
  10.2 1.7 %shard_map.112 = (bf16[4,4,128,128]{3,2,1,0:T(8,128)(2,1)S(1)}, bf16[4,4,128,128]{3,2,1,0:T(8,128)(2,1)S(1)}, bf16[128,128]{1,0:T(8,128)(2,1)S(1)}, f32[1,128]{1...) custom-call(bf16[1,1,8,4,128,128]{5,4,3,2,1,0:T(8,128)(2,1)S(1)} %copy-done, ...), custom_call_target="tpu_custom_call" | custom-call | bytes 2097152 | tf_op jit(solution)/shard_map/pallas_call | solution.py:158
  12.0 0.4 collective-permute-done.1.refs_0_
  12.3 0.0 collective-permute-done.x_ref
  12.4 0.1 collective-permute-start.2
  12.5 4.5 %collective-permute-start.6 = (bf16[1024,128]{1,0:T(8,128)(2,1)S(1)}, bf16[1024,128]{1,0:T(8,128)(2,1)S(1)}, u32[]{:S(2)}, u32[]{:S(2)}) collective-permute-start(bf16[1024,128]{1,0:T(8,128)(2,1)S(1)} %shard_map.113.refs_4_), channel_id=1, source_target_pairs={{0,12},{2,14},{4,8},{6,10},{8,4},{10,6},{12,0},{14,2},{16,28},{18,... | collective-permute-start | bytes 786440 | tf_op jit(solution)/shard_map/ppermute | solution.py:151
  17.0 0.0 collective-permute-done.2
  17.1 0.5 %collective-permute-start.7 = (bf16[1024,128]{1,0:T(8,128)(2,1)S(1)}, bf16[1024,128]{1,0:T(8,128)(2,1)S(1)}, u32[]{:S(2)}, u32[]{:S(2)}) collective-permute-start(bf16[1024,128]{1,0:T(8,128)(2,1)S(1)} %broadcast_select_fusion.1.refs_0_), channel_id=1, source_target_pairs={{0,8},{1,5},{2,10},{3,7},{4,12},{5,1},{6,14},{7,3},{8,0},{9,13},{1... | collective-permute-start | bytes 786440 | tf_op jit(solution)/shard_map/ppermute | solution.py:143
  17.6 1.8 %collective-permute-start.5 = (bf16[768,128]{1,0:T(8,128)(2,1)S(1)}, bf16[768,128]{1,0:T(8,128)(2,1)S(1)}, u32[]{:S(2)}, u32[]{:S(2)}) collective-permute-start(bf16[768,128]{1,0:T(8,128)(2,1)S(1)} %shard_map.116), channel_id=1, source_target_pairs={{0,2},{1,3},{2,0},{3,1},{4,6},{5,7},{6,4},{7,5},{8,10},{9,11},{10,... | collective-permute-start | bytes 589832 | tf_op jit(solution)/shard_map/ppermute | solution.py:140
  19.5 0.0 copy-start.8
  19.5 0.1 collective-permute-start.4
  19.6 0.5 collective-permute-start.3
  20.1 1.7 %collective-permute-done.6 = bf16[1024,128]{1,0:T(8,128)(2,1)S(1)} collective-permute-done((bf16[1024,128]{1,0:T(8,128)(2,1)S(1)}, bf16[1024,128]{1,0:T(8,128)(2,1)S(1)}, u32[]{:S(2)}, u32[]{:S(2)}) %collective-permute-start.6) | collective-permute-done | bytes 262176 | tf_op jit(solution)/shard_map/ppermute | solution.py:151
  21.7 0.0 copy-done.8
  21.8 1.6 %collective-permute-done.5 = bf16[768,128]{1,0:T(8,128)(2,1)S(1)} collective-permute-done((bf16[768,128]{1,0:T(8,128)(2,1)S(1)}, bf16[768,128]{1,0:T(8,128)(2,1)S(1)}, u32[]{:S(2)}, u32[]{:S(2)}) %collective-permute-start.5) | collective-permute-done | bytes 196640 | tf_op jit(solution)/shard_map/ppermute | solution.py:140
  23.5 0.0 collective-permute-done.3.refs_1_
  23.5 1.2 %collective-permute-done.7.refs_7_ = bf16[1024,128]{1,0:T(8,128)(2,1)S(1)} collective-permute-done((bf16[1024,128]{1,0:T(8,128)(2,1)S(1)}, bf16[1024,128]{1,0:T(8,128)(2,1)S(1)}, u32[]{:S(2)}, u32[]{:S(2)}) %collective-permute-start.7) | collective-permute-done | bytes 262176 | tf_op jit(solution)/shard_map/ppermute | solution.py:143
  24.6 0.0 collective-permute-done.4.refs_3_
  24.6 1.1 %shard_map.117 = (f32[512,128]{1,0:T(8,128)S(1)}, f32[512,128]{1,0:T(8,128)S(1)}) custom-call(s32[4,8]{1,0:T(4,128)S(1)} %get-tuple-element.16.x_ref.refs_0_, s32[4,8]{1,0:T(4,128)S(1)} %collective-permute-done.3.refs_1_, bf16[4,4,128,128]{3,2,1,0:T(8,128)(2,1)S(1)} %get-tuple-element.18.refs_2_, ...), custom_call_target="tpu_custom_call" | custom-call | tf_op jit(solution)/shard_map/pallas_call | solution.py:231
  25.8 0.1 collective-permute-start.8
  25.9 1.5 %collective-permute-done.8 = f32[512,128]{1,0:T(8,128)S(1)} collective-permute-done((f32[512,128]{1,0:T(8,128)S(1)}, f32[512,128]{1,0:T(8,128)S(1)}, u32[]{:S(2)}, u32[]{:S(2)}) %collective-permute-start.8) | collective-permute-done | bytes 262176 | tf_op jit(solution)/shard_map/ppermute | solution.py:140
  27.4 1.8 %collective-permute-start.9 = (f16[512,128]{1,0:T(8,128)(2,1)S(1)}, f16[512,128]{1,0:T(8,128)(2,1)S(1)}, u32[]{:S(2)}, u32[]{:S(2)}) collective-permute-start(f16[512,128]{1,0:T(8,128)(2,1)S(1)} %multiply_convert_fusion.1), channel_id=1, source_target_pairs={{0,2},{1,3},{2,0},{3,1},{4,6},{5,7},{6,4},{7,5},{8,10},{9,11},{10,... | collective-permute-start | bytes 393224 | tf_op jit(solution)/shard_map/ppermute | solution.py:140
  29.2 3.8 %collective-permute-done.9 = f16[512,128]{1,0:T(8,128)(2,1)S(1)} collective-permute-done((f16[512,128]{1,0:T(8,128)(2,1)S(1)}, f16[512,128]{1,0:T(8,128)(2,1)S(1)}, u32[]{:S(2)}, u32[]{:S(2)}) %collective-permute-start.9) | collective-permute-done | bytes 131104 | tf_op jit(solution)/shard_map/ppermute | solution.py:140
  33.1 0.4 shard_map.118
  33.5 0.1 collective-permute-start.10
  33.6 1.2 %collective-permute-done.10 = f32[72,128]{1,0:T(8,128)S(1)} collective-permute-done((f32[72,128]{1,0:T(8,128)S(1)}, f32[72,128]{1,0:T(8,128)S(1)}, u32[]{:S(2)}, u32[]{:S(2)}) %collective-permute-start.10) | collective-permute-done | bytes 36896 | tf_op jit(solution)/shard_map/ppermute | solution.py:140
  34.8 0.4 collective-permute-start.11
  35.2 3.5 %collective-permute-done.11 = f32[72,128]{1,0:T(8,128)S(1)} collective-permute-done((f32[72,128]{1,0:T(8,128)S(1)}, f32[72,128]{1,0:T(8,128)S(1)}, u32[]{:S(2)}, u32[]{:S(2)}) %collective-permute-start.11) | collective-permute-done | bytes 36896 | tf_op jit(solution)/shard_map/ppermute | solution.py:143
  38.8 1.6 %collective-permute-start.12 = (f32[72,128]{1,0:T(8,128)S(1)}, f32[72,128]{1,0:T(8,128)S(1)}, u32[]{:S(2)}, u32[]{:S(2)}) collective-permute-start(f32[72,128]{1,0:T(8,128)S(1)} %add.39), channel_id=1, source_target_pairs={{0,8},{1,17},{2,10},{3,19},{4,12},{5,21},{6,14},{7,23},{8,0},{9,25... | collective-permute-start | bytes 110600 | tf_op jit(solution)/shard_map/ppermute | solution.py:143
  40.3 2.4 %collective-permute-done.12 = f32[72,128]{1,0:T(8,128)S(1)} collective-permute-done((f32[72,128]{1,0:T(8,128)S(1)}, f32[72,128]{1,0:T(8,128)S(1)}, u32[]{:S(2)}, u32[]{:S(2)}) %collective-permute-start.12) | collective-permute-done | bytes 36896 | tf_op jit(solution)/shard_map/ppermute | solution.py:143
  42.7 2.1 %collective-permute-start.13 = (f32[72,128]{1,0:T(8,128)S(1)}, f32[72,128]{1,0:T(8,128)S(1)}, u32[]{:S(2)}, u32[]{:S(2)}) collective-permute-start(f32[72,128]{1,0:T(8,128)S(1)} %add.40), channel_id=1, source_target_pairs={{0,16},{1,5},{2,18},{3,7},{4,20},{5,1},{6,22},{7,3},{8,24},{9,13},... | collective-permute-start | bytes 110600 | tf_op jit(solution)/shard_map/ppermute | solution.py:143
  44.8 2.8 %collective-permute-done.13 = f32[72,128]{1,0:T(8,128)S(1)} collective-permute-done((f32[72,128]{1,0:T(8,128)S(1)}, f32[72,128]{1,0:T(8,128)S(1)}, u32[]{:S(2)}, u32[]{:S(2)}) %collective-permute-start.13) | collective-permute-done | bytes 36896 | tf_op jit(solution)/shard_map/ppermute | solution.py:143
  47.6 0.0 collective-permute-start.14
  47.6 0.6 %dynamic-slice_convert_fusion = bf16[256,128]{1,0:T(8,128)(2,1)} fusion(f32[512,128]{1,0:T(8,128)S(1)} %get-tuple-element.24, s32[]{:T(128)S(6)} %select_n.71), kind=kLoop, calls=%fused_computation.7 | loop fusion | bytes 131076 | tf_op jit(solution)/shard_map/convert_element_type | solution.py:266
  48.3 0.6 %collective-permute-done.14.other_ref = f32[72,128]{1,0:T(8,128)S(1)} collective-permute-done((f32[72,128]{1,0:T(8,128)S(1)}, f32[72,128]{1,0:T(8,128)S(1)}, u32[]{:S(2)}, u32[]{:S(2)}) %collective-permute-start.14) | collective-permute-done | bytes 36896 | tf_op jit(solution)/shard_map/ppermute | solution.py:140
  48.8 0.6 %shard_map.119 = (f32[128,128]{1,0:T(8,128)}, f32[1,128]{1,0:T(1,128)}) custom-call(f32[72,128]{1,0:T(8,128)S(1)} %add.41.mine_ref, f32[72,128]{1,0:T(8,128)S(1)} %collective-permute-done.14.other_ref), custom_call_target="tpu_custom_call" | custom-call | tf_op jit(solution)/shard_map/pallas_call | solution.py:271
  (23 shorter events, 0.3 us)
Async XLA Ops:
  0.6 11.7 %collective-permute-start = (bf16[1024,128]{1,0:T(8,128)(2,1)}, bf16[1024,128]{1,0:T(8,128)(2,1)S(1)}, u32[]{:S(2)}, u32[]{:S(2)}) collective-permute-start(bf16[1024,128]{1,0:T(8,128)(2,1)} %param.9), channel_id=1, source_target_pairs={{0,16},{1,5},{2,18},{3,7},{4,20},{5,1},{6,22},{7,3},{8,24},{9,13},... | collective-permute-start | bytes 786440 | tf_op jit(solution)/shard_map/ppermute | solution.py:143
  4.7 3.6 %copy-start.1 = (bf16[256,128]{1,0:T(8,128)(2,1)S(1)}, bf16[256,128]{1,0:T(8,128)(2,1)}, u32[]{:S(2)}) copy-start(bf16[256,128]{1,0:T(8,128)(2,1)} %refs_4_.1) | copy-start | bytes 196612
  4.7 3.6 %copy-start.2 = (bf16[128,128]{1,0:T(8,128)(2,1)S(1)}, bf16[128,128]{1,0:T(8,128)(2,1)}, u32[]{:S(2)}) copy-start(bf16[128,128]{1,0:T(8,128)(2,1)} %refs_1_.1) | copy-start | bytes 98308
  4.7 3.6 %copy-start.7 = (s32[1,1,8]{2,1,0:T(1,128)S(1)}, s32[1,1,8]{2,1,0:T(1,128)}, u32[]{:S(2)}) copy-start(s32[1,1,8]{2,1,0:T(1,128)} %refs_7_.1) | copy-start | bytes 100
  5.7 6.6 %collective-permute-start.1 = (bf16[512,128]{1,0:T(8,128)(2,1)S(1)}, bf16[512,128]{1,0:T(8,128)(2,1)S(1)}, u32[]{:S(2)}, u32[]{:S(2)}) collective-permute-start(bf16[512,128]{1,0:T(8,128)(2,1)S(1)} %constant_dynamic-slice_fusion), channel_id=1, source_target_pairs={{0,12},{1,9},{2,14},{3,11},{4,8},{5,13},{6,10},{7,15},{8,4},{9,1},... | collective-permute-start | bytes 393224 | tf_op jit(solution)/shard_map/ppermute | solution.py:143
  8.3 0.7 %copy-start.4 = (s32[1,1,8,4]{2,3,1,0:T(4,128)S(1)}, s32[1,1,8,4]{2,3,1,0:T(4,128)}, u32[]{:S(2)}) copy-start(s32[1,1,8,4]{2,3,1,0:T(4,128)} %param.14) | copy-start | bytes 388
  8.3 0.7 %copy-start.3 = (s32[1,1,8,4]{2,3,1,0:T(4,128)S(1)}, s32[1,1,8,4]{2,3,1,0:T(4,128)}, u32[]{:S(2)}) copy-start(s32[1,1,8,4]{2,3,1,0:T(4,128)} %param.13) | copy-start | bytes 388
  8.3 0.7 %copy-start.5 = (s32[256]{0:T(256)S(1)}, s32[256]{0:T(256)}, u32[]{:S(2)}) copy-start(s32[256]{0:T(256)} %param.16) | copy-start | bytes 3076
  8.3 0.7 %copy-start.6 = (f32[128]{0:T(128)S(1)}, f32[128]{0:T(128)}, u32[]{:S(2)}) copy-start(f32[128]{0:T(128)} %param.11) | copy-start | bytes 1540
  9.0 1.2 %copy-start = (bf16[1,1,8,4,128,128]{5,4,3,2,1,0:T(8,128)(2,1)S(1)}, bf16[1,1,8,4,128,128]{5,4,3,2,1,0:T(8,128)(2,1)}, u32[]{:S(2)}) copy-start(bf16[1,1,8,4,128,128]{5,4,3,2,1,0:T(8,128)(2,1)} %refs_0_.1) | copy-start | bytes 3145732
  12.4 4.7 %collective-permute-start.2 = (bf16[1024,128]{1,0:T(8,128)(2,1)S(1)}, bf16[1024,128]{1,0:T(8,128)(2,1)S(1)}, u32[]{:S(2)}, u32[]{:S(2)}) collective-permute-start(bf16[1024,128]{1,0:T(8,128)(2,1)S(1)} %shard_map.113.refs_4_), channel_id=1, source_target_pairs={{0,1},{1,0},{2,3},{3,2},{4,5},{5,4},{6,7},{7,6},{8,9},{9,8},{10,11... | collective-permute-start | bytes 786440 | tf_op jit(solution)/shard_map/ppermute | solution.py:140
  12.5 9.3 %collective-permute-start.6 = (bf16[1024,128]{1,0:T(8,128)(2,1)S(1)}, bf16[1024,128]{1,0:T(8,128)(2,1)S(1)}, u32[]{:S(2)}, u32[]{:S(2)}) collective-permute-start(bf16[1024,128]{1,0:T(8,128)(2,1)S(1)} %shard_map.113.refs_4_), channel_id=1, source_target_pairs={{0,12},{2,14},{4,8},{6,10},{8,4},{10,6},{12,0},{14,2},{16,28},{18,... | collective-permute-start | bytes 786440 | tf_op jit(solution)/shard_map/ppermute | solution.py:151
  17.1 7.6 %collective-permute-start.7 = (bf16[1024,128]{1,0:T(8,128)(2,1)S(1)}, bf16[1024,128]{1,0:T(8,128)(2,1)S(1)}, u32[]{:S(2)}, u32[]{:S(2)}) collective-permute-start(bf16[1024,128]{1,0:T(8,128)(2,1)S(1)} %broadcast_select_fusion.1.refs_0_), channel_id=1, source_target_pairs={{0,8},{1,5},{2,10},{3,7},{4,12},{5,1},{6,14},{7,3},{8,0},{9,13},{1... | collective-permute-start | bytes 786440 | tf_op jit(solution)/shard_map/ppermute | solution.py:143
  17.6 5.7 %collective-permute-start.5 = (bf16[768,128]{1,0:T(8,128)(2,1)S(1)}, bf16[768,128]{1,0:T(8,128)(2,1)S(1)}, u32[]{:S(2)}, u32[]{:S(2)}) collective-permute-start(bf16[768,128]{1,0:T(8,128)(2,1)S(1)} %shard_map.116), channel_id=1, source_target_pairs={{0,2},{1,3},{2,0},{3,1},{4,6},{5,7},{6,4},{7,5},{8,10},{9,11},{10,... | collective-permute-start | bytes 589832 | tf_op jit(solution)/shard_map/ppermute | solution.py:140
  19.5 2.3 %copy-start.8 = (bf16[1024,128]{1,0:T(8,128)(2,1)S(1)}, bf16[1024,128]{1,0:T(8,128)(2,1)}, u32[]{:S(2)}) copy-start(bf16[1024,128]{1,0:T(8,128)(2,1)} %param.9) | copy-start | bytes 786436
  19.5 5.2 %collective-permute-start.4 = (bf16[4,4,128,128]{3,2,1,0:T(8,128)(2,1)S(1)}, bf16[4,4,128,128]{3,2,1,0:T(8,128)(2,1)S(1)}, u32[]{:S(2)}, u32[]{:S(2)}) collective-permute-start(bf16[4,4,128,128]{3,2,1,0:T(8,128)(2,1)S(1)} %shard_map.115), channel_id=1, source_target_pairs={{0,1},{1,0},{2,3},{3,2},{4,5},{5,4},{6,7},{7,6},{8,9},{9,8},{10,11... | collective-permute-start | bytes 1572872 | tf_op jit(solution)/shard_map/ppermute | solution.py:140
  19.6 3.9 %collective-permute-start.3 = (s32[4,8]{1,0:T(4,128)S(1)}, s32[4,8]{1,0:T(4,128)S(1)}, u32[]{:S(2)}, u32[]{:S(2)}) collective-permute-start(s32[4,8]{1,0:T(4,128)S(1)} %shard_map.114), channel_id=1, source_target_pairs={{0,1},{1,0},{2,3},{3,2},{4,5},{5,4},{6,7},{7,6},{8,9},{9,8},{10,11... | collective-permute-start | bytes 392 | tf_op jit(solution)/shard_map/ppermute | solution.py:140
  25.8 1.6 %collective-permute-start.8 = (f32[512,128]{1,0:T(8,128)S(1)}, f32[512,128]{1,0:T(8,128)S(1)}, u32[]{:S(2)}, u32[]{:S(2)}) collective-permute-start(f32[512,128]{1,0:T(8,128)S(1)} %get-tuple-element.21), channel_id=1, source_target_pairs={{0,1},{1,0},{2,3},{3,2},{4,5},{5,4},{6,7},{7,6},{8,9},{9,8},{10,11... | collective-permute-start | bytes 786440 | tf_op jit(solution)/shard_map/ppermute | solution.py:140
  27.4 5.6 %collective-permute-start.9 = (f16[512,128]{1,0:T(8,128)(2,1)S(1)}, f16[512,128]{1,0:T(8,128)(2,1)S(1)}, u32[]{:S(2)}, u32[]{:S(2)}) collective-permute-start(f16[512,128]{1,0:T(8,128)(2,1)S(1)} %multiply_convert_fusion.1), channel_id=1, source_target_pairs={{0,2},{1,3},{2,0},{3,1},{4,6},{5,7},{6,4},{7,5},{8,10},{9,11},{10,... | collective-permute-start | bytes 393224 | tf_op jit(solution)/shard_map/ppermute | solution.py:140
  33.5 1.3 %collective-permute-start.10 = (f32[72,128]{1,0:T(8,128)S(1)}, f32[72,128]{1,0:T(8,128)S(1)}, u32[]{:S(2)}, u32[]{:S(2)}) collective-permute-start(f32[72,128]{1,0:T(8,128)S(1)} %get-tuple-element.26), channel_id=1, source_target_pairs={{0,1},{1,0},{2,3},{3,2},{4,5},{5,4},{6,7},{7,6},{8,9},{9,8},{10,11... | collective-permute-start | bytes 110600 | tf_op jit(solution)/shard_map/ppermute | solution.py:140
  34.8 4.0 %collective-permute-start.11 = (f32[72,128]{1,0:T(8,128)S(1)}, f32[72,128]{1,0:T(8,128)S(1)}, u32[]{:S(2)}, u32[]{:S(2)}) collective-permute-start(f32[72,128]{1,0:T(8,128)S(1)} %add.38), channel_id=1, source_target_pairs={{0,4},{1,9},{2,6},{3,11},{4,0},{5,13},{6,2},{7,15},{8,12},{9,1},{1... | collective-permute-start | bytes 110600 | tf_op jit(solution)/shard_map/ppermute | solution.py:143
  38.8 4.0 %collective-permute-start.12 = (f32[72,128]{1,0:T(8,128)S(1)}, f32[72,128]{1,0:T(8,128)S(1)}, u32[]{:S(2)}, u32[]{:S(2)}) collective-permute-start(f32[72,128]{1,0:T(8,128)S(1)} %add.39), channel_id=1, source_target_pairs={{0,8},{1,17},{2,10},{3,19},{4,12},{5,21},{6,14},{7,23},{8,0},{9,25... | collective-permute-start | bytes 110600 | tf_op jit(solution)/shard_map/ppermute | solution.py:143
  42.7 4.9 %collective-permute-start.13 = (f32[72,128]{1,0:T(8,128)S(1)}, f32[72,128]{1,0:T(8,128)S(1)}, u32[]{:S(2)}, u32[]{:S(2)}) collective-permute-start(f32[72,128]{1,0:T(8,128)S(1)} %add.40), channel_id=1, source_target_pairs={{0,16},{1,5},{2,18},{3,7},{4,20},{5,1},{6,22},{7,3},{8,24},{9,13},... | collective-permute-start | bytes 110600 | tf_op jit(solution)/shard_map/ppermute | solution.py:143
  47.6 1.2 %collective-permute-start.14 = (f32[72,128]{1,0:T(8,128)S(1)}, f32[72,128]{1,0:T(8,128)S(1)}, u32[]{:S(2)}, u32[]{:S(2)}) collective-permute-start(f32[72,128]{1,0:T(8,128)S(1)} %add.41.mine_ref), channel_id=1, source_target_pairs={{0,1},{1,0},{2,3},{3,2},{4,5},{5,4},{6,7},{7,6},{8,9},{9,8},{10,11... | collective-permute-start | bytes 110600 | tf_op jit(solution)/shard_map/ppermute | solution.py:140

commit v6 on v4

--- a/solution.py
+++ b/solution.py
@@ -237,7 +237,7 @@
         compiler_params=params(),
     )(code, code_x, tiles_keep, tiles_x, *pieces, cot)
 
-    total, got = keep, rep_swap(send, 1)
+    total, got = keep, 0.25 * rep_swap((4.0 * send).astype(jnp.float16), 1).astype(jnp.float32)
     total = total + got
     if npair == 2:
         sent = lax.optimization_barrier((4.0 * total).astype(jnp.float16))

time: 49.7 us -> 49.6 us (level)
  no operation moved by 1% of the time
where the time goes in v6:
time: 49.6 us; the launch traced here: 49.3 us
  waiting for transfers between devices  20.5 us (41%)
  starting transfers between devices  20.2 us (41%)
  Pallas kernels  4 us (8%)
  local copies, waits for them, and re-layouts  3.54 us (7%)
  between operations  0.86 us (2%)
    ppermute x3, waiting for transfers between devices, blk_swap(): return lax.ppermute(x, 'blk', [(i, i ^ off) for i in range(nblk)])  8.72 us
    ppermute x8, waiting for transfers between devices, rep_swap(): return lax.ppermute(x, 'rep', [(i, i ^ off) for i in range(nrep)])  8.48 us
    ppermute x3, starting transfers between devices, two_ways(): lax.ppermute(x, BOTH, [(b * nrep + r, (b ^ (off1 if r % 2 else off0)) * n...  7.19 us
    ppermute x1, starting transfers between devices, one_core(): lax.ppermute(x, BOTH, [(b * nrep + r, (b ^ off) * nrep + r) for b in rang...  4.54 us
    ppermute x8, starting transfers between devices, rep_swap(): return lax.ppermute(x, 'rep', [(i, i ^ off) for i in range(nrep)])  4.39 us
    ppermute x3, starting transfers between devices, blk_swap(): return lax.ppermute(x, 'blk', [(i, i ^ off) for i in range(nblk)])  4.05 us
    unnamed x18, local copies, waits for them, and re-layouts  1.92 us
    pallas_call x1, Pallas kernels, stage(): pl.pallas_call(functools.partial(stage_kernel, rblk, plan), out_shape=(ja...  1.73 us
  transfers between devices with their start and end apart: 15, of which 11 were waited for; matrix products, arithmetic and copies ran while one was open for 4% of the time, Pallas kernels for 4%

profile of v6, /device:TPU:0, one launch (start us, length us, event | category | flops | bytes accessed | tf_op | source)
XLA Modules:
  0.0 49.3 jit_solution(12217305812342449707)
XLA Ops:
  0.6 4.1 %collective-permute-start = (bf16[1024,128]{1,0:T(8,128)(2,1)}, bf16[1024,128]{1,0:T(8,128)(2,1)S(1)}, u32[]{:S(2)}, u32[]{:S(2)}) collective-permute-start(bf16[1024,128]{1,0:T(8,128)(2,1)} %param.9), channel_id=1, source_target_pairs={{0,16},{1,5},{2,18},{3,7},{4,20},{5,1},{6,22},{7,3},{8,24},{9,13},... | collective-permute-start | bytes 786440 | tf_op jit(solution)/shard_map/ppermute | solution.py:143
  4.7 0.0 copy-start.1
  4.7 1.0 %constant_dynamic-slice_fusion = bf16[512,128]{1,0:T(8,128)(2,1)S(1)} fusion(bf16[1024,128]{1,0:T(8,128)(2,1)} %param.9, s32[]{:T(128)S(6)} %select_n.62), kind=kLoop, calls=%fused_computation.13 | loop fusion | bytes 262148 | tf_op jit(solution)/shard_map/dynamic_slice | solution.py:206
  5.7 2.6 %collective-permute-start.1 = (bf16[512,128]{1,0:T(8,128)(2,1)S(1)}, bf16[512,128]{1,0:T(8,128)(2,1)S(1)}, u32[]{:S(2)}, u32[]{:S(2)}) collective-permute-start(bf16[512,128]{1,0:T(8,128)(2,1)S(1)} %constant_dynamic-slice_fusion), channel_id=1, source_target_pairs={{0,12},{1,9},{2,14},{3,11},{4,8},{5,13},{6,10},{7,15},{8,4},{9,1},... | collective-permute-start | bytes 393224 | tf_op jit(solution)/shard_map/ppermute | solution.py:143
  8.3 0.0 copy-done.1
  8.3 0.0 copy-done.2
  8.3 0.0 copy-done.7
  8.3 0.6 %copy-done.4 = s32[1,1,8,4]{2,3,1,0:T(4,128)S(1)} copy-done((s32[1,1,8,4]{2,3,1,0:T(4,128)S(1)}, s32[1,1,8,4]{2,3,1,0:T(4,128)}, u32[]{:S(2)}) %copy-start.4) | copy-done | bytes 152
  9.0 0.0 copy-done.3
  9.0 0.0 copy-done.5
  9.0 0.0 copy-done.6
  9.0 1.2 %copy-done = bf16[1,1,8,4,128,128]{5,4,3,2,1,0:T(8,128)(2,1)S(1)} copy-done((bf16[1,1,8,4,128,128]{5,4,3,2,1,0:T(8,128)(2,1)S(1)}, bf16[1,1,8,4,128,128]{5,4,3,2,1,0:T(8,128)(2,1)}, u32[]{:S(2)}) %copy-start) | copy-done | bytes 1048600
  10.2 1.7 %shard_map.112 = (bf16[4,4,128,128]{3,2,1,0:T(8,128)(2,1)S(1)}, bf16[4,4,128,128]{3,2,1,0:T(8,128)(2,1)S(1)}, bf16[128,128]{1,0:T(8,128)(2,1)S(1)}, f32[1,128]{1...) custom-call(bf16[1,1,8,4,128,128]{5,4,3,2,1,0:T(8,128)(2,1)S(1)} %copy-done, ...), custom_call_target="tpu_custom_call" | custom-call | bytes 2097152 | tf_op jit(solution)/shard_map/pallas_call | solution.py:158
  12.0 0.4 collective-permute-done.1.refs_0_
  12.3 0.0 collective-permute-done.x_ref
  12.4 0.1 collective-permute-start.2
  12.5 4.5 %collective-permute-start.6 = (bf16[1024,128]{1,0:T(8,128)(2,1)S(1)}, bf16[1024,128]{1,0:T(8,128)(2,1)S(1)}, u32[]{:S(2)}, u32[]{:S(2)}) collective-permute-start(bf16[1024,128]{1,0:T(8,128)(2,1)S(1)} %shard_map.113.refs_4_), channel_id=1, source_target_pairs={{0,12},{2,14},{4,8},{6,10},{8,4},{10,6},{12,0},{14,2},{16,28},{18,... | collective-permute-start | bytes 786440 | tf_op jit(solution)/shard_map/ppermute | solution.py:151
  17.0 0.0 collective-permute-done.2
  17.1 0.5 %collective-permute-start.7 = (bf16[1024,128]{1,0:T(8,128)(2,1)S(1)}, bf16[1024,128]{1,0:T(8,128)(2,1)S(1)}, u32[]{:S(2)}, u32[]{:S(2)}) collective-permute-start(bf16[1024,128]{1,0:T(8,128)(2,1)S(1)} %broadcast_select_fusion.1.refs_0_), channel_id=1, source_target_pairs={{0,8},{1,5},{2,10},{3,7},{4,12},{5,1},{6,14},{7,3},{8,0},{9,13},{1... | collective-permute-start | bytes 786440 | tf_op jit(solution)/shard_map/ppermute | solution.py:143
  17.6 1.8 %collective-permute-start.5 = (bf16[768,128]{1,0:T(8,128)(2,1)S(1)}, bf16[768,128]{1,0:T(8,128)(2,1)S(1)}, u32[]{:S(2)}, u32[]{:S(2)}) collective-permute-start(bf16[768,128]{1,0:T(8,128)(2,1)S(1)} %shard_map.116), channel_id=1, source_target_pairs={{0,2},{1,3},{2,0},{3,1},{4,6},{5,7},{6,4},{7,5},{8,10},{9,11},{10,... | collective-permute-start | bytes 589832 | tf_op jit(solution)/shard_map/ppermute | solution.py:140
  19.5 0.0 copy-start.8
  19.5 0.1 collective-permute-start.4
  19.6 0.5 collective-permute-start.3
  20.1 1.7 %collective-permute-done.6 = bf16[1024,128]{1,0:T(8,128)(2,1)S(1)} collective-permute-done((bf16[1024,128]{1,0:T(8,128)(2,1)S(1)}, bf16[1024,128]{1,0:T(8,128)(2,1)S(1)}, u32[]{:S(2)}, u32[]{:S(2)}) %collective-permute-start.6) | collective-permute-done | bytes 262176 | tf_op jit(solution)/shard_map/ppermute | solution.py:151
  21.7 0.0 copy-done.8
  21.8 1.6 %collective-permute-done.5 = bf16[768,128]{1,0:T(8,128)(2,1)S(1)} collective-permute-done((bf16[768,128]{1,0:T(8,128)(2,1)S(1)}, bf16[768,128]{1,0:T(8,128)(2,1)S(1)}, u32[]{:S(2)}, u32[]{:S(2)}) %collective-permute-start.5) | collective-permute-done | bytes 196640 | tf_op jit(solution)/shard_map/ppermute | solution.py:140
  23.5 0.0 collective-permute-done.3.refs_1_
  23.5 1.2 %collective-permute-done.7.refs_7_ = bf16[1024,128]{1,0:T(8,128)(2,1)S(1)} collective-permute-done((bf16[1024,128]{1,0:T(8,128)(2,1)S(1)}, bf16[1024,128]{1,0:T(8,128)(2,1)S(1)}, u32[]{:S(2)}, u32[]{:S(2)}) %collective-permute-start.7) | collective-permute-done | bytes 262176 | tf_op jit(solution)/shard_map/ppermute | solution.py:143
  24.6 0.0 collective-permute-done.4.refs_3_
  24.6 1.1 %shard_map.117 = (f32[512,128]{1,0:T(8,128)S(1)}, f32[512,128]{1,0:T(8,128)S(1)}) custom-call(s32[4,8]{1,0:T(4,128)S(1)} %get-tuple-element.16.x_ref.refs_0_, s32[4,8]{1,0:T(4,128)S(1)} %collective-permute-done.3.refs_1_, bf16[4,4,128,128]{3,2,1,0:T(8,128)(2,1)S(1)} %get-tuple-element.18.refs_2_, ...), custom_call_target="tpu_custom_call" | custom-call | tf_op jit(solution)/shard_map/pallas_call | solution.py:231
  25.8 0.1 collective-permute-start.8
  25.9 1.3 %collective-permute-done.8 = f16[512,128]{1,0:T(8,128)(2,1)S(1)} collective-permute-done((f16[512,128]{1,0:T(8,128)(2,1)S(1)}, f16[512,128]{1,0:T(8,128)(2,1)S(1)}, u32[]{:S(2)}, u32[]{:S(2)}) %collective-permute-start.8) | collective-permute-done | bytes 131104 | tf_op jit(solution)/shard_map/ppermute | solution.py:140
  27.2 0.1 multiply_convert_fusion.1
  27.3 1.8 %collective-permute-start.9 = (f16[512,128]{1,0:T(8,128)(2,1)S(1)}, f16[512,128]{1,0:T(8,128)(2,1)S(1)}, u32[]{:S(2)}, u32[]{:S(2)}) collective-permute-start(f16[512,128]{1,0:T(8,128)(2,1)S(1)} %multiply_convert_fusion.1), channel_id=1, source_target_pairs={{0,2},{1,3},{2,0},{3,1},{4,6},{5,7},{6,4},{7,5},{8,10},{9,11},{10,... | collective-permute-start | bytes 393224 | tf_op jit(solution)/shard_map/ppermute | solution.py:140
  29.1 3.8 %collective-permute-done.9 = f16[512,128]{1,0:T(8,128)(2,1)S(1)} collective-permute-done((f16[512,128]{1,0:T(8,128)(2,1)S(1)}, f16[512,128]{1,0:T(8,128)(2,1)S(1)}, u32[]{:S(2)}, u32[]{:S(2)}) %collective-permute-start.9) | collective-permute-done | bytes 131104 | tf_op jit(solution)/shard_map/ppermute | solution.py:140
  33.0 0.4 shard_map.118
  33.4 0.1 collective-permute-start.10
  33.5 1.2 %collective-permute-done.10 = f32[72,128]{1,0:T(8,128)S(1)} collective-permute-done((f32[72,128]{1,0:T(8,128)S(1)}, f32[72,128]{1,0:T(8,128)S(1)}, u32[]{:S(2)}, u32[]{:S(2)}) %collective-permute-start.10) | collective-permute-done | bytes 36896 | tf_op jit(solution)/shard_map/ppermute | solution.py:140
  34.7 0.4 collective-permute-start.11
  35.1 3.5 %collective-permute-done.11 = f32[72,128]{1,0:T(8,128)S(1)} collective-permute-done((f32[72,128]{1,0:T(8,128)S(1)}, f32[72,128]{1,0:T(8,128)S(1)}, u32[]{:S(2)}, u32[]{:S(2)}) %collective-permute-start.11) | collective-permute-done | bytes 36896 | tf_op jit(solution)/shard_map/ppermute | solution.py:137
  38.6 1.6 %collective-permute-start.12 = (f32[72,128]{1,0:T(8,128)S(1)}, f32[72,128]{1,0:T(8,128)S(1)}, u32[]{:S(2)}, u32[]{:S(2)}) collective-permute-start(f32[72,128]{1,0:T(8,128)S(1)} %add.39), channel_id=1, source_target_pairs={{0,8},{4,12},{8,0},{12,4},{16,24},{20,28},{24,16},{28,20},{1,9},{5... | collective-permute-start | bytes 110600 | tf_op jit(solution)/shard_map/ppermute | solution.py:137
  40.2 2.4 %collective-permute-done.12 = f32[72,128]{1,0:T(8,128)S(1)} collective-permute-done((f32[72,128]{1,0:T(8,128)S(1)}, f32[72,128]{1,0:T(8,128)S(1)}, u32[]{:S(2)}, u32[]{:S(2)}) %collective-permute-start.12) | collective-permute-done | bytes 36896 | tf_op jit(solution)/shard_map/ppermute | solution.py:137
  42.6 2.1 %collective-permute-start.13 = (f32[72,128]{1,0:T(8,128)S(1)}, f32[72,128]{1,0:T(8,128)S(1)}, u32[]{:S(2)}, u32[]{:S(2)}) collective-permute-start(f32[72,128]{1,0:T(8,128)S(1)} %add.40), channel_id=1, source_target_pairs={{0,16},{4,20},{8,24},{12,28},{16,0},{20,4},{24,8},{28,12},{1,17},{... | collective-permute-start | bytes 110600 | tf_op jit(solution)/shard_map/ppermute | solution.py:137
  44.7 2.8 %collective-permute-done.13 = f32[72,128]{1,0:T(8,128)S(1)} collective-permute-done((f32[72,128]{1,0:T(8,128)S(1)}, f32[72,128]{1,0:T(8,128)S(1)}, u32[]{:S(2)}, u32[]{:S(2)}) %collective-permute-start.13) | collective-permute-done | bytes 36896 | tf_op jit(solution)/shard_map/ppermute | solution.py:137
  47.5 0.0 collective-permute-start.14
  47.5 0.6 %dynamic-slice_convert_fusion = bf16[256,128]{1,0:T(8,128)(2,1)} fusion(f32[512,128]{1,0:T(8,128)S(1)} %get-tuple-element.24, s32[]{:T(128)S(6)} %select_n.71), kind=kLoop, calls=%fused_computation.8 | loop fusion | bytes 131076 | tf_op jit(solution)/shard_map/convert_element_type | solution.py:266
  48.1 0.6 %collective-permute-done.14.other_ref = f32[72,128]{1,0:T(8,128)S(1)} collective-permute-done((f32[72,128]{1,0:T(8,128)S(1)}, f32[72,128]{1,0:T(8,128)S(1)}, u32[]{:S(2)}, u32[]{:S(2)}) %collective-permute-start.14) | collective-permute-done | bytes 36896 | tf_op jit(solution)/shard_map/ppermute | solution.py:140
  48.7 0.6 %shard_map.119 = (f32[128,128]{1,0:T(8,128)}, f32[1,128]{1,0:T(1,128)}) custom-call(f32[72,128]{1,0:T(8,128)S(1)} %add.41.mine_ref, f32[72,128]{1,0:T(8,128)S(1)} %collective-permute-done.14.other_ref), custom_call_target="tpu_custom_call" | custom-call | tf_op jit(solution)/shard_map/pallas_call | solution.py:272
  (24 shorter events, 0.3 us)
Async XLA Ops:
  0.6 11.7 %collective-permute-start = (bf16[1024,128]{1,0:T(8,128)(2,1)}, bf16[1024,128]{1,0:T(8,128)(2,1)S(1)}, u32[]{:S(2)}, u32[]{:S(2)}) collective-permute-start(bf16[1024,128]{1,0:T(8,128)(2,1)} %param.9), channel_id=1, source_target_pairs={{0,16},{1,5},{2,18},{3,7},{4,20},{5,1},{6,22},{7,3},{8,24},{9,13},... | collective-permute-start | bytes 786440 | tf_op jit(solution)/shard_map/ppermute | solution.py:143
  4.7 3.6 %copy-start.1 = (bf16[256,128]{1,0:T(8,128)(2,1)S(1)}, bf16[256,128]{1,0:T(8,128)(2,1)}, u32[]{:S(2)}) copy-start(bf16[256,128]{1,0:T(8,128)(2,1)} %refs_4_.1) | copy-start | bytes 196612
  4.7 3.6 %copy-start.2 = (bf16[128,128]{1,0:T(8,128)(2,1)S(1)}, bf16[128,128]{1,0:T(8,128)(2,1)}, u32[]{:S(2)}) copy-start(bf16[128,128]{1,0:T(8,128)(2,1)} %refs_1_.1) | copy-start | bytes 98308
  4.7 3.6 %copy-start.7 = (s32[1,1,8]{2,1,0:T(1,128)S(1)}, s32[1,1,8]{2,1,0:T(1,128)}, u32[]{:S(2)}) copy-start(s32[1,1,8]{2,1,0:T(1,128)} %refs_7_.1) | copy-start | bytes 100
  5.7 6.6 %collective-permute-start.1 = (bf16[512,128]{1,0:T(8,128)(2,1)S(1)}, bf16[512,128]{1,0:T(8,128)(2,1)S(1)}, u32[]{:S(2)}, u32[]{:S(2)}) collective-permute-start(bf16[512,128]{1,0:T(8,128)(2,1)S(1)} %constant_dynamic-slice_fusion), channel_id=1, source_target_pairs={{0,12},{1,9},{2,14},{3,11},{4,8},{5,13},{6,10},{7,15},{8,4},{9,1},... | collective-permute-start | bytes 393224 | tf_op jit(solution)/shard_map/ppermute | solution.py:143
  8.3 0.7 %copy-start.4 = (s32[1,1,8,4]{2,3,1,0:T(4,128)S(1)}, s32[1,1,8,4]{2,3,1,0:T(4,128)}, u32[]{:S(2)}) copy-start(s32[1,1,8,4]{2,3,1,0:T(4,128)} %param.14) | copy-start | bytes 388
  8.3 0.7 %copy-start.3 = (s32[1,1,8,4]{2,3,1,0:T(4,128)S(1)}, s32[1,1,8,4]{2,3,1,0:T(4,128)}, u32[]{:S(2)}) copy-start(s32[1,1,8,4]{2,3,1,0:T(4,128)} %param.13) | copy-start | bytes 388
  8.3 0.7 %copy-start.5 = (s32[256]{0:T(256)S(1)}, s32[256]{0:T(256)}, u32[]{:S(2)}) copy-start(s32[256]{0:T(256)} %param.16) | copy-start | bytes 3076
  8.3 0.7 %copy-start.6 = (f32[128]{0:T(128)S(1)}, f32[128]{0:T(128)}, u32[]{:S(2)}) copy-start(f32[128]{0:T(128)} %param.11) | copy-start | bytes 1540
  9.0 1.2 %copy-start = (bf16[1,1,8,4,128,128]{5,4,3,2,1,0:T(8,128)(2,1)S(1)}, bf16[1,1,8,4,128,128]{5,4,3,2,1,0:T(8,128)(2,1)}, u32[]{:S(2)}) copy-start(bf16[1,1,8,4,128,128]{5,4,3,2,1,0:T(8,128)(2,1)} %refs_0_.1) | copy-start | bytes 3145732
  12.4 4.7 %collective-permute-start.2 = (bf16[1024,128]{1,0:T(8,128)(2,1)S(1)}, bf16[1024,128]{1,0:T(8,128)(2,1)S(1)}, u32[]{:S(2)}, u32[]{:S(2)}) collective-permute-start(bf16[1024,128]{1,0:T(8,128)(2,1)S(1)} %shard_map.113.refs_4_), channel_id=1, source_target_pairs={{0,1},{1,0},{2,3},{3,2},{4,5},{5,4},{6,7},{7,6},{8,9},{9,8},{10,11... | collective-permute-start | bytes 786440 | tf_op jit(solution)/shard_map/ppermute | solution.py:140
  12.5 9.3 %collective-permute-start.6 = (bf16[1024,128]{1,0:T(8,128)(2,1)S(1)}, bf16[1024,128]{1,0:T(8,128)(2,1)S(1)}, u32[]{:S(2)}, u32[]{:S(2)}) collective-permute-start(bf16[1024,128]{1,0:T(8,128)(2,1)S(1)} %shard_map.113.refs_4_), channel_id=1, source_target_pairs={{0,12},{2,14},{4,8},{6,10},{8,4},{10,6},{12,0},{14,2},{16,28},{18,... | collective-permute-start | bytes 786440 | tf_op jit(solution)/shard_map/ppermute | solution.py:151
  17.1 7.6 %collective-permute-start.7 = (bf16[1024,128]{1,0:T(8,128)(2,1)S(1)}, bf16[1024,128]{1,0:T(8,128)(2,1)S(1)}, u32[]{:S(2)}, u32[]{:S(2)}) collective-permute-start(bf16[1024,128]{1,0:T(8,128)(2,1)S(1)} %broadcast_select_fusion.1.refs_0_), channel_id=1, source_target_pairs={{0,8},{1,5},{2,10},{3,7},{4,12},{5,1},{6,14},{7,3},{8,0},{9,13},{1... | collective-permute-start | bytes 786440 | tf_op jit(solution)/shard_map/ppermute | solution.py:143
  17.6 5.7 %collective-permute-start.5 = (bf16[768,128]{1,0:T(8,128)(2,1)S(1)}, bf16[768,128]{1,0:T(8,128)(2,1)S(1)}, u32[]{:S(2)}, u32[]{:S(2)}) collective-permute-start(bf16[768,128]{1,0:T(8,128)(2,1)S(1)} %shard_map.116), channel_id=1, source_target_pairs={{0,2},{1,3},{2,0},{3,1},{4,6},{5,7},{6,4},{7,5},{8,10},{9,11},{10,... | collective-permute-start | bytes 589832 | tf_op jit(solution)/shard_map/ppermute | solution.py:140
  19.5 2.3 %copy-start.8 = (bf16[1024,128]{1,0:T(8,128)(2,1)S(1)}, bf16[1024,128]{1,0:T(8,128)(2,1)}, u32[]{:S(2)}) copy-start(bf16[1024,128]{1,0:T(8,128)(2,1)} %param.9) | copy-start | bytes 786436
  19.5 5.2 %collective-permute-start.4 = (bf16[4,4,128,128]{3,2,1,0:T(8,128)(2,1)S(1)}, bf16[4,4,128,128]{3,2,1,0:T(8,128)(2,1)S(1)}, u32[]{:S(2)}, u32[]{:S(2)}) collective-permute-start(bf16[4,4,128,128]{3,2,1,0:T(8,128)(2,1)S(1)} %shard_map.115), channel_id=1, source_target_pairs={{0,1},{1,0},{2,3},{3,2},{4,5},{5,4},{6,7},{7,6},{8,9},{9,8},{10,11... | collective-permute-start | bytes 1572872 | tf_op jit(solution)/shard_map/ppermute | solution.py:140
  19.6 3.9 %collective-permute-start.3 = (s32[4,8]{1,0:T(4,128)S(1)}, s32[4,8]{1,0:T(4,128)S(1)}, u32[]{:S(2)}, u32[]{:S(2)}) collective-permute-start(s32[4,8]{1,0:T(4,128)S(1)} %shard_map.114), channel_id=1, source_target_pairs={{0,1},{1,0},{2,3},{3,2},{4,5},{5,4},{6,7},{7,6},{8,9},{9,8},{10,11... | collective-permute-start | bytes 392 | tf_op jit(solution)/shard_map/ppermute | solution.py:140
  25.8 1.4 %collective-permute-start.8 = (f16[512,128]{1,0:T(8,128)(2,1)S(1)}, f16[512,128]{1,0:T(8,128)(2,1)S(1)}, u32[]{:S(2)}, u32[]{:S(2)}) collective-permute-start(f16[512,128]{1,0:T(8,128)(2,1)S(1)} %multiply_convert_fusion.2), channel_id=1, source_target_pairs={{0,1},{1,0},{2,3},{3,2},{4,5},{5,4},{6,7},{7,6},{8,9},{9,8},{10,11... | collective-permute-start | bytes 393224 | tf_op jit(solution)/shard_map/ppermute | solution.py:140
  27.3 5.6 %collective-permute-start.9 = (f16[512,128]{1,0:T(8,128)(2,1)S(1)}, f16[512,128]{1,0:T(8,128)(2,1)S(1)}, u32[]{:S(2)}, u32[]{:S(2)}) collective-permute-start(f16[512,128]{1,0:T(8,128)(2,1)S(1)} %multiply_convert_fusion.1), channel_id=1, source_target_pairs={{0,2},{1,3},{2,0},{3,1},{4,6},{5,7},{6,4},{7,5},{8,10},{9,11},{10,... | collective-permute-start | bytes 393224 | tf_op jit(solution)/shard_map/ppermute | solution.py:140
  33.4 1.3 %collective-permute-start.10 = (f32[72,128]{1,0:T(8,128)S(1)}, f32[72,128]{1,0:T(8,128)S(1)}, u32[]{:S(2)}, u32[]{:S(2)}) collective-permute-start(f32[72,128]{1,0:T(8,128)S(1)} %get-tuple-element.26), channel_id=1, source_target_pairs={{0,1},{1,0},{2,3},{3,2},{4,5},{5,4},{6,7},{7,6},{8,9},{9,8},{10,11... | collective-permute-start | bytes 110600 | tf_op jit(solution)/shard_map/ppermute | solution.py:140
  34.7 4.0 %collective-permute-start.11 = (f32[72,128]{1,0:T(8,128)S(1)}, f32[72,128]{1,0:T(8,128)S(1)}, u32[]{:S(2)}, u32[]{:S(2)}) collective-permute-start(f32[72,128]{1,0:T(8,128)S(1)} %add.38), channel_id=1, source_target_pairs={{0,4},{4,0},{8,12},{12,8},{16,20},{20,16},{24,28},{28,24},{1,5},{5... | collective-permute-start | bytes 110600 | tf_op jit(solution)/shard_map/ppermute | solution.py:137
  38.6 4.0 %collective-permute-start.12 = (f32[72,128]{1,0:T(8,128)S(1)}, f32[72,128]{1,0:T(8,128)S(1)}, u32[]{:S(2)}, u32[]{:S(2)}) collective-permute-start(f32[72,128]{1,0:T(8,128)S(1)} %add.39), channel_id=1, source_target_pairs={{0,8},{4,12},{8,0},{12,4},{16,24},{20,28},{24,16},{28,20},{1,9},{5... | collective-permute-start | bytes 110600 | tf_op jit(solution)/shard_map/ppermute | solution.py:137
  42.6 4.9 %collective-permute-start.13 = (f32[72,128]{1,0:T(8,128)S(1)}, f32[72,128]{1,0:T(8,128)S(1)}, u32[]{:S(2)}, u32[]{:S(2)}) collective-permute-start(f32[72,128]{1,0:T(8,128)S(1)} %add.40), channel_id=1, source_target_pairs={{0,16},{4,20},{8,24},{12,28},{16,0},{20,4},{24,8},{28,12},{1,17},{... | collective-permute-start | bytes 110600 | tf_op jit(solution)/shard_map/ppermute | solution.py:137
  47.5 1.2 %collective-permute-start.14 = (f32[72,128]{1,0:T(8,128)S(1)}, f32[72,128]{1,0:T(8,128)S(1)}, u32[]{:S(2)}, u32[]{:S(2)}) collective-permute-start(f32[72,128]{1,0:T(8,128)S(1)} %add.41.mine_ref), channel_id=1, source_target_pairs={{0,1},{1,0},{2,3},{3,2},{4,5},{5,4},{6,7},{7,6},{8,9},{9,8},{10,11... | collective-permute-start | bytes 110600 | tf_op jit(solution)/shard_map/ppermute | solution.py:140
